TPU v7x, 128 devices: a whole 4x4x4 slice. The times are simulated.
128 devices in a mesh: dp: 8 (over z_hi, y), seq: 16 (over z_lo, x, core).
Axes of the slice: x: 4, y: 4, z: 4 (z_hi: 2, z_lo: 2; z = z_hi * 2 + z_lo), core: 2. Of those that a mesh axis runs over, the one named last changes fastest.
Arguments:
- tokens: bfloat16 [8, 2048, 1024], P('dp', 'seq'), may hold values from -6 to 6
- w_qkv: bfloat16 [1024, 3072], P('dp'), may hold values from -0.1875 to 0.1875
- qv_bias: bfloat16 [2048], P('dp'), may hold values from -3 to 3
- w_out: bfloat16 [1024, 1024], P('dp'), may hold values from -0.1875 to 0.1875
- out_bias: bfloat16 [1024], P('dp'), may hold values from -3 to 3
- w_up: bfloat16 [1024, 4096], P('dp'), may hold values from -0.1875 to 0.1875
- up_bias: bfloat16 [4096], P('dp'), may hold values from -3 to 3
- w_down: bfloat16 [4096, 1024], P('dp'), may hold values from -0.09375 to 0.09375
- down_bias: bfloat16 [1024], P('dp'), may hold values from -3 to 3
- gain_one: bfloat16 [1024], P('dp'), may hold values from 0.5 to 1.5
- shift_one: bfloat16 [1024], P('dp'), may hold values from -3 to 3
- gain_two: bfloat16 [1024], P('dp'), may hold values from 0.5 to 1.5
- shift_two: bfloat16 [1024], P('dp'), may hold values from -3 to 3
- cotangent: bfloat16 [8, 2048, 1024], P('dp', 'seq'), may hold values from -6 to 6
Outputs:
- activations: bfloat16 [8, 2048, 1024], P('dp', 'seq')
- input_grad: bfloat16 [8, 2048, 1024], P('dp', 'seq')
- w_qkv_grad: float32 [1024, 3072], P(('dp', 'seq'))
- qv_bias_grad: float32 [2048], P(('dp', 'seq'))
- w_out_grad: float32 [1024, 1024], P(('dp', 'seq'))
- out_bias_grad: float32 [1024], P(('dp', 'seq'))
- w_up_grad: float32 [1024, 4096], P(('dp', 'seq'))
- up_bias_grad: float32 [4096], P(('dp', 'seq'))
- w_down_grad: float32 [4096, 1024], P(('dp', 'seq'))
- down_bias_grad: float32 [1024], P(('dp', 'seq'))
- gain_one_grad: float32 [1024], P(('dp', 'seq'))
- shift_one_grad: float32 [1024], P(('dp', 'seq'))
- gain_two_grad: float32 [1024], P(('dp', 'seq'))
- shift_two_grad: float32 [1024], P(('dp', 'seq'))
All inputs are finite; a program needn't handle non-finite values.
Results may differ from a plain program's by a relative error of at most 0.034.
Values may be sent and summed in bfloat16 or wider, within the bound.
A program may use at most 192 MiB of HBM per device.

v0:
```python
import math

import jax
import jax.numpy as jnp
from jax import lax
from jax.sharding import PartitionSpec as P

H = 16


EPS = 1e-06


def in_one_piece(arrays, axis, dim, along):
    widths = [math.prod(a.shape[along:]) for a in arrays]
    both = jnp.concatenate(
        [a.reshape(*a.shape[:along], w) for a, w in zip(arrays, widths)], axis=along
    )
    filled = lax.all_gather(both, axis, axis=dim, tiled=True)
    blocks = jnp.split(filled, [sum(widths[:k]) for k in range(1, len(widths))], axis=along)
    return tuple(
        (b.reshape(*filled.shape[:along], *a.shape[along:]) for a, b in zip(arrays, blocks))
    )


def sent_together(arrays, axis, dim, along):
    widths = [math.prod(a.shape[along:]) for a in arrays]
    both = jnp.concatenate(
        [a.reshape(*a.shape[:along], w) for a, w in zip(arrays, widths)], axis=along
    )
    filled = lax.psum_scatter(both, axis, scatter_dimension=dim, tiled=True)
    blocks = jnp.split(filled, [sum(widths[:k]) for k in range(1, len(widths))], axis=along)
    return tuple(
        (b.reshape(*filled.shape[:along], *a.shape[along:]) for a, b in zip(arrays, blocks))
    )


def split_up(array, dim, devices):
    before, after = (array.shape[:dim], array.shape[dim + 1 :])
    return jnp.moveaxis(array.reshape(*before, devices, -1, *after), dim, 0)


def one_scatter(arrays, axis, dims):
    devices = lax.axis_size(axis)
    blocks = [split_up(a, dim, devices) for a, dim in zip(arrays, dims)]
    lines = jnp.concatenate([b.reshape(devices, -1) for b in blocks], axis=1)
    rows = max(16, -(-lines.shape[1] // 1024) * 8)
    lines = jnp.pad(lines, ((0, 0), (0, rows * 128 - lines.shape[1]))).reshape(-1, 128)
    flat, at, outs = (lax.psum_scatter(lines, axis, tiled=True).reshape(-1), 0, [])
    for b in blocks:
        part = b[0]
        outs.append(flat[at : at + part.size].reshape(part.shape))
        at += part.size
    return tuple(outs)


def norm_rows(values, gain, shift):
    center = values - jnp.mean(values, axis=-1, keepdims=True)
    spread = jnp.mean(center * center, axis=-1, keepdims=True)
    return center * lax.rsqrt(spread + EPS) * gain + shift


def exact_gelu(values):
    return jax.nn.gelu(values, approximate=False)


def forward_attention(queries, keys, values, block, scale):
    length, heads_here, width = queries.shape

    def forward_one_block(query_part):
        raw = jnp.einsum("bhd,khd->hbk", query_part, keys, preferred_element_type=jnp.float32)
        scores = raw * scale
        top = jnp.max(scores, axis=-1, keepdims=True)
        expo = jnp.exp(scores - top)
        total = jnp.sum(expo, axis=-1, keepdims=True)
        prob = (expo / total).astype(jnp.bfloat16)
        result = jnp.einsum("hbk,khd->bhd", prob, values, preferred_element_type=jnp.float32)
        return (result.astype(jnp.bfloat16), (top + jnp.log(total))[:, :, 0])

    blocks = queries.reshape(length // block, block, heads_here, width)
    outputs, logsums = lax.map(forward_one_block, blocks)
    return (outputs.reshape(length, heads_here * width), logsums)


def backward_attention(queries, keys, values, grad_out, logsums, block, scale):
    length, heads_here, width = queries.shape

    def backward_one_block(carry, pieces):
        key_acc, value_acc = carry
        query_part, grad_part, logsum_part = pieces
        raw = jnp.einsum("bhd,khd->hbk", query_part, keys, preferred_element_type=jnp.float32)
        prob = jnp.exp(raw * scale - logsum_part[:, :, None])
        prob_low = prob.astype(jnp.bfloat16)
        value_acc = value_acc + jnp.einsum(
            "hbk,bhd->khd", prob_low, grad_part, preferred_element_type=jnp.float32
        )
        grad_prob = jnp.einsum(
            "bhd,khd->hbk", grad_part, values, preferred_element_type=jnp.float32
        )
        inner = jnp.sum(prob * grad_prob, axis=-1, keepdims=True)
        grad_raw = (scale * (prob * (grad_prob - inner))).astype(jnp.bfloat16)
        grad_query = jnp.einsum("hbk,khd->bhd", grad_raw, keys, preferred_element_type=jnp.float32)
        key_acc = key_acc + jnp.einsum(
            "hbk,bhd->khd", grad_raw, query_part, preferred_element_type=jnp.float32
        )
        return ((key_acc, value_acc), grad_query)

    count = length // block
    start = (
        jnp.zeros((length, heads_here, width), jnp.float32),
        jnp.zeros((length, heads_here, width), jnp.float32),
    )
    pieces = (
        queries.reshape(count, block, heads_here, width),
        grad_out.reshape(count, block, heads_here, width),
        logsums,
    )
    (grad_keys, grad_values), grad_queries = lax.scan(backward_one_block, start, pieces)
    return (grad_queries.reshape(length, heads_here, width), grad_keys, grad_values)


def on_device(
    tokens,
    w_qkv,
    qv_bias,
    w_out,
    out_bias,
    w_up,
    up_bias,
    w_down,
    down_bias,
    gain_one,
    shift_one,
    gain_two,
    shift_two,
    cotangent,
):
    attn_set = (
        lax.all_gather(w_qkv, "dp", axis=0, tiled=True),
        lax.all_gather(qv_bias, "dp", axis=0, tiled=True),
        *in_one_piece((w_out, out_bias, gain_one, shift_one), "dp", 0, 1),
    )
    mlp_set = (
        lax.all_gather(w_up, "dp", axis=0, tiled=True),
        *in_one_piece((up_bias, w_down), "dp", 0, 1),
        lax.all_gather(down_bias, "dp", axis=0, tiled=True),
        lax.all_gather(gain_two, "dp", axis=0, tiled=True),
        lax.all_gather(shift_two, "dp", axis=0, tiled=True),
    )
    full_qkv, full_qvb, full_out, full_ob, full_gone, full_sone = attn_set
    full_up, full_ub, full_down, full_db, full_gtwo, full_stwo = mlp_set
    width = full_out.shape[0]
    local_tokens = tokens.shape[1]
    inputs = tokens[0].astype(jnp.float32)
    gain_a = full_gone.astype(jnp.float32)
    shift_a = full_sone.astype(jnp.float32)
    gain_b = full_gtwo.astype(jnp.float32)
    shift_b = full_stwo.astype(jnp.float32)
    normed_one = norm_rows(inputs, gain_a, shift_a).astype(jnp.bfloat16)
    bias_all = jnp.concatenate(
        [
            full_qvb[:width].astype(jnp.float32),
            jnp.zeros((width,), jnp.float32),
            full_qvb[width:].astype(jnp.float32),
        ]
    )
    qkv = (jnp.dot(normed_one, full_qkv, preferred_element_type=jnp.float32) + bias_all).astype(
        jnp.bfloat16
    )
    by_head = lax.all_to_all(
        qkv.reshape(local_tokens, 3, width), "seq", split_axis=2, concat_axis=0, tiled=True
    )
    length = by_head.shape[0]
    columns = by_head.shape[2]
    head_width = width // H
    heads_here = columns // head_width
    block = min(512, length)
    scale = head_width ** (-0.5)
    queries = by_head[:, 0].reshape(length, heads_here, head_width)
    keys = by_head[:, 1].reshape(length, heads_here, head_width)
    values = by_head[:, 2].reshape(length, heads_here, head_width)
    attended, logsums = forward_attention(queries, keys, values, block, scale)
    mixed_tokens = lax.all_to_all(attended, "seq", split_axis=0, concat_axis=1, tiled=True)
    mid = (
        inputs
        + jnp.dot(mixed_tokens, full_out, preferred_element_type=jnp.float32)
        + full_ob.astype(jnp.float32)
    )
    normed_two = norm_rows(mid, gain_b, shift_b).astype(jnp.bfloat16)
    pre = jnp.dot(normed_two, full_up, preferred_element_type=jnp.float32) + full_ub.astype(
        jnp.float32
    )
    act = exact_gelu(pre).astype(jnp.bfloat16)
    result = (
        mid
        + jnp.dot(act, full_down, preferred_element_type=jnp.float32)
        + full_db.astype(jnp.float32)
    )
    back_qkv = attn_set[0]
    back_out = attn_set[2]
    back_up = mlp_set[0]
    back_down = mlp_set[2]
    grad_top = cotangent[0]
    grad_in = grad_top.astype(jnp.float32)
    down_bias_grad = jnp.sum(grad_in, axis=0)
    w_down_grad = jnp.einsum("tf,td->fd", act, grad_top, preferred_element_type=jnp.float32)
    grad_act = jnp.einsum("td,fd->tf", grad_top, back_down, preferred_element_type=jnp.float32)
    gelu_pull = jax.vjp(exact_gelu, pre)[1]
    grad_pre = gelu_pull(grad_act)[0].astype(jnp.bfloat16)
    up_bias_grad = jnp.sum(grad_pre.astype(jnp.float32), axis=0)
    w_up_grad = jnp.einsum("td,tf->df", normed_two, grad_pre, preferred_element_type=jnp.float32)
    grad_normed_two = jnp.einsum("tf,df->td", grad_pre, back_up, preferred_element_type=jnp.float32)
    norm_two_pull = jax.vjp(norm_rows, mid, gain_b, shift_b)[1]
    part_mid, gain_two_grad, shift_two_grad = norm_two_pull(grad_normed_two)
    grad_mid = grad_in + part_mid
    grad_branch = grad_mid.astype(jnp.bfloat16)
    out_bias_grad = jnp.sum(grad_branch.astype(jnp.float32), axis=0)
    w_out_grad = jnp.einsum(
        "td,te->de", mixed_tokens, grad_branch, preferred_element_type=jnp.float32
    )
    grad_mixed = jnp.einsum(
        "te,de->td", grad_branch, back_out, preferred_element_type=jnp.float32
    ).astype(jnp.bfloat16)
    grad_heads = lax.all_to_all(grad_mixed, "seq", split_axis=1, concat_axis=0, tiled=True)
    grad_queries, grad_keys, grad_values = backward_attention(
        queries,
        keys,
        values,
        grad_heads.reshape(length, heads_here, head_width),
        logsums,
        block,
        scale,
    )
    stacked = jnp.stack(
        [
            grad_queries.reshape(length, columns),
            grad_keys.reshape(length, columns),
            grad_values.reshape(length, columns),
        ],
        axis=1,
    ).astype(jnp.bfloat16)
    grad_qkv = lax.all_to_all(stacked, "seq", split_axis=0, concat_axis=2, tiled=True).reshape(
        local_tokens, 3 * width
    )
    column_sums = jnp.sum(grad_qkv.astype(jnp.float32), axis=0)
    qv_bias_grad = jnp.concatenate([column_sums[:width], column_sums[2 * width :]])
    w_qkv_grad = jnp.einsum("td,te->de", normed_one, grad_qkv, preferred_element_type=jnp.float32)
    grad_normed_one = jnp.einsum(
        "te,de->td", grad_qkv, back_qkv, preferred_element_type=jnp.float32
    )
    norm_one_pull = jax.vjp(norm_rows, inputs, gain_a, shift_a)[1]
    part_in, gain_one_grad, shift_one_grad = norm_one_pull(grad_normed_one)
    input_grad = (grad_mid + part_in).astype(jnp.bfloat16)
    first_sums = (
        lax.psum_scatter(
            w_qkv_grad.astype(jnp.bfloat16), "dp", scatter_dimension=0, tiled=True
        ).astype(jnp.float32),
        lax.psum_scatter(
            qv_bias_grad.astype(jnp.bfloat16), "dp", scatter_dimension=0, tiled=True
        ).astype(jnp.float32),
        *tuple(
            (
                part.astype(jnp.float32)
                for part in sent_together(
                    (
                        w_out_grad.astype(jnp.bfloat16),
                        out_bias_grad.astype(jnp.bfloat16),
                        w_up_grad.astype(jnp.bfloat16),
                    ),
                    "dp",
                    0,
                    1,
                )
            )
        ),
        *tuple(
            (
                part.astype(jnp.float32)
                for part in sent_together(
                    (up_bias_grad.astype(jnp.bfloat16), w_down_grad.astype(jnp.bfloat16)),
                    "dp",
                    0,
                    1,
                )
            )
        ),
        lax.psum_scatter(
            down_bias_grad.astype(jnp.bfloat16), "dp", scatter_dimension=0, tiled=True
        ).astype(jnp.float32),
        lax.psum_scatter(
            gain_one_grad.astype(jnp.bfloat16), "dp", scatter_dimension=0, tiled=True
        ).astype(jnp.float32),
        lax.psum_scatter(
            shift_one_grad.astype(jnp.bfloat16), "dp", scatter_dimension=0, tiled=True
        ).astype(jnp.float32),
        lax.psum_scatter(
            gain_two_grad.astype(jnp.bfloat16), "dp", scatter_dimension=0, tiled=True
        ).astype(jnp.float32),
        lax.psum_scatter(
            shift_two_grad.astype(jnp.bfloat16), "dp", scatter_dimension=0, tiled=True
        ).astype(jnp.float32),
    )
    summed = tuple(
        (
            part.astype(jnp.float32)
            for part in one_scatter(
                (
                    first_sums[0].astype(jnp.bfloat16),
                    first_sums[1].astype(jnp.bfloat16),
                    first_sums[2].astype(jnp.bfloat16),
                    first_sums[3].astype(jnp.bfloat16),
                    first_sums[4].astype(jnp.bfloat16),
                    first_sums[5].astype(jnp.bfloat16),
                    first_sums[6].astype(jnp.bfloat16),
                    first_sums[7].astype(jnp.bfloat16),
                    first_sums[8].astype(jnp.bfloat16),
                    first_sums[9].astype(jnp.bfloat16),
                    first_sums[10].astype(jnp.bfloat16),
                    first_sums[11].astype(jnp.bfloat16),
                ),
                "seq",
                (0, 0, 0, 0, 0, 0, 0, 0, 0, 0, 0, 0),
            )
        )
    )
    return (
        result.astype(jnp.bfloat16)[None],
        input_grad[None],
        summed[0],
        summed[1],
        summed[2],
        summed[3],
        summed[4],
        summed[5],
        summed[6],
        summed[7],
        summed[8],
        summed[9],
        summed[10],
        summed[11],
    )


def solution(mesh):
    return jax.shard_map(
        on_device,
        mesh=mesh,
        in_specs=(
            P("dp", "seq", None),
            P("dp", None),
            P("dp"),
            P("dp", None),
            P("dp"),
            P("dp", None),
            P("dp"),
            P("dp", None),
            P("dp"),
            P("dp"),
            P("dp"),
            P("dp"),
            P("dp"),
            P("dp", "seq", None),
        ),
        out_specs=(
            P("dp", "seq", None),
            P("dp", "seq", None),
            P(("dp", "seq"), None),
            P(("dp", "seq")),
            P(("dp", "seq"), None),
            P(("dp", "seq")),
            P(("dp", "seq"), None),
            P(("dp", "seq")),
            P(("dp", "seq"), None),
            P(("dp", "seq")),
            P(("dp", "seq")),
            P(("dp", "seq")),
            P(("dp", "seq")),
            P(("dp", "seq")),
        ),
        check_vma=False,
    )
```

profile of v0, /device:TPU:1, one launch (start us, length us, event | category | flops | bytes accessed | tf_op | source)
XLA Modules:
  0.0 1049.9 jit_solution(5124076739047708903)
XLA Ops:
  9.7 1.8 concatenate.22
  13.1 1.6 pad_maximum_fusion.1
  15.4 21.5 %all-gather = bf16[8,1,256]{2,1,0:T(2,128)(2,1)S(1)} all-gather(bf16[1,1,256]{2,1,0:T(2,128)(2,1)S(1)} %reshape.368), channel_id=1, replica_groups=mesh['dp'=8,'seq'=16] {'dp'}, dimensions={0}, use_global_device_ids=true | all-gather | bytes 4608 | tf_op jit(solution)/shard_map/all_gather | solution.py:140
  37.3 33.6 %all-gather.9.cloned.1.call-done = bf16[1024,1027]{1,0:T(8,128)(2,1)} async-done(((bf16[128,1027]{1,0:T(8,128)(2,1)}), bf16[1024,1027]{1,0:T(8,128)(2,1)}) %all-gather.9.cloned.1.call-update) | async-done | bytes 2103312 | tf_op jit(solution)/shard_map/all_gather | solution.py:19
  70.8 1.7 convert_reduce_fusion.2
  72.6 89.5 %all-gather.11.cloned.1.call-done = bf16[1024,3072]{1,0:T(8,128)(2,1)} async-done(((bf16[128,3072]{1,0:T(8,128)(2,1)}), bf16[1024,3072]{1,0:T(8,128)(2,1)}) %all-gather.11.cloned.1.call-update) | async-done | bytes 6291472 | tf_op jit(solution)/shard_map/all_gather | solution.py:139
  162.1 3.9 fusion.39
  166.4 1.7 copy.135
  168.0 5.4 all-to-all-start
  173.5 17.0 %all-to-all-done = bf16[128,3,1024]{0,1,2:T(4,128)(2,1)S(1)} async-done(((bf16[128,3,1024]{0,1,2:T(4,128)(2,1)}), bf16[128,3,1024]{0,1,2:T(4,128)(2,1)S(1)}, u32[]{:S(2)}, u32[]{:S(2)}) %all-to-all-start) | async-done | bytes 786464 | tf_op jit(solution)/shard_map/all_to_all | solution.py:170
  191.6 14.6 %while.27 = (s32[]{:T(128)}, bf16[4,512,1,64]{1,3,2,0:T(8,128)(2,1)S(1)}, f32[4,1,512]{2,1,0:T(1,128)S(1)}, bf16[4,512,1,64]{1,3,2,0:T(8,128)(2,1)}, bf16[2048,1...) while((s32[]{:T(128)}, bf16[4,512,1,64]{1,3,2,0:T(8,128)(2,1)S(1)}, ...), condition=%wide.region_5.6_spmd, body=%wide.region_2.5_spmd.sunk | while | flops 277904896 | bytes 13258849 | solution.py:81
  191.6 1.6 multiply_reduce_fusion.7
  195.2 1.7 multiply_reduce_fusion.7
  198.9 1.7 multiply_reduce_fusion.7
  202.5 1.7 multiply_reduce_fusion.7
  207.3 4.4 all-to-all-start.1
  211.6 15.4 %all-gather.2 = bf16[8,1,128]{2,1,0:T(2,128)(2,1)S(1)} all-gather(bf16[1,1,128]{2,1,0:T(2,128)(2,1)S(1)} %bitcast.252), channel_id=1, replica_groups=mesh['dp'=8,'seq'=16] {'dp'}, dimensions={0}, use_global_device_ids=true | all-gather | bytes 2304 | tf_op jit(solution)/shard_map/all_gather | solution.py:148
  227.1 16.1 %all-gather.1 = bf16[8,1,128]{2,1,0:T(2,128)(2,1)S(1)} all-gather(bf16[1,1,128]{2,1,0:T(2,128)(2,1)S(1)} %bitcast.253), channel_id=1, replica_groups=mesh['dp'=8,'seq'=16] {'dp'}, dimensions={0}, use_global_device_ids=true | all-gather | bytes 2304 | tf_op jit(solution)/shard_map/all_gather | solution.py:147
  243.2 2.2 fusion.113
  245.6 45.4 %all-gather.15.cloned.1.call-done = bf16[4096,1025]{1,0:T(8,128)(2,1)} async-done(((bf16[512,1025]{1,0:T(8,128)(2,1)}), bf16[4096,1025]{1,0:T(8,128)(2,1)}) %all-gather.15.cloned.1.call-update) | async-done | bytes 8396816 | tf_op jit(solution)/shard_map/all_gather | solution.py:19
  292.6 107.3 %all-gather.13.cloned.1.call-done = bf16[1024,4096]{1,0:T(8,128)(2,1)} async-done(((bf16[128,4096]{1,0:T(8,128)(2,1)}), bf16[1024,4096]{1,0:T(8,128)(2,1)}) %all-gather.13.cloned.1.call-update) | async-done | bytes 8388624 | tf_op jit(solution)/shard_map/all_gather | solution.py:144
  399.9 9.2 multiply_convert_fusion.1
  409.1 8.1 fusion.114
  417.3 3.0 multiply_reduce_fusion.2
  424.0 5.4 all-to-all-start.2
  429.7 6.9 all-to-all-done.2
  437.6 48.9 %while.28 = (s32[]{:T(128)}, f32[2048,1,64]{0,2,1:T(8,128)}, f32[2048,1,64]{0,2,1:T(8,128)S(1)}, bf16[4,512,1,64]{1,3,2,0:T(8,128)(2,1)}, bf16[4,512,1,64]{1,3,2...) while((s32[]{:T(128)}, f32[2048,1,64]{0,2,1:T(8,128)}, ...), condition=%wide.region_12.13_spmd.clone, body=%wide.region_10.12_spmd.clone.sunk | while | flops 681049600 | bytes 53618920 | solution.py:118
  439.2 2.1 multiply_reduce_fusion.8
  443.3 2.1 fusion.158
  445.4 2.8 fusion.159
  451.3 2.1 multiply_reduce_fusion.8
  455.3 2.4 fusion.158
  457.7 2.8 fusion.159
  463.5 2.1 multiply_reduce_fusion.8
  467.6 2.4 fusion.158
  469.9 2.8 fusion.159
  475.8 2.1 multiply_reduce_fusion.8
  479.9 2.4 fusion.158
  482.2 2.8 fusion.159
  491.6 16.8 %all_to_all.68 = bf16[16,2,12288]{2,1,0:T(2,128)(2,1)} all-to-all(bf16[16,2,12288]{2,1,0:T(2,128)(2,1)S(1)} %reshape.402), channel_id=1, replica_groups=mesh['dp'=8,'seq'=16] {'seq'}, dimensions={0} | all-to-all | bytes 1572864 | tf_op jit(solution)/shard_map/all_to_all | solution.py:242
  508.3 2.9 reshape.403
  512.5 4.6 convolution_convert_fusion.2
  518.0 6.9 convolution_convert_fusion
  525.0 9.5 pad_maximum_fusion
  535.5 2.2 convolution_convert_fusion.3
  537.7 4.0 copy.152
  542.0 7.0 convolution_convert_fusion.1
  549.0 19.2 %concatenate.26 = bf16[1024,5121]{1,0:T(8,128)(2,1)} concatenate(bf16[1024,1024]{1,0:T(8,128)(2,1)} %copy.152, bf16[1024,1]{1,0:T(8,128)(2,1)S(1)} %reshape.388, bf16[1024,4096]{1,0:T(8,128)(2,1)} %convolution_convert_fusion.1), dimensions={1} | concatenate | bytes 20975616 | tf_op jit(solution)/shard_map/concatenate | solution.py:28
  570.7 1.9 copy.155
  572.6 1.6 bitcast_reduce_fusion
  574.5 5.5 fusion.107
  580.4 32.4 %all-reduce.8 = (bf16[2048]{0:T(1024)(128)(2,1)S(1)}, bf16[1024]{0:T(1024)(128)(2,1)S(1)}, bf16[1024]{0:T(1024)(128)(2,1)S(1)}, bf16[1024]{0:T(1024)(128)(2,1)S(...) all-reduce(bf16[2048]{0:T(1024)(128)(2,1)S(1)} %pad_maximum_fusion., ...), channel_id=3, replica_groups=mesh['dp'=8,'seq'=16] {'dp'}, use_global_device_ids=true, to_apply=%region_17.18.clone | all-reduce | flops 7168 | bytes 28672
  617.7 113.6 %reduce-scatter.8.cloned.1.call-done = bf16[512,1025]{0,1:T(8,128)(2,1)} async-done(((bf16[4096,1025]{0,1:T(8,128)(2,1)}), bf16[512,1025]{0,1:T(8,128)(2,1)}) %reduce-scatter.8.cloned.1.call-update) | async-done | bytes 1049616 | tf_op jit(solution)/shard_map/reduce_scatter | solution.py:31
  736.5 132.9 %reduce-scatter.6.cloned.1.call-done = bf16[128,5121]{1,0:T(8,128)(2,1)} async-done(((bf16[1024,5121]{1,0:T(8,128)(2,1)}), bf16[128,5121]{1,0:T(8,128)(2,1)}) %reduce-scatter.6.cloned.1.call-update) | async-done | bytes 1310992 | tf_op jit(solution)/shard_map/reduce_scatter | solution.py:31
  871.4 2.6 split.52
  874.0 2.3 reshape_reshape.18
  876.4 3.6 dynamic-update-slice.2
  881.5 7.7 dynamic-update-slice.4
  890.6 6.9 dynamic-update-slice.6
  904.3 3.8 pad.4
  908.0 4.0 reshape.358
  912.7 14.9 %all-gather.3 = bf16[8,1,128]{2,1,0:T(2,128)(2,1)S(1)} all-gather(bf16[1,1,128]{2,1,0:T(2,128)(2,1)S(1)} %bitcast.254), channel_id=1, replica_groups=mesh['dp'=8,'seq'=16] {'dp'}, dimensions={0}, use_global_device_ids=true | all-gather | bytes 2304 | tf_op jit(solution)/shard_map/all_gather | solution.py:146
  928.9 7.2 fusion.70
  937.0 99.6 %all-reduce.11.cloned.1.call-done = bf16[12416,128]{1,0:T(8,128)(2,1)} async-done(((bf16[12416,128]{1,0:T(8,128)(2,1)}), bf16[12416,128]{1,0:T(8,128)(2,1)}) %all-reduce.11.cloned.1.call-update) | async-done | bytes 3178512
  (234 shorter events, 82.3 us)
Async XLA Ops:
  7.2 5.9 copy-start.14
  7.2 63.7 %all-gather.9.cloned.1.call-start = ((), (), s32[]{:S(2)}) async-start(), calls=%async_computation.7 | async-start | bytes 2654208 | tf_op jit(solution)/shard_map/all_gather | solution.py:19
  11.5 150.6 %all-gather.11.cloned.1.call-start = ((), (), s32[]{:S(2)}) async-start(), calls=%async_computation.8 | async-start | bytes 7077888 | tf_op jit(solution)/shard_map/all_gather | solution.py:139
  12.2 278.8 %all-gather.15.cloned.1.call-start = ((), (), s32[]{:S(2)}) async-start(), calls=%async_computation.10 | async-start | bytes 10616832 | tf_op jit(solution)/shard_map/all_gather | solution.py:19
  13.1 2.3 copy-start.25
  13.1 23.8 %copy-start.1 = (bf16[1,128,1024]{2,1,0:T(8,128)(2,1)S(1)}, bf16[1,128,1024]{2,1,0:T(8,128)(2,1)}, u32[]{:S(2)}) copy-start(bf16[1,128,1024]{2,1,0:T(8,128)(2,1)} %param.18) | copy-start | bytes 786436
  14.8 385.1 %all-gather.13.cloned.1.call-start = ((), (), s32[]{:S(2)}) async-start(), calls=%async_computation.9 | async-start | bytes 9437184 | tf_op jit(solution)/shard_map/all_gather | solution.py:144
  37.3 128.7 %copy-start.20 = (f32[128]{0:T(128)}, f32[128]{0:T(128)S(1)}, u32[]{:S(2)}) copy-start(f32[128]{0:T(128)S(1)} %fusion.83) | copy-start | bytes 1540
  168.0 22.4 %all-to-all-start = ((bf16[128,3,1024]{0,1,2:T(4,128)(2,1)}), bf16[128,3,1024]{0,1,2:T(4,128)(2,1)S(1)}, u32[]{:S(2)}, u32[]{:S(2)}) async-start(bf16[128,3,1024]{0,1,2:T(4,128)(2,1)} %copy.135), calls=%async_computation | async-start | bytes 2097152 | tf_op jit(solution)/shard_map/all_to_all | solution.py:170
  206.1 5.5 copy-start.22
  206.2 20.9 %copy-start.23 = (bf16[128]{0:T(256)(128)(2,1)S(1)}, bf16[128]{0:T(256)(128)(2,1)}, u32[]{:S(2)}) copy-start(bf16[128]{0:T(256)(128)(2,1)} %param.29) | copy-start | bytes 772
  207.3 35.9 %all-to-all-start.1 = ((bf16[16,128,64]{1,2,0:T(8,128)(2,1)}), bf16[16,128,64]{1,2,0:T(8,128)(2,1)S(1)}, u32[]{:S(2)}, u32[]{:S(2)}) async-start(bf16[16,128,64]{1,2,0:T(8,128)(2,1)} %copy.140), calls=%async_computation.1 | async-start | bytes 524288 | tf_op jit(solution)/shard_map/all_to_all | solution.py:183
  243.2 49.4 %copy-start.11 = (bf16[16,128,64]{1,2,0:T(8,128)(2,1)}, bf16[16,128,64]{1,2,0:T(8,128)(2,1)S(1)}, u32[]{:S(2)}) copy-start(bf16[16,128,64]{1,2,0:T(8,128)(2,1)S(1)} %all-to-all-done.1) | copy-start | bytes 786436
  245.4 175.0 %copy-start.2 = (f32[128,1024]{1,0:T(8,128)}, f32[128,1024]{1,0:T(8,128)S(1)}, u32[]{:S(2)}) copy-start(f32[128,1024]{1,0:T(8,128)S(1)} %get-tuple-element.285) | copy-start | bytes 1572868
  399.9 9.2 copy-start.8
  399.9 9.2 copy-start.19
  399.9 17.4 %slice-start = ((s8[8388608]{0:T(1024)(128)(4,1)}), s8[4194304]{0:T(1024)(128)(4,1)S(1)}, s32[]{:S(2)}) async-start(s8[8388608]{0:T(1024)(128)(4,1)} %bitcast.225), calls=%async_computation.15 | async-start | bytes 8388608
  409.1 8.2 slice-start.1
  417.3 3.1 copy-start.7
  420.3 2.0 copy-start.10
  420.6 3.3 copy-start.5
  420.8 15.9 %copy-start.15 = (bf16[128,1024]{1,0:T(8,128)(2,1)}, bf16[128,1024]{1,0:T(8,128)(2,1)S(1)}, u32[]{:S(2)}) copy-start(bf16[128,1024]{1,0:T(8,128)(2,1)S(1)} %get-tuple-element.262) | copy-start | bytes 786436
  424.0 12.6 %all-to-all-start.2 = ((bf16[128,16,64]{0,2,1:T(8,128)(2,1)}), bf16[128,16,64]{0,2,1:T(8,128)(2,1)S(1)}, u32[]{:S(2)}, u32[]{:S(2)}) async-start(bf16[128,16,64]{0,2,1:T(8,128)(2,1)} %bitcast.28), calls=%async_computation.2 | async-start | bytes 524288 | tf_op jit(solution)/shard_map/all_to_all | solution.py:224
  429.4 184.5 %reduce-scatter.4.cloned.1.call-start = ((), (), s32[]{:S(2)}) async-start(), calls=%async_computation.11 | async-start | bytes 7077888 | tf_op jit(solution)/shard_map/reduce_scatter | solution.py:255
  441.3 1.9 copy-start
  445.4 2.8 copy-start.17
  449.0 0.7 copy-start.18
  453.4 1.9 copy-start
  457.7 2.8 copy-start.17
  461.2 0.7 copy-start.18
  465.7 1.9 copy-start
  469.9 2.8 copy-start.17
  473.5 0.7 copy-start.18
  477.9 1.9 copy-start
  482.2 2.8 copy-start.17
  485.8 0.7 copy-start.18
  512.5 4.6 copy-start.4
  517.1 1.0 copy-start.9
  517.1 214.2 %reduce-scatter.8.cloned.1.call-start = ((), (), s32[]{:S(2)}) async-start(), calls=%async_computation.13 | async-start | bytes 9510912 | tf_op jit(solution)/shard_map/reduce_scatter | solution.py:31
  534.5 1.0 copy-start.12
  534.5 1.0 copy-start.16
  534.5 334.9 %reduce-scatter.6.cloned.1.call-start = ((), (), s32[]{:S(2)}) async-start(), calls=%async_computation.12 | async-start | bytes 12091392 | tf_op jit(solution)/shard_map/reduce_scatter | solution.py:31
  537.7 4.3 copy-start.3
  568.2 0.7 copy-start.27
  568.2 468.4 %all-reduce.11.cloned.1.call-start = ((), (), s32[]{:S(2)}) async-start(), calls=%async_computation.14 | async-start | bytes 6356992
  574.5 5.5 copy-start.21
  912.1 0.7 copy-start.24
  912.1 15.6 %copy-start.26 = (u32[128]{0:T(128)S(1)}, u32[128]{0:T(128)}, u32[]{:S(2)}) copy-start(u32[128]{0:T(128)} %constant.152) | copy-start | bytes 1540
  912.1 16.8 %copy-start.13 = (bf16[128,4096]{1,0:T(8,128)(2,1)S(1)}, bf16[128,4096]{1,0:T(8,128)(2,1)}, u32[]{:S(2)}) copy-start(bf16[128,4096]{1,0:T(8,128)(2,1)} %get-tuple-element.286) | copy-start | bytes 3145732
  928.9 7.2 copy-start.6
Sparse Core Ops, SparseCore 0:
  11.6 59.2 all-gather.8
  73.2 88.8 all-gather.10
  164.4 126.5 all-gather.14
  293.2 106.6 all-gather.12
  517.2 95.8 reduce-scatter.3
  617.4 113.8 reduce-scatter.7
  735.7 133.5 reduce-scatter.5
  912.2 124.3 all-reduce.10
where the time goes:
time: 1060 us; the launch traced here: 1050 us
  waiting for transfers between devices  647 us (61%)
  blocking collectives  117 us (11%)
  local copies, waits for them, and re-layouts  114 us (11%)
  matrix products  110 us (10%)
  other arithmetic  27.9 us (3%)
  between operations  16.9 us (2%)
  starting transfers between devices  16.2 us (2%)
    reduce_scatter x2, waiting for transfers between devices, sent_together(): filled = lax.psum_scatter(both, axis, scatter_dimension=dim, tiled=True)  247 us
    all_gather x1, waiting for transfers between devices, on_device(): lax.all_gather(w_up, 'dp', axis=0, tiled=True)  107 us
    unnamed x9, waiting for transfers between devices  101 us
    all_gather x1, waiting for transfers between devices, on_device(): lax.all_gather(w_qkv, 'dp', axis=0, tiled=True)  89.5 us
    all_gather x2, waiting for transfers between devices, in_one_piece(): filled = lax.all_gather(both, axis, axis=dim, tiled=True)  78.9 us
    unnamed x77, local copies, waits for them, and re-layouts  39.7 us
    unnamed x1, blocking collectives  32.4 us
    all_gather x1, blocking collectives, on_device(): lax.all_gather(qv_bias, 'dp', axis=0, tiled=True)  21.5 us
  transfers between devices with their start and end apart: 11, of which 9 were waited for; matrix products, arithmetic and copies ran while one was open for 10% of the time, Pallas kernels for 0%

commit v1 on v0

v1 whole, which is shorter than its diff:
```python
import functools

import jax
import jax.numpy as jnp
from jax import lax
from jax.experimental import pallas as pl
from jax.experimental.pallas import tpu as pltpu
from jax.sharding import PartitionSpec as P

MESH = pl.DeviceIdType.MESH
EPS = 1e-06
BF = jnp.bfloat16
F32 = jnp.float32
D = 1024
T = 128
VMEM = pltpu.VMEM
ANY = pl.ANY
DMA = pltpu.SemaphoreType.DMA


class Place:
    def __init__(self):
        self.i, self.j = lax.axis_index("dp"), lax.axis_index("seq")
        self.zh, self.y = self.i // 4, self.i % 4
        self.zl, self.xc = self.j // 8, self.j % 8
        self.x, self.c = self.xc // 2, self.xc % 2
        self.z = self.zh * 2 + self.zl

    def in_group(self, dx, dc):
        return (self.i, self.zl * 8 + ((self.x + dx) % 4) * 2 + (self.c + dc) % 2)

    def sibling(self):
        return self.in_group(0, 1)

    def across(self):
        return (self.i, (1 - self.zl) * 8 + self.xc)

    def along_y(self, dy):
        return (self.zh * 4 + (self.y + dy) % 4, self.j)

    def along_z(self, dz):
        z = (self.z + dz) % 4
        return ((z // 2) * 4 + self.y, (z % 2) * 8 + self.xc)

    def holder(self, dh, dy):
        near = (self.zl + dh) % 2
        return (((self.zh + dh) % 2) * 4 + (self.y + dy) % 4, near * 8 + self.xc)


GROUP = [(dx, dc) for dx in range(4) for dc in range(2) if (dx, dc) != (0, 0)]
RING = [(1, 0), (3, 0), (2, 0), (0, 1)]
HOLDERS = [(dh, dy) for dh in range(2) for dy in range(4) if (dh, dy) != (0, 0)]


def greet(devices, more=0):
    barrier = pltpu.get_barrier_semaphore()
    for device in devices:
        pl.semaphore_signal(barrier, inc=1, device_id=device, device_id_type=MESH)
    pl.semaphore_wait(barrier, len(devices) + more)


class Lines:
    def __init__(self, send, recv):
        self.send, self.recv, self.used = send, recv, 0

    def copy(self, src, dst, device):
        k = self.used
        self.used += 1
        return pltpu.make_async_remote_copy(
            src_ref=src,
            dst_ref=dst,
            send_sem=self.send.at[k],
            recv_sem=self.recv.at[k],
            device_id=device,
            device_id_type=MESH,
        )


def gather_group(at, lines, own, slots):
    started = []
    for dx in (1, 3, 2):
        copy = lines.copy(own, slots.at[at.xc], at.in_group(dx, 0))
        copy.start()
        started.append((dx, copy))
    beside = lines.copy(own, slots.at[at.xc], at.sibling())
    beside.start()

    def finish():
        forwards = []
        for dx, copy in started:
            copy.wait_recv()
            slot = ((at.x + 4 - dx) % 4) * 2 + at.c
            forward = lines.copy(slots.at[slot], slots.at[slot], at.sibling())
            forward.start()
            forwards.append(forward)
        beside.wait()
        for forward in forwards:
            forward.wait()
        for _, copy in started:
            copy.wait_send()

    return finish


def reduce_group(at, lines, parts, from_core, sums, from_ring):
    order = (2, 1, 3, 0)
    cores = {}
    for dx in order:
        slot = ((at.x + dx) % 4) * 2 + 1 - at.c
        cores[dx] = lines.copy(parts.at[slot], from_core.at[dx], at.sibling())
        cores[dx].start()
    ring = []
    for dx in order[:3]:
        slot = ((at.x + dx) % 4) * 2 + at.c
        cores[dx].wait_recv()
        sums[dx] = (parts[slot].astype(F32) + from_core[dx].astype(F32)).astype(BF)
        copy = lines.copy(sums.at[dx], from_ring.at[dx], at.in_group(dx, 0))
        copy.start()
        ring.append((dx, copy))

    def finish():
        cores[0].wait_recv()
        total = parts[at.xc].astype(F32) + from_core[0].astype(F32)
        for dx, copy in ring:
            copy.wait_recv()
            total = total + from_ring[dx].astype(F32)
        for dx in order:
            cores[dx].wait_send()
        for _, copy in ring:
            copy.wait_send()
        return total

    return finish


REDUCE_SCRATCH = [VMEM((4, T, D), BF), VMEM((4, T, D), BF), VMEM((4, T, D), BF)]


def normed(values):
    center = values - jnp.mean(values, axis=-1, keepdims=True)
    rstd = lax.rsqrt(jnp.mean(center * center, axis=-1, keepdims=True) + EPS)
    return center * rstd, rstd


def lanes_of(head, value):
    lane = lax.broadcasted_iota(jnp.int32, (1, 128), 1)
    mine = (lane < 64) if head == 0 else (lane >= 64)
    return jnp.where(mine, value, 0.0).astype(F32)


def by_head(zero, one):
    lane = lax.broadcasted_iota(jnp.int32, (1, 128), 1)
    return jnp.where(lane < 64, zero, one)


def dot(a, b, ca, cb):
    return lax.dot_general(a, b, (((ca,), (cb,)), ((), ())), preferred_element_type=F32)


QB = 256


def head_kernel(
    tok, cot, wq, wu, wd, wo, vec,
    n1, cg, wqg, wug, wdg, wog, vg, q, k, v, kr, vr, att, lse,
    xg, rows, bias, top, total, send, recv, local,
):
    at = Place()
    greet(
        [at.in_group(*d) for d in RING]
        + [at.holder(*d) for d in HOLDERS]
        + [at.across()]
    )
    lines = Lines(send, recv)
    first = []
    for dh, dy in HOLDERS:
        for src, dst in ((vec, vg.at[at.i]), (wq, wqg.at[at.i])):
            copy = lines.copy(src, dst, at.holder(dh, dy))
            copy.start()
            first.append(copy)
    x_done = gather_group(at, lines, tok, xg)
    own = [
        pltpu.make_async_copy(src, dst, local.at[n])
        for n, (src, dst) in enumerate(
            (
                (cot, cg.at[at.xc]),
                (wu, wug.at[at.i]),
                (wd, wdg.at[at.i]),
                (wo, wog.at[at.i, at.c]),
            )
        )
    ]
    for copy in own:
        copy.start()
    xg[at.xc] = tok[...]
    vg[at.i] = vec[...]
    wqg[at.i] = wq[...]
    later, halves = [], []
    for dh, dy in HOLDERS:
        device = at.holder(dh, dy)
        copy = lines.copy(wo, wog.at[at.i, at.c], device)
        copy.start()
        halves.append((dh, dy, copy))
        for src, dst in ((wu, wug.at[at.i]), (wd, wdg.at[at.i])):
            copy = lines.copy(src, dst, device)
            copy.start()
            later.append(copy)
    beside = lines.copy(wo, wog.at[at.i, at.c], at.sibling())
    beside.start()
    later.append(beside)
    for copy in first:
        copy.wait()
    for d in range(8):
        for r in range(2):
            rows[r : r + 1, d * 128 : (d + 1) * 128] = vg[d, 2 + r : 3 + r, :].astype(F32)
    for d in range(8):
        bias[d] = vg[d].astype(F32)
    x_done()
    cot_done = gather_group(at, lines, cot, cg)

    gain, shift = rows[0:1, :], rows[1:2, :]

    def norm_step(b, _):
        hat, _ = normed(xg[b].astype(F32))
        n1[b] = (hat * gain + shift).astype(BF)
        return 0

    lax.fori_loop(0, 8, norm_step, 0)
    at_row = pl.ds(10 + at.xc % 2, 1)
    q_bias = bias[at.xc // 2, at_row, :]
    v_bias = bias[4 + at.xc // 2, at_row, :]

    def kv_step(b, _):
        part = pl.ds(pl.multiple_of(b * T, T), T)
        acc = dot(n1[b], wqg[...].reshape(D, 384), 1, 0)
        q[part, :] = (acc[:, 0:128] + q_bias).astype(BF)
        k[part, :] = acc[:, 128:256].astype(BF)
        v[part, :] = (acc[:, 256:384] + v_bias).astype(BF)
        return 0

    lax.fori_loop(0, 8, kv_step, 0)
    swaps = [lines.copy(k, kr, at.across()), lines.copy(v, vr, at.across())]
    for copy in swaps:
        copy.start()

    def attend(keys, values, fresh):
        def step(t, _):
            part = pl.ds(pl.multiple_of(t * QB, QB), QB)
            block = q[part, :]
            tops, sums, outs, fades = [], [], [], []
            for h in range(2):
                mine = block * lanes_of(h, 0.125).astype(BF)
                score = dot(mine, keys[...], 1, 1)
                peak = jnp.max(score, axis=-1, keepdims=True)
                if not fresh:
                    old = top[part, 64 * h : 64 * h + 1]
                    peak = jnp.maximum(old, peak)
                    fades.append(jnp.exp(old - peak))
                expo = jnp.exp(score - peak)
                tops.append(peak)
                sums.append(jnp.sum(expo, axis=-1, keepdims=True))
                outs.append(dot(expo.astype(BF), values[...], 1, 0))
            peak, added, out = by_head(*tops), by_head(*sums), by_head(*outs)
            if fresh:
                top[part, :] = peak
                lse[part, :] = added
                total[part, :] = out
            else:
                fade = by_head(*fades)
                mass = lse[part, :] * fade + added
                att[part, :] = ((total[part, :] * fade + out) / mass).astype(BF)
                lse[part, :] = peak + jnp.log(mass)
            return 0

        lax.fori_loop(0, 1024 // QB, step, 0)

    attend(k, v, True)
    for copy in swaps:
        copy.wait()
    attend(kr, vr, False)
    cot_done()
    forwards = []
    for dh, dy, copy in halves:
        copy.wait_recv()
        holder = ((at.zh + dh) % 2) * 4 + (at.y + 4 - dy) % 4
        forward = lines.copy(wog.at[holder, at.c], wog.at[holder, at.c], at.sibling())
        forward.start()
        forwards.append(forward)
    for copy in later:
        copy.wait()
    for _, _, copy in halves:
        copy.wait_send()
    for copy in forwards:
        copy.wait()
    for copy in own:
        copy.wait()


def any_spec():
    return pl.BlockSpec(memory_space=ANY)


def vm_spec():
    return pl.BlockSpec(memory_space=VMEM)


def shape(*dims, of=BF):
    return jax.ShapeDtypeStruct(dims, of)


def call(kernel, name, ident, ins, outs, scratch, args):
    return pl.pallas_call(
        kernel,
        name=name,
        in_specs=[any_spec() if s == "a" else vm_spec() for s in ins],
        out_specs=[any_spec() if s == "a" else vm_spec() for s, _ in outs],
        out_shape=[o for _, o in outs],
        scratch_shapes=scratch,
        compiler_params=pltpu.CompilerParams(
            collective_id=ident, has_side_effects=True, vmem_limit_bytes=52 * 2**20
        ),
    )(*args)


def mid_kernel(att, x, wout, rows, mid, n2g, mixed, own, send, recv):
    at = Place()
    greet([at.in_group(*d) for d in GROUP])
    lines = Lines(send, recv)
    mine = pl.ds(pl.multiple_of(at.xc * 128, 128), 128)
    copies = []
    for dx, dc in GROUP:
        to = ((at.x + dx) % 4) * 2 + (at.c + dc) % 2
        copy = lines.copy(
            att.at[pl.ds(pl.multiple_of(to * T, T), T)], mixed.at[:, mine], at.in_group(dx, dc)
        )
        copy.start()
        copies.append(copy)
    mixed[:, mine] = att[pl.ds(pl.multiple_of(at.xc * T, T), T), :]
    for copy in copies:
        copy.wait()
    middle = x[...].astype(F32) + dot(mixed[...], wout[...], 1, 0) + rows[0:1, :]
    mid[...] = middle
    hat, _ = normed(middle)
    own[...] = (hat * rows[1:2, :] + rows[2:3, :]).astype(BF)
    done = gather_group(at, lines, own, n2g)
    n2g[at.xc] = own[...]
    done()


def back_kernel(parts, mid, cot, rows, dmid, dbg, sums, own, core, part, ring, send, recv):
    at = Place()
    greet([at.in_group(*d) for d in RING])
    lines = Lines(send, recv)
    finish = reduce_group(at, lines, parts, core, part, ring)
    hat, rstd = normed(mid[...])
    pulled = finish()
    sums[0:1, :] = jnp.sum(pulled * hat, axis=0, keepdims=True)
    sums[1:2, :] = jnp.sum(pulled, axis=0, keepdims=True)
    scaled = pulled * rows[1:2, :]
    inner = jnp.mean(scaled * hat, axis=-1, keepdims=True)
    middle = cot[...].astype(F32) + rstd * (
        scaled - jnp.mean(scaled, axis=-1, keepdims=True) - hat * inner
    )
    dmid[...] = middle
    low = middle.astype(BF)
    own[...] = low
    done = gather_group(at, lines, own, dbg)
    dbg[at.xc] = low
    low = low.astype(F32)
    sums[2:3, :] = jnp.sum(low, axis=0, keepdims=True)
    sums[3:4, :] = jnp.sum(cot[...].astype(F32), axis=0, keepdims=True)
    sums[4:8, :] = jnp.zeros((4, D), F32)
    done()


def pull_kernel(
    db, wout, att, q, k, v, kr, vr, lse,
    wog, dqkv,
    do, delta, dq, dk, dv, away, back, send, recv,
):
    at = Place()
    greet([at.across()])
    lines = Lines(send, recv)
    rows_w = wout[pl.ds(pl.multiple_of(at.xc * 128, 128), 128), :]
    grads = dot(db[...], rows_w, 1, 1).astype(BF)
    do[...] = grads
    wog[...] = dot(att[...], db[...], 0, 0).astype(BF)
    both = grads.astype(F32) * att[...].astype(F32)
    delta[...] = by_head(
        jnp.sum(both * lanes_of(0, 1.0), axis=-1, keepdims=True),
        jnp.sum(both * lanes_of(1, 1.0), axis=-1, keepdims=True),
    )

    def pull(keys, values, fresh):
        dk[...] = jnp.zeros_like(dk)
        dv[...] = jnp.zeros_like(dv)

        def step(t, _):
            part = pl.ds(pl.multiple_of(t * QB, QB), QB)
            block, grad = q[part, :], do[part, :]
            outs = []
            for h in range(2):
                mine = block * lanes_of(h, 0.125).astype(BF)
                pulled = grad * lanes_of(h, 1.0).astype(BF)
                prob = jnp.exp(dot(mine, keys[...], 1, 1) - lse[part, 64 * h : 64 * h + 1])
                dprob = dot(pulled, values[...], 1, 1)
                raw = (prob * (dprob - delta[part, 64 * h : 64 * h + 1])).astype(BF)
                dv[...] += dot(pulled, prob.astype(BF), 0, 0)
                dk[...] += dot(mine, raw, 0, 0)
                outs.append(dot(raw, keys[...], 1, 0))
            out = by_head(*outs) * 0.125
            dq[part, :] = out if fresh else dq[part, :] + out
            return 0

        lax.fori_loop(0, 1024 // QB, step, 0)

    pull(kr, vr, True)
    away[0] = dk[...].astype(BF)
    away[1] = dv[...].astype(BF)
    swap = lines.copy(away, back, at.across())
    swap.start()
    pull(k, v, False)
    swap.wait()
    dqkv[:, 0:128] = dq[...].astype(BF)
    dqkv[:, 128:256] = jnp.transpose(dk[...] + back[0].astype(F32)).astype(BF)
    dqkv[:, 256:384] = jnp.transpose(dv[...] + back[1].astype(F32)).astype(BF)


RA, RB, CA = 64, 48, 896


def last_kernel(
    parts, ends, ga, gb, tok, dmid, mid, rows,
    xgrad, result, wide, tall, vecs,
    core, part, ring, core2, part2, ring2, ra, rb, sa, sb, ra2, rb2, low, turn, row, send, recv,
):
    at = Place()
    swapped = (at.xc, at.zl * 8 + at.i)
    barrier = pltpu.get_barrier_semaphore()

    @pl.when(at.i != at.xc)
    def _():
        pl.semaphore_signal(barrier, inc=1, device_id=swapped, device_id_type=MESH)

    greet(
        [at.in_group(*d) for d in GROUP]
        + [at.along_y(d) for d in (1, 2, 3)]
        + [at.along_z(d) for d in (1, 2, 3)],
        jnp.where(at.i != at.xc, 1, 0),
    )
    lines = Lines(send, recv)
    first_a, first_b = [], []
    for d in (2, 1, 3):
        copy = lines.copy(ga.at[:, (at.y + d) % 4], ra.at[d - 1], at.along_y(d))
        copy.start()
        first_a.append((d, copy))
        z = (at.z + d) % 4
        copy = lines.copy(gb.at[z // 2, :, z % 2], rb.at[d - 1], at.along_z(d))
        copy.start()
        first_b.append((d, copy))
    finish = reduce_group(at, lines, parts, core, part, ring)
    finish2 = reduce_group(at, lines, ends, core2, part2, ring2)

    for d, copy in first_a:
        copy.wait_recv()
    for zh in range(2):
        for zl in range(2):
            acc = ga[zh, at.y, zl].astype(F32)
            for d in range(3):
                acc = acc + ra[d, zh, zl].astype(F32)
            sa[zh * 2 + zl] = acc.astype(BF)
    second = []
    for d in (2, 1, 3):
        copy = lines.copy(sa.at[(at.z + d) % 4], ra2.at[d - 1], at.along_z(d))
        copy.start()
        second.append(copy)
    for d, copy in first_b:
        copy.wait_recv()
    for y in range(4):
        acc = gb[at.zh, y, at.zl].astype(F32)
        for d in range(3):
            acc = acc + rb[d, y].astype(F32)
        sb[y] = acc.astype(BF)
    for d in (2, 1, 3):
        copy = lines.copy(sb.at[(at.y + d) % 4], rb2.at[d - 1], at.along_y(d))
        copy.start()
        second.append(copy)

    pulled = finish()
    hat, rstd = normed(tok[...].astype(F32))
    scaled = pulled * rows[3:4, :]
    inner = jnp.mean(scaled * hat, axis=-1, keepdims=True)
    xgrad[...] = (
        dmid[...] + rstd * (scaled - jnp.mean(scaled, axis=-1, keepdims=True) - hat * inner)
    ).astype(BF)
    result[...] = (mid[...] + finish2() + rows[4:5, :]).astype(BF)

    for copy in second:
        copy.wait_recv()
    acc = sa[at.z].astype(F32)
    for d in range(3):
        acc = acc + ra2[d].astype(F32)
    for b in range(8):
        low[b] = acc[b * 8 : (b + 1) * 8, :]
    acc = sb[at.y].astype(F32)
    for d in range(3):
        acc = acc + rb2[d].astype(F32)
    tall[0:32, :] = acc[0:32, :]
    turn[...] = acc[32:40, :]
    row[...] = acc[40:48, :]
    third = []
    for dx, dc in GROUP:
        to = ((at.x + dx) % 4) * 2 + (at.c + dc) % 2
        for src, dst in ((low.at[to], wide.at[at.xc]), (row, vecs.at[at.xc])):
            copy = lines.copy(src, dst, at.in_group(dx, dc))
            copy.start()
            third.append(copy)
    wide[at.xc] = low[at.xc]
    vecs[at.xc] = row[...]
    across = lines.copy(turn, tall.at[32:40, :], swapped)

    @pl.when(at.i != at.xc)
    def _():
        across.start()
        across.wait()

    @pl.when(at.i == at.xc)
    def _():
        tall[32:40, :] = turn[...]

    for copy in third:
        copy.wait()
    for _, copy in first_a + first_b:
        copy.wait_send()
    for copy in second:
        copy.wait_send()


def exact_gelu(values):
    return jax.nn.gelu(values, approximate=False)


def on_device(
    tokens, w_qkv, qv_bias, w_out, out_bias, w_up, up_bias, w_down, down_bias,
    gain_one, shift_one, gain_two, shift_two, cotangent,
):
    i, j = lax.axis_index("dp"), lax.axis_index("seq")
    zl, xc = j // 8, j % 8
    c = j % 2
    x, cot = tokens[0], cotangent[0]
    wq = jnp.concatenate(
        [lax.dynamic_slice_in_dim(w_qkv, n * D + xc * 128, 128, axis=1) for n in range(3)], axis=1
    )
    at_row = lax.broadcasted_iota(jnp.int32, (1024, 128), 0)
    at_col = lax.broadcasted_iota(jnp.int32, (1024, 128), 1)
    pick = (
        at_row == (at_col // 64) * 512 + ((at_col // 32) % 2) * 256 + xc * 32 + at_col % 32
    ).astype(BF)
    wu = jnp.concatenate(
        [
            jnp.dot(w_up[:, n * 1024 : (n + 1) * 1024], pick, preferred_element_type=F32).astype(BF)
            for n in range(4)
        ],
        axis=1,
    )
    wd = lax.dynamic_index_in_dim(w_down.reshape(2, 8, 32, D), xc, axis=1, keepdims=False)
    wd = wd.reshape(64, D)
    wo = lax.dynamic_slice_in_dim(w_out, c * 64, 64, axis=0)
    vec = jnp.concatenate(
        [
            out_bias, down_bias, gain_one, shift_one, gain_two, shift_two, up_bias, qv_bias,
            jnp.zeros((512,), BF),
        ]
    ).reshape(16, 128)
    n_lines = 14 + 14 + 21 + 1 + 2 + 7
    (n1, cg, wqg, wug, wdg, wog, vg, q, k, v, kr, vr, att, lse) = call(
        head_kernel, "gather_and_attend", 1, "vavaaav",
        [
            ("v", shape(8, T, D)), ("a", shape(8, T, D)), ("v", shape(8, 128, 384)),
            ("a", shape(8, 128, 512)), ("a", shape(8, 64, D)), ("a", shape(8, 2, 64, D)),
            ("v", shape(8, 16, 128)),
            *[("v", shape(1024, 128))] * 6,
            ("v", shape(1024, 128, of=F32)),
        ],
        [
            VMEM((8, T, D), BF), VMEM((8, D), F32), VMEM((8, 16, 128), F32),
            VMEM((1024, 128), F32), VMEM((1024, 128), F32),
            DMA((n_lines,)), DMA((n_lines,)), DMA((4,)),
        ],
        (x, cot, wq, wu, wd, wo, vec),
    )
    full_out = wog.reshape(D, D)
    flat = vg[:, :6].astype(F32)
    flat = jnp.moveaxis(flat, 1, 0).reshape(6, D)
    rows = jnp.stack([flat[0], flat[4], flat[5], flat[2], flat[1], flat[0], flat[0], flat[0]])
    ub = lax.dynamic_index_in_dim(vg[:, 6:10].reshape(8, 2, 8, 32), xc, axis=2, keepdims=False)
    ub = ub.reshape(512).astype(F32)
    mid, n2g = call(
        mid_kernel, "project_and_norm", 2, "vvvv",
        [("v", shape(T, D, of=F32)), ("v", shape(8, T, D))],
        [VMEM((T, D), BF), VMEM((T, D), BF), DMA((14,)), DMA((14,))],
        (att, x, full_out, rows),
    )
    n2 = n2g.reshape(D, D)
    cot_all = cg.reshape(D, D)
    w_up_here, w_down_here = wug.reshape(D, 512), wdg.reshape(512, D)
    pre = jnp.dot(n2, w_up_here, preferred_element_type=F32) + ub
    gelu, pull = jax.vjp(exact_gelu, pre)
    act = gelu.astype(BF)
    grad_act = dot(cot_all, w_down_here, 1, 1)
    grad_pre = pull(grad_act)[0].astype(BF)
    part_norm = dot(grad_pre, w_up_here, 1, 1).astype(BF).reshape(8, T, D)
    ends = jnp.dot(act, w_down_here, preferred_element_type=F32).astype(BF).reshape(8, T, D)
    dmid, dbg, sums = call(
        back_kernel, "norm_two_back", 3, "vvvv",
        [("v", shape(T, D, of=F32)), ("v", shape(8, T, D)), ("v", shape(8, D, of=F32))],
        [VMEM((T, D), BF), *REDUCE_SCRATCH, DMA((14,)), DMA((14,))],
        (part_norm, mid, cot, rows),
    )
    wdown_grad = dot(act, cot_all, 0, 0)
    wup_grad = dot(n2, grad_pre, 0, 0)
    up_sum = jnp.sum(grad_pre.astype(F32), axis=0)
    wout_grad, dqkv = call(
        pull_kernel, "attention_back", 4, "v" * 9,
        [("v", shape(128, D)), ("v", shape(D, 384))],
        [
            VMEM((1024, 128), BF), VMEM((1024, 128), F32), VMEM((1024, 128), F32),
            VMEM((128, 1024), F32), VMEM((128, 1024), F32),
            VMEM((2, 128, 1024), BF), VMEM((2, 128, 1024), BF), DMA((1,)), DMA((1,)),
        ],
        (dbg.reshape(D, D), full_out, att, q, k, v, kr, vr, lse),
    )
    wq_all = wqg.reshape(D, 384)
    part_one = dot(dqkv, wq_all, 1, 1).astype(BF).reshape(8, T, D)
    wqkv_grad = dot(n1.reshape(D, D), dqkv, 0, 0)
    qkv_sum = jnp.sum(dqkv.astype(F32), axis=0)
    shift_sum = jnp.sum(wq_all.astype(F32) * qkv_sum, axis=1)
    both_sum = jnp.sum(wq_all.astype(F32) * wqkv_grad, axis=1)
    gain_sum = (both_sum - flat[3] * shift_sum) / flat[2]
    vectors = jnp.stack([sums[2], sums[3], gain_sum, shift_sum, sums[0], sums[1]])
    vectors = jnp.moveaxis(vectors.reshape(6, 16, 64), 1, 0).reshape(16, 384)
    n = lax.broadcasted_iota(jnp.int32, (16, 1), 0)
    qv = jnp.where(n == xc, qkv_sum[0:128], jnp.where(n == 8 + xc, qkv_sum[256:384], 0.0))
    line = jnp.concatenate(
        [vectors, up_sum.reshape(16, 32), qv, jnp.zeros((16, 480), F32)], axis=1
    )
    ga = jnp.concatenate([wqkv_grad, wup_grad], axis=1).astype(BF).reshape(2, 4, 2, RA, CA)
    turned = jnp.moveaxis(wout_grad.reshape(2, 8, 8, D), 0, 1).reshape(16, 8, D)
    gb = jnp.concatenate(
        [
            wdown_grad.astype(BF).reshape(16, 32, D), turned,
            jnp.broadcast_to(line[:, None].astype(BF), (16, 8, D)),
        ],
        axis=1,
    ).reshape(2, 4, 2, RB, D)
    lines = 6 + 14 + 6 + 14 + 1
    xgrad, result, wide, tall, vecs = call(
        last_kernel, "reduce_gradients", 5, "v" * 8,
        [
            ("v", shape(T, D)), ("v", shape(T, D)), ("v", shape(8, 8, CA, of=F32)),
            ("v", shape(40, D, of=F32)), ("v", shape(8, 8, D, of=F32)),
        ],
        [
            *REDUCE_SCRATCH, *REDUCE_SCRATCH,
            VMEM((3, 2, 2, RA, CA), BF), VMEM((3, 4, RB, D), BF),
            VMEM((4, RA, CA), BF), VMEM((4, RB, D), BF),
            VMEM((3, RA, CA), BF), VMEM((3, RB, D), BF),
            VMEM((8, 8, CA), F32), VMEM((8, D), F32), VMEM((8, D), F32),
            DMA((lines,)), DMA((lines,)),
        ],
        (part_one, ends, ga, gb, x, dmid, mid, rows),
    )
    own = jnp.sum(vecs[:, 0, :], axis=0)
    small = lax.dynamic_slice_in_dim(own[:384].reshape(6, 64), xc * 8, 8, axis=1)
    up_bias_grad = lax.dynamic_index_in_dim(vecs[:, 0, 384:416], xc, axis=0, keepdims=False)
    qv_grad = lax.dynamic_slice_in_dim(own[416:544], xc * 16, 16, axis=0)
    w_qkv_grad = jnp.transpose(wide[:, :, :384].reshape(8, 8, 3, 128), (1, 2, 0, 3)).reshape(8, 3 * D)
    w_up_grad = jnp.transpose(
        wide[:, :, 384:].reshape(8, 8, 8, 2, 32), (1, 2, 3, 0, 4)
    ).reshape(8, 4 * D)
    return (
        result[None], xgrad[None], w_qkv_grad, qv_grad, tall[32:40], small[0], w_up_grad,
        up_bias_grad, tall[:32], small[1], small[2], small[3], small[4], small[5],
    )


def solution(mesh):
    return jax.shard_map(
        on_device,
        mesh=mesh,
        in_specs=(
            P("dp", "seq", None), P("dp", None), P("dp"), P("dp", None), P("dp"), P("dp", None),
            P("dp"), P("dp", None), P("dp"), P("dp"), P("dp"), P("dp"), P("dp"),
            P("dp", "seq", None),
        ),
        out_specs=(
            P("dp", "seq", None), P("dp", "seq", None), P(("dp", "seq"), None), P(("dp", "seq")),
            P(("dp", "seq"), None), P(("dp", "seq")), P(("dp", "seq"), None), P(("dp", "seq")),
            P(("dp", "seq"), None), P(("dp", "seq")), P(("dp", "seq")), P(("dp", "seq")),
            P(("dp", "seq")), P(("dp", "seq")),
        ),
        check_vma=False,
    )
```

time: 1060 us -> 263 us (0.25)
  waiting for transfers between devices: 647 us -> 0 us
  Pallas kernels: 0 us -> 202 us
  blocking collectives: 117 us -> 0 us
  local copies, waits for them, and re-layouts: 114 us -> 20.9 us
  matrix products: 110 us -> 32.2 us
  other arithmetic: 27.9 us -> 5.34 us
  starting transfers between devices: 16.2 us -> 0 us
  between operations: 16.9 us -> 1.25 us
    all_gather x4 -> x0, waiting for transfers between devices: 276 us -> none  [the longest x1 107 us: on_device(): lax.all_gather(w_up, 'dp', axis=0, tiled=True)]
    reduce_scatter x3 -> x0, waiting for transfers between devices: 247 us -> none  [the longest x2 247 us: sent_together(): filled = lax.psum_scatter(both, axis, scatter_dimension=dim, tiled=True)]
    pallas_call x0 -> x5, Pallas kernels: none -> 202 us  [call(): pl.pallas_call(kernel, name=name, in_specs=[any_spec() if s == 'a' else v...]
    unnamed x9 -> x0, waiting for transfers between devices: 101 us -> none
    dot_general x40 -> x12, matrix products: 110 us -> 32.2 us  [the longest x6 23 us: dot(): lax.dot_general(a, b, (((ca,), (cb,)), ((), ())), preferred_element_type=...]
    all_gather x4 -> x0, blocking collectives: 67.9 us -> none  [the longest x1 21.5 us: on_device(): lax.all_gather(qv_bias, 'dp', axis=0, tiled=True)]
    unnamed x1 -> x0, blocking collectives: 32.4 us -> none
    unnamed x77 -> x74, local copies, waits for them, and re-layouts: 39.7 us -> 7.5 us
  transfers between devices with their start and end apart: 11 -> 0, of which waited for: 9 -> 0; matrix products, arithmetic and copies ran while one was open for 10% -> 0% of each run, Pallas kernels for 0% -> 0%
where the time goes in v1:
time: 263 us; the launch traced here: 261 us
  Pallas kernels  202 us (77%)
  matrix products  32.2 us (12%)
  local copies, waits for them, and re-layouts  20.9 us (8%)
  other arithmetic  5.34 us (2%)
    pallas_call x5, Pallas kernels, call(): pl.pallas_call(kernel, name=name, in_specs=[any_spec() if s == 'a' else v...  202 us
    dot_general x6, matrix products, dot(): lax.dot_general(a, b, (((ca,), (cb,)), ((), ())), preferred_element_type=...  23 us
    unnamed x74, local copies, waits for them, and re-layouts  7.5 us

profile of v1, /device:TPU:1, one launch (start us, length us, event | category | flops | bytes accessed | tf_op | source)
XLA Modules:
  0.0 261.4 jit_solution(10680465308400901430)
XLA Ops:
  0.7 1.4 fusion.6
  2.1 0.3 fusion.7
  2.4 0.3 fusion.8
  2.8 0.3 fusion.9
  3.1 0.5 copy-done.17
  3.7 0.8 constant_dynamic-slice_fusion.6
  4.6 0.2 dynamic-update-slice
  4.8 0.2 dynamic-update-slice.1
  5.0 0.2 dynamic-update-slice.2
  5.2 0.2 dynamic-update-slice.3
  5.5 0.2 dynamic-update-slice.4
  5.7 0.2 dynamic-update-slice.5
  5.9 0.2 dynamic-update-slice.6
  6.1 0.2 dynamic-update-slice.7
  6.3 0.2 dynamic-update-slice.8
  6.5 67.7 %gather_and_attend.1 = (bf16[8,128,1024]{2,1,0:T(8,128)(2,1)}, bf16[8,128,1024]{2,1,0:T(8,128)(2,1)}, bf16[8,128,384]{2,1,0:T(8,128)(2,1)}, bf16[8,128,512]{2,1,...) custom-call(bf16[128,1024]{1,0:T(8,128)(2,1)} %bitcast.95, ...), custom_call_target="tpu_custom_call" | custom-call | tf_op jit(solution)/shard_map/gather_and_attend/pallas_call | solution.py:312
  74.2 0.7 copy-done.6
  75.1 0.9 copy-done.4
  76.0 28.8 %project_and_norm.1 = (f32[128,1024]{1,0:T(8,128)S(1)}, bf16[8,128,1024]{2,1,0:T(8,128)(2,1)}) custom-call(bf16[1024,128]{1,0:T(8,128)(2,1)S(1)} %copy-done.4, bf16[128,1024]{1,0:T(8,128)(2,1)S(1)} %bitcast.96, bf16[1024,1024]{1,0:T(8,128)(2,1)} %bitcast.105, f32[8,1024]{1,0:T(8,128)S(1)} %stack.13.rows), custom_call_target="tpu_custom_call" | custom-call | tf_op jit(solution)/shard_map/project_and_norm/pallas_call | solution.py:312
  104.8 4.4 %fusion.32 = f32[1024,512]{1,0:T(8,128)} fusion(bf16[1024,1024]{1,0:T(8,128)(2,1)} %bitcast.112, bf16[1024,512]{1,0:T(8,128)(2,1)S(1)} %bitcast.125), kind=kOutput, calls=%fused_computation.99 | convolution fusion | flops 1073741824 | bytes 5242880 | tf_op jit(solution)/shard_map/dot_general | solution.py:607
  109.3 0.1 reshape.278
  109.4 0.1 reshape.293
  109.5 8.3 %fusion.28 = (bf16[512]{0:T(512)(128)(2,1)S(1)}, bf16[1024,512]{1,0:T(8,128)(2,1)S(1)}, f32[1024,512]{1,0:T(8,128)S(1)}) fusion(f32[1024,512]{1,0:T(8,128)} %fusion.32, f32[512]{0:T(512)S(1)} %reshape.293, bf16[1024,1024]{1,0:T(8,128)(2,1)} %bitcast.114, bf16[512,1024]{1,0:T(8,128)(2,1)} %bitcast.123), kind=kOutput, calls=%fused_computation.96 | convolution fusion | flops 1112538624 | bytes 8391680 | tf_op jit(solution)/shard_map/dot_general | solution.py:157
  117.8 0.6 multiply_convert_fusion
  118.4 1.4 copy-done.12
  119.7 2.3 convolution_convert_fusion.3
  122.1 2.7 %convolution_convert_fusion.2 = bf16[1024,1024]{1,0:T(8,128)(2,1)} fusion(bf16[1024,512]{1,0:T(8,128)(2,1)S(1)} %get-tuple-element.69, bf16[1024,512]{1,0:T(8,128)(2,1)S(1)} %bitcast.126), kind=kOutput, calls=%fused_computation.19 | convolution fusion | flops 1074790400 | bytes 4194304 | tf_op jit(solution)/shard_map/dot_general | solution.py:157
  124.8 36.4 %norm_two_back.1 = (f32[128,1024]{1,0:T(8,128)S(1)}, bf16[8,128,1024]{2,1,0:T(8,128)(2,1)}, f32[8,1024]{1,0:T(8,128)S(1)}) custom-call(bf16[8,128,1024]{2,1,0:T(8,128)(2,1)} %bitcast.116, f32[128,1024]{1,0:T(8,128)S(1)} %get-tuple-element.47.mid, bf16[128,1024]{1,0:T(8,128)(2,1)S(1)} %bitcast.99, f32[8,1024]{1,0:T(8,128)S(1)} %stack.13.rows), custom_call_target="tpu_custom_call" | custom-call | tf_op jit(solution)/shard_map/norm_two_back/pallas_call | solution.py:312
  161.2 23.5 %attention_back.1 = (bf16[128,1024]{1,0:T(8,128)(2,1)S(1)}, bf16[1024,384]{1,0:T(8,128)(2,1)}) custom-call(bf16[1024,1024]{1,0:T(8,128)(2,1)} %bitcast.109, bf16[1024,1024]{1,0:T(8,128)(2,1)} %bitcast.106, bf16[1024,128]{1,0:T(8,128)(2,1)S(1)} %copy-done.5, bf16[1024,128]{1,0:T(8,128)(2,1)S(1)} %get-tuple-element.49.q, ...), custom_call_target="tpu_custom_call" | custom-call | tf_op jit(solution)/shard_map/attention_back/pallas_call | solution.py:312
  184.7 1.3 convert_reduce_fusion
  186.0 0.2 multiply_reduce_fusion
  186.2 0.1 reduce_sum.53
  186.3 4.3 %multiply_reduce_fusion.1 = (f32[1024]{0:T(1024)S(1)}, bf16[1024,384]{1,0:T(8,128)(2,1)}) fusion(bf16[8,128,384]{2,1,0:T(8,128)(2,1)} %get-tuple-element.56, bf16[1024,1024]{1,0:T(8,128)(2,1)} %bitcast.122, bf16[1024,384]{1,0:T(8,128)(2,1)} %get-tuple-element.55), kind=kOutput, calls=%fused_computation.24 | convolution fusion | flops 806878208 | bytes 4460544 | tf_op jit(solution)/shard_map/dot_general | solution.py:157
  190.5 0.1 reduce_sum.50
  190.6 0.1 squeeze.42
  190.8 0.1 stack.14
  190.9 0.1 stack.15
  191.1 0.1 concatenate.45
  191.2 0.1 select_convert_fusion
  191.3 0.1 concatenate.46
  191.4 0.1 pad.6.clone
  191.5 0.1 maximum_maximum_fusion
  191.6 1.3 pad_maximum_fusion.1.gb
  193.0 4.0 %copy.56 = bf16[1024,1024]{1,0:T(8,128)(2,1)} copy(bf16[1024,1024]{0,1:T(8,128)(2,1)} %bitcast.113) | data formatting | bytes 4194304 | tf_op jit(solution)/shard_map/dot_general | solution.py:157
  197.0 2.9 %convolution_convert_fusion.4 = bf16[2,4,2,64,512]{4,3,2,1,0:T(8,128)(2,1)S(1)} fusion(bf16[2,4,2,64,1024]{4,3,2,1,0:T(8,128)(2,1)} %bitcast.117, bf16[1024,512]{1,0:T(8,128)(2,1)S(1)} %copy-done.31), kind=kOutput, calls=%fused_computation.26 | convolution fusion | flops 1074266112 | bytes 4194304 | tf_op jit(solution)/shard_map/dot_general | solution.py:157
  199.9 1.5 pad_maximum_fusion.ga
  201.4 0.7 copy-done.27
  202.1 2.6 convolution_convert_fusion.1
  204.7 2.6 convolution_convert_fusion
  207.3 45.3 %reduce_gradients.1 = (bf16[128,1024]{1,0:T(8,128)(2,1)S(1)}, bf16[128,1024]{1,0:T(8,128)(2,1)S(1)}, f32[8,8,896]{2,1,0:T(8,128)S(1)}, f32[40,1024]{1,0:T(8,128)S(1)}, f32[8,8,1024]{2,1,0:T(8,128)S(1)}) custom-call(bf16[8,128,1024]{2,1,0:T(8,128)(2,1)} %bitcast.110, bf16[8,128,1024]{2,1,0:T(8,128)(2,1)} %bitcast.108, ...), custom_call_target="tpu_custom_call" | custom-call | tf_op jit(solution)/shard_map/reduce_gradients/pallas_call | solution.py:312
  252.6 0.4 reshape.291
  253.1 1.1 copy.63
  254.2 1.9 reshape.292
  256.1 0.6 copy.62
  256.8 0.7 slice.153
  257.5 0.1 reshape.290
  257.5 0.1 constant_dynamic-slice_fusion.1
  257.6 0.5 slice_bitcast_fusion.6
  258.2 0.6 slice.148
  258.8 0.1 slice.147
  258.8 0.6 dynamic_slice.36
  259.4 0.5 fusion.23
  259.9 0.7 copy.81
  260.7 0.7 copy.82
  (94 shorter events, 0.7 us)
Async XLA Ops:
  0.6 3.9 %copy-start = (bf16[512,1024]{1,0:T(8,128)(2,1)S(1)}, bf16[512,1024]{1,0:T(8,128)(2,1)}, u32[]{:S(2)}) copy-start(bf16[512,1024]{1,0:T(8,128)(2,1)} %param.21) | copy-start | bytes 3145732
  0.7 1.5 copy-start.26
  2.7 1.0 copy-start.17
  2.7 1.9 copy-start.19
  2.7 2.1 copy-start.20
  2.7 2.3 copy-start.21
  2.7 2.5 copy-start.22
  2.7 2.7 %copy-start.23 = (bf16[128]{0:T(256)(128)(2,1)S(1)}, bf16[128]{0:T(256)(128)(2,1)}, u32[]{:S(2)}) copy-start(bf16[128]{0:T(256)(128)(2,1)} %param.25) | copy-start | bytes 772
  2.8 2.9 %copy-start.24 = (bf16[128]{0:T(256)(128)(2,1)S(1)}, bf16[128]{0:T(256)(128)(2,1)}, u32[]{:S(2)}) copy-start(bf16[128]{0:T(256)(128)(2,1)} %param.26) | copy-start | bytes 772
  2.8 3.1 %copy-start.18 = (bf16[512]{0:T(512)(128)(2,1)S(1)}, bf16[512]{0:T(512)(128)(2,1)}, u32[]{:S(2)}) copy-start(bf16[512]{0:T(512)(128)(2,1)} %param.20) | copy-start | bytes 3076
  2.8 3.3 %copy-start.25 = (bf16[256]{0:T(256)(128)(2,1)S(1)}, bf16[256]{0:T(256)(128)(2,1)}, u32[]{:S(2)}) copy-start(bf16[256]{0:T(256)(128)(2,1)} %param.16) | copy-start | bytes 1540
  3.1 72.0 %copy-start.1 = (bf16[1,128,1024]{2,1,0:T(8,128)(2,1)S(1)}, bf16[1,128,1024]{2,1,0:T(8,128)(2,1)}, u32[]{:S(2)}) copy-start(bf16[1,128,1024]{2,1,0:T(8,128)(2,1)} %param.14) | copy-start | bytes 786436
  74.2 0.7 copy-start.6
  75.0 1.0 copy-start.4
  76.0 28.8 %copy-start.28 = (bf16[8,128,512]{2,1,0:T(8,128)(2,1)S(1)}, bf16[8,128,512]{2,1,0:T(8,128)(2,1)}, u32[]{:S(2)}) copy-start(bf16[8,128,512]{2,1,0:T(8,128)(2,1)} %get-tuple-element.44) | copy-start | bytes 3145732
  104.8 20.0 %copy-start.2 = (f32[128,1024]{1,0:T(8,128)}, f32[128,1024]{1,0:T(8,128)S(1)}, u32[]{:S(2)}) copy-start(f32[128,1024]{1,0:T(8,128)S(1)} %get-tuple-element.47.mid) | copy-start | bytes 1572868
  109.5 8.3 %copy-start.11 = (f32[1024,512]{1,0:T(8,128)S(1)}, f32[1024,512]{1,0:T(8,128)}, u32[]{:S(2)}) copy-start(f32[1024,512]{1,0:T(8,128)} %fusion.32) | copy-start | bytes 6291460
  117.8 4.3 %copy-start.30 = (bf16[1024,512]{1,0:T(8,128)(2,1)}, bf16[1024,512]{1,0:T(8,128)(2,1)S(1)}, u32[]{:S(2)}) copy-start(bf16[1024,512]{1,0:T(8,128)(2,1)S(1)} %get-tuple-element.69) | copy-start | bytes 3145732
  117.8 2.0 copy-start.12
  119.7 2.3 copy-start.8
  119.7 2.3 copy-start.29
  122.0 2.7 %copy-start.3 = (bf16[1,128,1024]{2,1,0:T(8,128)(2,1)S(1)}, bf16[1,128,1024]{2,1,0:T(8,128)(2,1)}, u32[]{:S(2)}) copy-start(bf16[1,128,1024]{2,1,0:T(8,128)(2,1)} %param.27) | copy-start | bytes 786436
  124.7 36.4 %copy-start.5 = (bf16[1024,128]{1,0:T(8,128)(2,1)S(1)}, bf16[1024,128]{1,0:T(8,128)(2,1)}, u32[]{:S(2)}) copy-start(bf16[1024,128]{1,0:T(8,128)(2,1)} %get-tuple-element.40.att) | copy-start | bytes 786436
  124.7 36.4 %copy-start.7 = (bf16[1024,128]{1,0:T(8,128)(2,1)S(1)}, bf16[1024,128]{1,0:T(8,128)(2,1)}, u32[]{:S(2)}) copy-start(bf16[1024,128]{1,0:T(8,128)(2,1)} %copy-done.6) | copy-start | bytes 786436
  161.2 24.8 %copy-start.14 = (bf16[8,128,384]{2,1,0:T(8,128)(2,1)S(1)}, bf16[8,128,384]{2,1,0:T(8,128)(2,1)}, u32[]{:S(2)}) copy-start(bf16[8,128,384]{2,1,0:T(8,128)(2,1)} %get-tuple-element.56) | copy-start | bytes 2359300
  186.3 5.3 %copy-start.10 = (bf16[512,1024]{1,0:T(8,128)(2,1)S(1)}, bf16[512,1024]{1,0:T(8,128)(2,1)}, u32[]{:S(2)}) copy-start(bf16[512,1024]{1,0:T(8,128)(2,1)} %convolution_convert_fusion.3) | copy-start | bytes 3145732
  193.0 4.0 %copy-start.31 = (bf16[1024,512]{1,0:T(8,128)(2,1)S(1)}, bf16[1024,512]{1,0:T(8,128)(2,1)}, u32[]{:S(2)}) copy-start(bf16[1024,512]{1,0:T(8,128)(2,1)} %copy-done.30) | copy-start | bytes 3145732
  197.0 2.9 %copy-start.13 = (bf16[1024,384]{1,0:T(8,128)(2,1)S(1)}, bf16[1024,384]{1,0:T(8,128)(2,1)}, u32[]{:S(2)}) copy-start(bf16[1024,384]{1,0:T(8,128)(2,1)} %get-tuple-element.72) | copy-start | bytes 2359300
  199.9 1.5 copy-start.9
  199.9 2.2 copy-start.27
  202.1 2.6 copy-start.15
  202.1 2.6 copy-start.16

commit v2 on v1

v2 whole, which is shorter than its diff:
```python
import functools

import jax
import jax.numpy as jnp
from jax import lax
from jax.experimental import pallas as pl
from jax.experimental.pallas import tpu as pltpu
from jax.sharding import PartitionSpec as P

MESH = pl.DeviceIdType.MESH
EPS = 1e-06
BF = jnp.bfloat16
F32 = jnp.float32
D = 1024
T = 128
VMEM = pltpu.VMEM
ANY = pl.ANY
DMA = pltpu.SemaphoreType.DMA


class Place:
    def __init__(self):
        self.i, self.j = lax.axis_index("dp"), lax.axis_index("seq")
        self.zh, self.y = self.i // 4, self.i % 4
        self.zl, self.xc = self.j // 8, self.j % 8
        self.x, self.c = self.xc // 2, self.xc % 2
        self.z = self.zh * 2 + self.zl

    def in_group(self, dx, dc):
        return (self.i, self.zl * 8 + ((self.x + dx) % 4) * 2 + (self.c + dc) % 2)

    def sibling(self):
        return self.in_group(0, 1)

    def across(self):
        return (self.i, (1 - self.zl) * 8 + self.xc)

    def along_y(self, dy):
        return (self.zh * 4 + (self.y + dy) % 4, self.j)

    def along_z(self, dz):
        z = (self.z + dz) % 4
        return ((z // 2) * 4 + self.y, (z % 2) * 8 + self.xc)

    def holder(self, dh, dy):
        near = (self.zl + dh) % 2
        return (((self.zh + dh) % 2) * 4 + (self.y + dy) % 4, near * 8 + self.xc)


GROUP = [(dx, dc) for dx in range(4) for dc in range(2) if (dx, dc) != (0, 0)]
RING = [(1, 0), (3, 0), (2, 0), (0, 1)]
HOLDERS = [(dh, dy) for dh in range(2) for dy in range(4) if (dh, dy) != (0, 0)]


def greet(devices, more=0):
    barrier = pltpu.get_barrier_semaphore()
    for device in devices:
        pl.semaphore_signal(barrier, inc=1, device_id=device, device_id_type=MESH)
    pl.semaphore_wait(barrier, len(devices) + more)


class Lines:
    def __init__(self, send, recv):
        self.send, self.recv, self.used = send, recv, 0

    def copy(self, src, dst, device):
        k = self.used
        self.used += 1
        return pltpu.make_async_remote_copy(
            src_ref=src,
            dst_ref=dst,
            send_sem=self.send.at[k],
            recv_sem=self.recv.at[k],
            device_id=device,
            device_id_type=MESH,
        )


def slot_of(ref, k, size=T):
    return ref.at[pl.ds(pl.multiple_of(k * size, size), size)]


class Gather:
    def __init__(self, at, lines, own, slot):
        self.at, self.lines, self.slot = at, lines, slot
        self.ring, self.forwards = {}, {}
        for dx in (1, 3, 2):
            self.ring[dx] = lines.copy(own, slot(at.xc), at.in_group(dx, 0))
            self.ring[dx].start()
        self.beside = lines.copy(own, slot(at.xc), at.sibling())
        self.beside.start()

    def forward(self, dx):
        at = self.at
        self.ring[dx].wait_recv()
        here = self.slot(((at.x + 4 - dx) % 4) * 2 + at.c)
        self.forwards[dx] = self.lines.copy(here, here, at.sibling())
        self.forwards[dx].start()

    def arrived(self, dx):
        (self.forwards[dx] if dx else self.beside).wait_recv()

    def sent(self):
        self.beside.wait_send()
        for dx in (1, 3, 2):
            self.forwards[dx].wait_send()
            self.ring[dx].wait_send()

    def finish(self):
        for dx in (1, 3, 2):
            self.forward(dx)
        for dx in (0, 1, 3, 2):
            self.arrived(dx)
        self.sent()


class Reduce:
    def __init__(self, at, lines, slot, from_core, sums, from_ring):
        self.at, self.lines, self.slot = at, lines, slot
        self.from_core, self.sums, self.from_ring = from_core, sums, from_ring
        self.cores, self.ring = {}, {}

    def core(self, dx):
        at = self.at
        theirs = self.slot(((at.x + dx) % 4) * 2 + 1 - at.c)
        self.cores[dx] = self.lines.copy(theirs, self.from_core.at[dx], at.sibling())
        self.cores[dx].start()

    def pass_on(self, dx):
        at = self.at
        self.cores[dx].wait_recv()
        mine = self.slot(((at.x + dx) % 4) * 2 + at.c)
        self.sums[dx] = (mine[...].astype(F32) + self.from_core[dx].astype(F32)).astype(BF)
        copy = self.lines.copy(self.sums.at[dx], self.from_ring.at[dx], at.in_group(dx, 0))
        copy.start()
        self.ring[dx] = copy

    def total(self):
        self.cores[0].wait_recv()
        total = self.slot(self.at.xc)[...].astype(F32) + self.from_core[0].astype(F32)
        for dx, copy in self.ring.items():
            copy.wait_recv()
            total = total + self.from_ring[dx].astype(F32)
        return total

    def sent(self):
        for copy in [*self.cores.values(), *self.ring.values()]:
            copy.wait_send()


REDUCE_SCRATCH = [VMEM((4, T, D), BF), VMEM((4, T, D), BF), VMEM((4, T, D), BF)]


def normed(values):
    center = values - jnp.mean(values, axis=-1, keepdims=True)
    rstd = lax.rsqrt(jnp.mean(center * center, axis=-1, keepdims=True) + EPS)
    return center * rstd, rstd


def lanes_of(head, value):
    lane = lax.broadcasted_iota(jnp.int32, (1, 128), 1)
    mine = (lane < 64) if head == 0 else (lane >= 64)
    return jnp.where(mine, value, 0.0).astype(F32)


def by_head(zero, one):
    lane = lax.broadcasted_iota(jnp.int32, (1, 128), 1)
    return jnp.where(lane < 64, zero, one)


def dot(a, b, ca, cb):
    return lax.dot_general(a, b, (((ca,), (cb,)), ((), ())), preferred_element_type=F32)


QB = 256


def head_kernel(
    tok, cot, wq, wu, wd, wo, vec,
    n1, cg, wqg, wug, wdg, wog, vg, q, k, v, kr, vr, att, lse,
    xg, rows, bias, top, total, send, recv, local,
):
    at = Place()
    greet(
        [at.in_group(*d) for d in RING]
        + [at.holder(*d) for d in HOLDERS]
        + [at.across()]
    )
    lines = Lines(send, recv)
    first = []
    for dh, dy in HOLDERS:
        for src, dst in ((vec, vg.at[at.i]), (wq, wqg.at[at.i])):
            copy = lines.copy(src, dst, at.holder(dh, dy))
            copy.start()
            first.append(copy)
    x_in = Gather(at, lines, tok, lambda k: xg.at[k])
    own = [
        pltpu.make_async_copy(src, dst, local.at[n])
        for n, (src, dst) in enumerate(
            (
                (cot, cg.at[at.xc]),
                (wu, wug.at[at.i]),
                (wd, wdg.at[at.i]),
                (wo, wog.at[at.i, at.c]),
            )
        )
    ]
    for copy in own:
        copy.start()
    xg[at.xc] = tok[...]
    vg[at.i] = vec[...]
    wqg[at.i] = wq[...]
    later, halves = [], []
    for dh, dy in HOLDERS:
        device = at.holder(dh, dy)
        copy = lines.copy(wo, wog.at[at.i, at.c], device)
        copy.start()
        halves.append((dh, dy, copy))
        for src, dst in ((wu, wug.at[at.i]), (wd, wdg.at[at.i])):
            copy = lines.copy(src, dst, device)
            copy.start()
            later.append(copy)
    beside = lines.copy(wo, wog.at[at.i, at.c], at.sibling())
    beside.start()
    later.append(beside)
    for copy in first:
        copy.wait()
    for d in range(8):
        for r in range(2):
            rows[r : r + 1, d * 128 : (d + 1) * 128] = vg[d, 2 + r : 3 + r, :].astype(F32)
    for d in range(8):
        bias[d] = vg[d].astype(F32)
    x_in.finish()
    cot_in = Gather(at, lines, cot, lambda k: cg.at[k])

    gain, shift = rows[0:1, :], rows[1:2, :]

    def norm_step(b, _):
        hat, _ = normed(xg[b].astype(F32))
        n1[b] = (hat * gain + shift).astype(BF)
        return 0

    lax.fori_loop(0, 8, norm_step, 0)
    at_row = pl.ds(10 + at.xc % 2, 1)
    q_bias = bias[at.xc // 2, at_row, :]
    v_bias = bias[4 + at.xc // 2, at_row, :]

    def kv_step(b, _):
        part = pl.ds(pl.multiple_of(b * T, T), T)
        acc = dot(n1[b], wqg[...].reshape(D, 384), 1, 0)
        q[part, :] = (acc[:, 0:128] + q_bias).astype(BF)
        k[part, :] = acc[:, 128:256].astype(BF)
        v[part, :] = (acc[:, 256:384] + v_bias).astype(BF)
        return 0

    lax.fori_loop(0, 8, kv_step, 0)
    swaps = [lines.copy(k, kr, at.across()), lines.copy(v, vr, at.across())]
    for copy in swaps:
        copy.start()

    def attend(keys, values, fresh):
        def step(t, _):
            part = pl.ds(pl.multiple_of(t * QB, QB), QB)
            block = q[part, :]
            tops, sums, outs, fades = [], [], [], []
            for h in range(2):
                mine = block * lanes_of(h, 0.125).astype(BF)
                score = dot(mine, keys[...], 1, 1)
                peak = jnp.max(score, axis=-1, keepdims=True)
                if not fresh:
                    old = top[part, 64 * h : 64 * h + 1]
                    peak = jnp.maximum(old, peak)
                    fades.append(jnp.exp(old - peak))
                expo = jnp.exp(score - peak)
                tops.append(peak)
                sums.append(jnp.sum(expo, axis=-1, keepdims=True))
                outs.append(dot(expo.astype(BF), values[...], 1, 0))
            peak, added, out = by_head(*tops), by_head(*sums), by_head(*outs)
            if fresh:
                top[part, :] = peak
                lse[part, :] = added
                total[part, :] = out
            else:
                fade = by_head(*fades)
                mass = lse[part, :] * fade + added
                att[part, :] = ((total[part, :] * fade + out) / mass).astype(BF)
                lse[part, :] = peak + jnp.log(mass)
            return 0

        lax.fori_loop(0, 1024 // QB, step, 0)

    attend(k, v, True)
    for copy in swaps:
        copy.wait()
    attend(kr, vr, False)
    cot_in.finish()
    forwards = []
    for dh, dy, copy in halves:
        copy.wait_recv()
        holder = ((at.zh + dh) % 2) * 4 + (at.y + 4 - dy) % 4
        forward = lines.copy(wog.at[holder, at.c], wog.at[holder, at.c], at.sibling())
        forward.start()
        forwards.append(forward)
    for copy in later:
        copy.wait()
    for _, _, copy in halves:
        copy.wait_send()
    for copy in forwards:
        copy.wait()
    for copy in own:
        copy.wait()


def any_spec():
    return pl.BlockSpec(memory_space=ANY)


def vm_spec():
    return pl.BlockSpec(memory_space=VMEM)


def shape(*dims, of=BF):
    return jax.ShapeDtypeStruct(dims, of)


def call(kernel, name, ident, ins, outs, scratch, args):
    return pl.pallas_call(
        kernel,
        name=name,
        in_specs=[any_spec() if s == "a" else vm_spec() for s in ins],
        out_specs=[any_spec() if s == "a" else vm_spec() for s, _ in outs],
        out_shape=[o for _, o in outs],
        scratch_shapes=scratch,
        compiler_params=pltpu.CompilerParams(
            collective_id=ident, has_side_effects=True, vmem_limit_bytes=52 * 2**20
        ),
    )(*args)


def norm_back(pulled, hat, rstd, gain):
    scaled = pulled * gain
    inner = jnp.mean(scaled * hat, axis=-1, keepdims=True)
    return rstd * (scaled - jnp.mean(scaled, axis=-1, keepdims=True) - hat * inner)


def mlp_kernel(
    att, x, cot, rows, ub, wout_at, wu_at, wd_at, cg_at,
    mid, dmid, dbg, ends, wup_grad, wdown_grad, sums, up_sum,
    wout, wu, wd, cg, mixed, own, low, n2g, act, dpre, parts, core, part, ring, local, send, recv,
):
    at = Place()
    loads = [
        pltpu.make_async_copy(src, dst, local.at[n])
        for n, (src, dst) in enumerate(((wout_at, wout), (wu_at, wu), (wd_at, wd), (cg_at, cg)))
    ]
    for load in loads:
        load.start()
    greet([at.in_group(*d) for d in GROUP])
    lines = Lines(send, recv)
    mine = pl.ds(pl.multiple_of(at.xc * 128, 128), 128)
    copies = []
    for dx, dc in GROUP:
        to = ((at.x + dx) % 4) * 2 + (at.c + dc) % 2
        copy = lines.copy(slot_of(att, to), mixed.at[:, mine], at.in_group(dx, dc))
        copy.start()
        copies.append(copy)
    mixed[:, mine] = slot_of(att, at.xc)[...]
    loads[0].wait()
    for copy in copies:
        copy.wait_recv()
    middle = x[...].astype(F32) + dot(mixed[...], wout[...], 1, 0) + rows[0:1, :]
    mid[...] = middle
    hat, rstd = normed(middle)
    own[...] = (hat * rows[4:5, :] + rows[5:6, :]).astype(BF)
    tokens_in = Gather(at, lines, own, lambda k: slot_of(n2g, k))
    slot_of(n2g, at.xc)[...] = own[...]
    for load in loads[1:]:
        load.wait()
    up_sum[...] = jnp.zeros_like(up_sum)
    out = Reduce(at, lines, lambda k: slot_of(parts, k), core, part, ring)

    def pair(dx):
        here = pl.ds(pl.multiple_of(((at.x + 4 - dx) % 4) * 256, 256), 256)
        pre = dot(n2g[here, :], wu[...], 1, 0) + ub[...]
        grad = dot(cg[here, :], wd[...], 1, 1)
        cdf = 0.5 * (1.0 + lax.erf(pre * (0.5**0.5)))
        act[here, :] = (pre * cdf).astype(BF)
        slope = cdf + pre * (jnp.exp(-0.5 * pre * pre) * 0.3989422804014327)
        back = (grad * slope).astype(BF)
        dpre[here, :] = back
        up_sum[...] += jnp.sum(back.astype(F32), axis=0, keepdims=True)
        parts[here, :] = dot(back, wu[...], 1, 1).astype(BF)
        out.core((4 - dx) % 4)

    tokens_in.arrived(0)
    pair(0)
    tokens_in.forward(1)
    tokens_in.forward(3)
    tokens_in.arrived(1)
    pair(1)
    tokens_in.forward(2)
    tokens_in.arrived(3)
    pair(3)
    out.pass_on(3)
    tokens_in.arrived(2)
    pair(2)
    out.pass_on(1)
    out.pass_on(2)

    def end_step(b, _):
        here = pl.ds(pl.multiple_of(b * 256, 256), 256)
        ends[here, :] = dot(act[here, :], wd[...], 1, 0).astype(BF)
        return 0

    lax.fori_loop(0, 4, end_step, 0)
    wdown_grad[...] = dot(act[...], cg[...], 0, 0).astype(BF)
    pulled = out.total()
    sums[4:5, :] = jnp.sum(pulled * hat, axis=0, keepdims=True)
    sums[5:6, :] = jnp.sum(pulled, axis=0, keepdims=True)
    given = cot[...].astype(F32)
    middle = given + norm_back(pulled, hat, rstd, rows[4:5, :])
    dmid[...] = middle
    low[...] = middle.astype(BF)
    back_in = Gather(at, lines, low, lambda k: slot_of(dbg, k))
    slot_of(dbg, at.xc)[...] = low[...]
    sums[0:1, :] = jnp.sum(low[...].astype(F32), axis=0, keepdims=True)
    sums[1:2, :] = jnp.sum(given, axis=0, keepdims=True)
    sums[2:4, :] = jnp.zeros((2, D), F32)
    sums[6:8, :] = jnp.zeros((2, D), F32)
    wup_grad[...] = dot(n2g[...], dpre[...], 0, 0).astype(BF)
    back_in.finish()
    tokens_in.sent()
    out.sent()
    for copy in copies:
        copy.wait_send()


class Halving:
    def __init__(self, at, lines, whole, first, sums, second, y_first, cut=None):
        self.at, self.lines, self.whole, self.y_first = at, lines, whole, y_first
        self.first, self.sums, self.second = first, sums, second
        self.cut = () if cut is None else (slice(None),) * 2 + (cut,)
        self.one, self.two = [], []

    def block(self, y, z):
        return self.whole[(z // 2, y, z % 2) + self.cut[2:]]

    def start(self):
        at = self.at
        for d in (2, 1, 3):
            if self.y_first:
                to, device = (slice(None), (at.y + d) % 4, slice(None)), at.along_y(d)
            else:
                z = (at.z + d) % 4
                to, device = (z // 2, slice(None), z % 2), at.along_z(d)
            copy = self.lines.copy(self.whole.at[to + self.cut[2:]], self.first.at[d - 1], device)
            copy.start()
            self.one.append(copy)

    def turn(self):
        at = self.at
        for copy in self.one:
            copy.wait_recv()
        for n in range(4):
            acc = self.block(at.y, n) if self.y_first else self.block(n, at.z)
            acc = acc.astype(F32)
            for d in range(3):
                got = self.first[d, n // 2, n % 2] if self.y_first else self.first[d, n]
                acc = acc + got.astype(F32)
            self.sums[n] = acc.astype(self.sums.dtype)
        for d in (2, 1, 3):
            if self.y_first:
                to, device = (at.z + d) % 4, at.along_z(d)
            else:
                to, device = (at.y + d) % 4, at.along_y(d)
            copy = self.lines.copy(self.sums.at[to], self.second.at[d - 1], device)
            copy.start()
            self.two.append(copy)

    def total(self):
        for copy in self.two:
            copy.wait_recv()
        acc = self.sums[self.at.z if self.y_first else self.at.y].astype(F32)
        for d in range(3):
            acc = acc + self.second[d].astype(F32)
        return acc

    def sent(self):
        for copy in self.one + self.two:
            copy.wait_send()


def halving_scratch(y_first, dims, of=BF):
    lead = (3, 2, 2) if y_first else (3, 4)
    return [VMEM(lead + dims, of), VMEM((4,) + dims, of), VMEM((3,) + dims, of)]


def pull_kernel(
    db_at, wout_at, n1_at, wq_at, att, q, k, v, kr, vr, lse,
    ends, wup_grad, wdown_grad, tok, dmid, mid, rows, sums, up_sum,
    xgrad, result, wide_q, wide_u, wdown_out, wout_out, small,
    db, wout, n1, wq,
    do, delta, dq, dk, dv, away, back, dqkv, parts,
    core, part, ring, core2, part2, ring2,
    wout_grad, wqkv_grad, points,
    u1, u2, u3, d1, d2, d3, o1, o2, o3, p1, p2, p3, g1, g2, g3, v1, v2, v3,
    low_u, low_q, turn, point, local, send, recv,
):
    at = Place()
    loads = [
        pltpu.make_async_copy(src, dst, local.at[n])
        for n, (src, dst) in enumerate(((db_at, db), (wout_at, wout), (n1_at, n1), (wq_at, wq)))
    ]
    for load in loads:
        load.start()
    swapped = (at.xc, at.zl * 8 + at.i)
    barrier = pltpu.get_barrier_semaphore()

    @pl.when(at.i != at.xc)
    def _():
        pl.semaphore_signal(barrier, inc=1, device_id=swapped, device_id_type=MESH)

    greet(
        [at.in_group(*d) for d in GROUP]
        + [at.along_y(d) for d in (1, 2, 3)]
        + [at.along_z(d) for d in (1, 2, 3)],
        jnp.where(at.i != at.xc, 1, 0),
    )
    lines = Lines(send, recv)
    ups = Halving(at, lines, wup_grad, u1, u2, u3, True)
    downs = Halving(at, lines, wdown_grad, d1, d2, d3, False)
    outs = Halving(at, lines, wout_grad, o1, o2, o3, False)
    ups.start()
    downs.start()
    closing = Reduce(at, lines, lambda n: slot_of(ends, n), core2, part2, ring2)
    for dx in (2, 1, 3, 0):
        closing.core(dx)
    for load in loads:
        load.wait()
    rows_w = wout[pl.ds(pl.multiple_of(at.xc * 128, 128), 128), :]
    grads = dot(db[...], rows_w, 1, 1).astype(BF)
    do[...] = grads
    made = dot(att[...], db[...], 0, 0)
    for zl in range(2):
        for i in range(8):
            b = (zl * 8 + i) * 8
            wout_grad[i // 4, i % 4, zl] = made[b : b + 8, :]
    outs.start()
    both = grads.astype(F32) * att[...].astype(F32)
    delta[...] = by_head(
        jnp.sum(both * lanes_of(0, 1.0), axis=-1, keepdims=True),
        jnp.sum(both * lanes_of(1, 1.0), axis=-1, keepdims=True),
    )
    for dx in (2, 1, 3):
        closing.pass_on(dx)

    def pull(keys, values, fresh):
        dk[...] = jnp.zeros_like(dk)
        dv[...] = jnp.zeros_like(dv)

        def step(t, _):
            part = pl.ds(pl.multiple_of(t * QB, QB), QB)
            block, grad = q[part, :], do[part, :]
            outs = []
            for h in range(2):
                mine = block * lanes_of(h, 0.125).astype(BF)
                pulled = grad * lanes_of(h, 1.0).astype(BF)
                prob = jnp.exp(dot(mine, keys[...], 1, 1) - lse[part, 64 * h : 64 * h + 1])
                dprob = dot(pulled, values[...], 1, 1)
                raw = (prob * (dprob - delta[part, 64 * h : 64 * h + 1])).astype(BF)
                dv[...] += dot(pulled, prob.astype(BF), 0, 0)
                dk[...] += dot(mine, raw, 0, 0)
                outs.append(dot(raw, keys[...], 1, 0))
            out = by_head(*outs) * 0.125
            dq[part, :] = out if fresh else dq[part, :] + out
            return 0

        lax.fori_loop(0, 1024 // QB, step, 0)

    pull(kr, vr, True)
    away[0] = dk[...].astype(BF)
    away[1] = dv[...].astype(BF)
    swap = lines.copy(away, back, at.across())
    swap.start()
    ups.turn()
    downs.turn()
    outs.turn()
    pull(k, v, False)
    swap.wait()
    dqkv[:, 0:128] = dq[...].astype(BF)
    dqkv[:, 128:256] = jnp.transpose(dk[...] + back[0].astype(F32)).astype(BF)
    dqkv[:, 256:384] = jnp.transpose(dv[...] + back[1].astype(F32)).astype(BF)

    inner = Reduce(at, lines, lambda n: slot_of(parts, n), core, part, ring)
    shift_sum = jnp.zeros((1, D), F32)
    both_sum = jnp.zeros((1, D), F32)
    before = None
    for dx in (2, 1, 3, 0):
        here = pl.ds(pl.multiple_of(((at.x + dx) % 4) * 256, 256), 256)
        made = dot(dqkv[here, :], wq[...], 1, 1)
        parts[here, :] = made.astype(BF)
        inner.core(dx)
        shift_sum = shift_sum + jnp.sum(made, axis=0, keepdims=True)
        both_sum = both_sum + jnp.sum(made * n1[here, :].astype(F32), axis=0, keepdims=True)
        if before is not None:
            inner.pass_on(before)
        before = dx
    made = dot(n1[...], dqkv[...], 0, 0).astype(BF)
    for n in range(16):
        wqkv_grad[n // 8, (n // 2) % 4, n % 2] = made[n * 64 : n * 64 + 64, :]
    firsts = Halving(at, lines, wqkv_grad, p1, p2, p3, True, slice(0, 32))
    seconds = Halving(at, lines, wqkv_grad, g1, g2, g3, False, slice(32, 64))
    firsts.start()
    seconds.start()
    qkv_sum = jnp.sum(dqkv[...].astype(F32), axis=0, keepdims=True)
    gain_sum = (both_sum - rows[3:4, :] * shift_sum) / rows[2:3, :]
    for n in range(16):
        wide = slice((n // 2) * 128, (n // 2) * 128 + 128)
        to = (n // 8, (n // 2) % 4, n % 2)
        points[to + (slice(0, 2),)] = sums[0:2, wide]
        points[to + (slice(2, 3),)] = gain_sum[:, wide]
        points[to + (slice(3, 4),)] = shift_sum[:, wide]
        points[to + (slice(4, 6),)] = sums[4:6, wide]
        points[to + (slice(6, 7),)] = up_sum[:, (n // 4) * 128 : (n // 4) * 128 + 128]
        mine = qkv_sum[:, 0:128] if n < 8 else qkv_sum[:, 256:384]
        points[to + (slice(7, 8),)] = jnp.where(at.xc == n % 8, mine, 0.0)
    vectors = Halving(at, lines, points, v1, v2, v3, True)
    vectors.start()
    third = []

    def to_group(src, dst):
        for dx, dc in GROUP:
            to = ((at.x + dx) % 4) * 2 + (at.c + dc) % 2
            copy = lines.copy(src(to), dst, at.in_group(dx, dc))
            copy.start()
            third.append(copy)

    acc = ups.total()
    for b in range(8):
        low_u[b] = acc[b * 8 : (b + 1) * 8, :]
    to_group(lambda n: low_u.at[n], wide_u.at[at.xc])
    wide_u[at.xc] = low_u[at.xc]
    wdown_out[...] = downs.total()
    turn[...] = outs.total()
    across = lines.copy(turn, wout_out, swapped)

    @pl.when(at.i != at.xc)
    def _():
        across.start()

    @pl.when(at.i == at.xc)
    def _():
        wout_out[...] = turn[...]

    result[...] = (mid[...] + closing.total() + rows[1:2, :]).astype(BF)
    vectors.turn()
    firsts.turn()
    seconds.turn()
    pulled = inner.total()
    hat, rstd = normed(tok[...].astype(F32))
    xgrad[...] = (dmid[...] + norm_back(pulled, hat, rstd, rows[2:3, :])).astype(BF)
    point[...] = vectors.total()
    to_group(lambda n: point, small.at[at.xc])
    small[at.xc] = point[...]
    for half, acc in enumerate((firsts.total(), seconds.total())):
        for b in range(4):
            low_q[half * 4 + b] = acc[b * 8 : (b + 1) * 8, :]
    to_group(lambda n: low_q.at[n], wide_q.at[at.xc])
    wide_q[at.xc] = low_q[at.xc]

    @pl.when(at.i != at.xc)
    def _():
        across.wait()

    for copy in third:
        copy.wait()
    for part_sum in (ups, downs, outs, firsts, seconds, vectors, inner, closing):
        part_sum.sent()


def lay_kernel(
    xgrad_at, result_at, wide_q, wide_u, wdown_at, wout_at, small,
    result, xgrad, wqkv, qv, wout, ob, wup, ub, wdown, db, g1, s1, g2, s2,
):
    at = Place()
    xgrad[...] = xgrad_at[...]
    result[...] = result_at[...]
    wdown[...] = wdown_at[...]
    wout[...] = wout_at[...]
    for n in range(3):
        for b in range(8):
            wqkv[:, n * D + b * 128 : n * D + b * 128 + 128] = wide_q[b, :, n * 128 : n * 128 + 128]
    lane = lax.broadcasted_iota(jnp.int32, (8, 128), 1)
    for m in range(16):
        for half in range(2):
            out = jnp.zeros((8, 128), F32)
            for b in range(4):
                word = wide_u[half * 4 + b, :, (m // 4) * 128 : (m // 4) * 128 + 128]
                turned = pltpu.roll(word, (b * 32 - (m % 4) * 32) % 128, 1)
                out = jnp.where(lane // 32 == b, turned, out)
            wup[:, m * 256 + half * 128 : m * 256 + half * 128 + 128] = out
    total = small[0]
    for b in range(1, 8):
        total = total + small[b]
    spot = at.zl * 64 + at.xc * 8
    eight = pltpu.roll(total, (128 - spot) % 128, 1)
    for k, ref in enumerate((ob, db, g1, s1, g2, s2)):
        ref[...] = eight[k : k + 1, 0:8]
    own = pltpu.roll(small[at.xc], (128 - ((at.i * 2 + at.zl) % 4) * 32) % 128, 1)
    ub[...] = own[6:7, 0:32]
    bias = pltpu.roll(total, (128 - at.xc * 16) % 128, 1)
    qv[...] = bias[7:8, 0:16]


def on_device(
    tokens, w_qkv, qv_bias, w_out, out_bias, w_up, up_bias, w_down, down_bias,
    gain_one, shift_one, gain_two, shift_two, cotangent,
):
    i, j = lax.axis_index("dp"), lax.axis_index("seq")
    zl, xc = j // 8, j % 8
    c = j % 2
    x, cot = tokens[0], cotangent[0]
    wq = jnp.concatenate(
        [lax.dynamic_slice_in_dim(w_qkv, n * D + xc * 128, 128, axis=1) for n in range(3)], axis=1
    )
    at_row = lax.broadcasted_iota(jnp.int32, (1024, 128), 0)
    at_col = lax.broadcasted_iota(jnp.int32, (1024, 128), 1)
    pick = (
        at_row == (at_col // 64) * 512 + ((at_col // 32) % 2) * 256 + xc * 32 + at_col % 32
    ).astype(BF)
    wu = jnp.concatenate(
        [
            jnp.dot(w_up[:, n * 1024 : (n + 1) * 1024], pick, preferred_element_type=F32).astype(BF)
            for n in range(4)
        ],
        axis=1,
    )
    wd = lax.dynamic_index_in_dim(w_down.reshape(2, 8, 32, D), xc, axis=1, keepdims=False)
    wd = wd.reshape(64, D)
    wo = lax.dynamic_slice_in_dim(w_out, c * 64, 64, axis=0)
    vec = jnp.concatenate(
        [
            out_bias, down_bias, gain_one, shift_one, gain_two, shift_two, up_bias, qv_bias,
            jnp.zeros((512,), BF),
        ]
    ).reshape(16, 128)
    n_lines = 14 + 14 + 21 + 1 + 2 + 7
    (n1, cg, wqg, wug, wdg, wog, vg, q, k, v, kr, vr, att, lse) = call(
        head_kernel, "gather_and_attend", 1, "vavaaav",
        [
            ("v", shape(8, T, D)), ("a", shape(8, T, D)), ("v", shape(8, 128, 384)),
            ("a", shape(8, 128, 512)), ("a", shape(8, 64, D)), ("a", shape(8, 2, 64, D)),
            ("v", shape(8, 16, 128)),
            *[("v", shape(1024, 128))] * 6,
            ("v", shape(1024, 128, of=F32)),
        ],
        [
            VMEM((8, T, D), BF), VMEM((8, D), F32), VMEM((8, 16, 128), F32),
            VMEM((1024, 128), F32), VMEM((1024, 128), F32),
            DMA((n_lines,)), DMA((n_lines,)), DMA((4,)),
        ],
        (x, cot, wq, wu, wd, wo, vec),
    )
    full_out = wog.reshape(D, D)
    flat = vg[:, :6].astype(F32)
    flat = jnp.moveaxis(flat, 1, 0).reshape(6, D)
    rows = jnp.concatenate([flat, flat[:2]])
    ub = lax.dynamic_index_in_dim(vg[:, 6:10].reshape(8, 2, 8, 32), xc, axis=2, keepdims=False)
    ub = ub.reshape(1, 512).astype(F32)
    mid, dmid, dbg, ends, wup_grad, wdown_grad, sums, up_sum = call(
        mlp_kernel, "mlp", 2, "vvvvvaaaa",
        [
            ("v", shape(T, D, of=F32)), ("v", shape(T, D, of=F32)), ("v", shape(D, D)),
            ("v", shape(D, D)), ("v", shape(D, 512)), ("v", shape(512, D)),
            ("v", shape(8, D, of=F32)), ("v", shape(1, 512, of=F32)),
        ],
        [
            VMEM((D, D), BF), VMEM((D, 512), BF), VMEM((512, D), BF), VMEM((D, D), BF),
            VMEM((T, D), BF), VMEM((T, D), BF), VMEM((T, D), BF), VMEM((D, D), BF),
            VMEM((D, 512), BF), VMEM((D, 512), BF), VMEM((D, D), BF),
            *REDUCE_SCRATCH, DMA((4,)), DMA((28,)), DMA((28,)),
        ],
        (att, x, cot, rows, ub, full_out, wug.reshape(D, 512), wdg.reshape(512, D), cg.reshape(D, D)),
    )
    lines = 7 + 7 + 6 * 6 + 1 + 21 + 1
    parts = call(
        pull_kernel, "attention_back", 3, "aaaa" + "v" * 16,
        [
            ("v", shape(T, D)), ("v", shape(T, D)), ("v", shape(8, 8, 384, of=F32)),
            ("v", shape(8, 8, 512, of=F32)), ("v", shape(32, D, of=F32)),
            ("v", shape(8, D, of=F32)), ("v", shape(8, 8, 128, of=F32)),
        ],
        [
            VMEM((D, D), BF), VMEM((D, D), BF), VMEM((D, D), BF), VMEM((D, 384), BF),
            VMEM((1024, 128), BF), VMEM((1024, 128), F32), VMEM((1024, 128), F32),
            VMEM((128, 1024), F32), VMEM((128, 1024), F32),
            VMEM((2, 128, 1024), BF), VMEM((2, 128, 1024), BF),
            VMEM((D, 384), BF), VMEM((D, D), BF),
            *REDUCE_SCRATCH, *REDUCE_SCRATCH,
            VMEM((2, 4, 2, 8, D), F32), VMEM((2, 4, 2, 64, 384), BF), VMEM((2, 4, 2, 8, 128), F32),
            *halving_scratch(True, (64, 512)), *halving_scratch(False, (32, D)),
            *halving_scratch(False, (8, D), F32), *halving_scratch(True, (32, 384)),
            *halving_scratch(False, (32, 384)), *halving_scratch(True, (8, 128), F32),
            VMEM((8, 8, 512), F32), VMEM((8, 8, 384), F32), VMEM((8, D), F32), VMEM((8, 128), F32),
            DMA((4,)), DMA((lines,)), DMA((lines,)),
        ],
        (
            dbg, full_out, n1.reshape(D, D), wqg.reshape(D, 384), att, q, k, v, kr, vr, lse,
            ends, wup_grad.reshape(2, 4, 2, 64, 512), wdown_grad.reshape(2, 4, 2, 32, D),
            x, dmid, mid, rows, sums, up_sum,
        ),
    )
    line = shape(1, 8, of=F32)
    outs = pl.pallas_call(
        lay_kernel,
        name="lay_out",
        in_specs=[vm_spec()] * 7,
        out_specs=[vm_spec()] * 14,
        out_shape=[
            shape(T, D), shape(T, D), shape(8, 3 * D, of=F32), shape(1, 16, of=F32),
            shape(8, D, of=F32), line, shape(8, 4 * D, of=F32), shape(1, 32, of=F32),
            shape(32, D, of=F32), line, line, line, line, line,
        ],
    )(*parts)
    outs = list(outs)
    for n in (0, 1):
        outs[n] = outs[n][None]
    for n in (3, 5, 7, 9, 10, 11, 12, 13):
        outs[n] = outs[n].reshape(-1)
    return tuple(outs)


def solution(mesh):
    return jax.shard_map(
        on_device,
        mesh=mesh,
        in_specs=(
            P("dp", "seq", None), P("dp", None), P("dp"), P("dp", None), P("dp"), P("dp", None),
            P("dp"), P("dp", None), P("dp"), P("dp"), P("dp"), P("dp"), P("dp"),
            P("dp", "seq", None),
        ),
        out_specs=(
            P("dp", "seq", None), P("dp", "seq", None), P(("dp", "seq"), None), P(("dp", "seq")),
            P(("dp", "seq"), None), P(("dp", "seq")), P(("dp", "seq"), None), P(("dp", "seq")),
            P(("dp", "seq"), None), P(("dp", "seq")), P(("dp", "seq")), P(("dp", "seq")),
            P(("dp", "seq")), P(("dp", "seq")),
        ),
        check_vma=False,
    )
```

time: 263 us -> 213 us (0.81)
  matrix products: 32.2 us -> 2.04 us
  Pallas kernels: 202 us -> 191 us
  other arithmetic: 5.34 us -> 0.09 us
    dot_general x8 -> x0, matrix products: 30 us -> none  [the longest x6 23 us: dot(): lax.dot_general(a, b, (((ca,), (cb,)), ((), ())), preferred_element_type=...]
    pallas_call x5 -> x3, Pallas kernels: 202 us -> 188 us  [call(): pl.pallas_call(kernel, name=name, in_specs=[any_spec() if s == 'a' else v...]
    unnamed x74 -> x46, local copies, waits for them, and re-layouts: 7.5 us -> 17.2 us
    dot_general x1 -> x0, local copies, waits for them, and re-layouts: 4.01 us -> none  [dot(): lax.dot_general(a, b, (((ca,), (cb,)), ((), ())), preferred_element_type=...]
    concatenate x3 -> x1, other arithmetic: 2.93 us -> 0.01 us  [on_device(): rows = jnp.concatenate([flat, flat[:2]])]
where the time goes in v2:
time: 213 us; the launch traced here: 212 us
  Pallas kernels  191 us (90%)
  local copies, waits for them, and re-layouts  18.5 us (9%)
    pallas_call x3, Pallas kernels, call(): pl.pallas_call(kernel, name=name, in_specs=[any_spec() if s == 'a' else v...  188 us
    unnamed x46, local copies, waits for them, and re-layouts  17.2 us

profile of v2, /device:TPU:1, one launch (start us, length us, event | category | flops | bytes accessed | tf_op | source)
XLA Modules:
  0.0 212.4 jit_solution(4723963202688091028)
XLA Ops:
  0.6 0.0 copy-start
  0.7 0.0 copy-start.18
  0.7 1.2 copy-done
  1.9 0.9 dynamic-update-slice
  2.8 0.8 dynamic-update-slice.1
  3.6 0.8 dynamic-update-slice.2
  4.5 0.8 dynamic-update-slice.3
  5.3 0.8 dynamic-update-slice.4
  6.1 0.8 dynamic-update-slice.5
  7.0 0.9 dynamic-update-slice.6
  7.8 0.8 dynamic-update-slice.7
  8.6 0.2 dynamic-update-slice.8
  8.9 1.2 fusion.1
  10.1 0.0 copy-done.18
  10.1 0.3 fusion.2
  10.4 0.3 fusion.3
  10.7 0.0 copy-start.17
  10.7 0.3 fusion
  10.9 0.0 copy-start.1
  11.0 0.0 copy-start.4
  11.0 0.9 constant_dynamic-slice_fusion.5
  11.9 0.0 copy-done.17
  11.9 67.7 %gather_and_attend.1 = (bf16[8,128,1024]{2,1,0:T(8,128)(2,1)}, bf16[8,128,1024]{2,1,0:T(8,128)(2,1)}, bf16[8,128,384]{2,1,0:T(8,128)(2,1)}, bf16[8,128,512]{2,1,...) custom-call(bf16[128,1024]{1,0:T(8,128)(2,1)} %bitcast.43, ...), custom_call_target="tpu_custom_call" | custom-call | tf_op jit(solution)/shard_map/gather_and_attend/pallas_call | solution.py:327
  79.6 0.0 copy-start.7
  79.7 0.7 copy-done.7
  80.3 0.0 copy-start.8
  80.3 0.7 copy-done.8
  81.0 0.0 copy-start.9
  81.1 0.7 copy-done.9
  81.8 0.1 reshape.113
  81.9 0.1 reshape.130.ub
  82.0 0.0 copy-done.1
  82.0 0.0 copy-done.4
  82.0 0.0 copy-start.2
  82.0 0.9 copy-done.2
  83.0 0.0 copy-start.3
  83.0 59.3 %mlp.1 = (f32[128,1024]{1,0:T(8,128)S(1)}, f32[128,1024]{1,0:T(8,128)S(1)}, bf16[1024,1024]{1,0:T(8,128)(2,1)}, bf16[1024,1024]{1,0:T(8,128)(2,1)}, bf16[1024,51...) custom-call(bf16[1024,128]{1,0:T(8,128)(2,1)S(1)} %copy-done.2, ...), custom_call_target="tpu_custom_call" | custom-call | tf_op jit(solution)/shard_map/mlp/pallas_call | solution.py:327
  142.3 0.0 copy-start.5
  142.3 0.8 copy-done.5
  143.1 0.0 copy-start.6
  143.1 0.9 copy-done.6
  143.9 0.0 copy-done.3
  143.9 61.5 %attention_back.1 = (bf16[128,1024]{1,0:T(8,128)(2,1)S(1)}, bf16[128,1024]{1,0:T(8,128)(2,1)S(1)}, f32[8,8,384]{2,1,0:T(8,128)S(1)}, f32[8,8,512]{2,1,0:T(8,128)...) custom-call(bf16[1024,1024]{1,0:T(8,128)(2,1)} %get-tuple-element.63.db_at, ...), custom_call_target="tpu_custom_call" | custom-call | tf_op jit(solution)/shard_map/attention_back/pallas_call | solution.py:327
  205.4 0.0 copy-start.10
  205.4 0.7 copy-done.10
  206.2 0.0 copy-start.11
  206.2 0.7 copy-done.11
  206.8 0.0 copy-start.12
  206.8 0.7 copy-done.12
  207.5 0.0 copy-start.13
  207.5 0.6 copy-done.13
  208.2 0.0 copy-start.14
  208.2 0.6 copy-done.14
  208.8 0.0 copy-start.15
  208.8 0.6 copy-done.15
  209.4 0.0 copy-start.16
  209.4 0.6 copy-done.16
  210.0 2.2 %lay_out.1 = (bf16[128,1024]{1,0:T(8,128)(2,1)}, bf16[128,1024]{1,0:T(8,128)(2,1)}, f32[8,3072]{1,0:T(8,128)}, f32[1,16]{1,0:T(1,128)}, f32[8,1024]{1,0:T(8,128)...) custom-call(bf16[128,1024]{1,0:T(8,128)(2,1)} %copy-done.10, ...), custom_call_target="tpu_custom_call" | custom-call | tf_op jit(solution)/shard_map/lay_out/pallas_call | solution.py:814
  (17 shorter events, 0.2 us)
Async XLA Ops:
  0.6 1.2 copy-start
  0.7 9.4 %copy-start.18 = (bf16[128,4096]{1,0:T(8,128)(2,1)S(1)}, bf16[128,4096]{1,0:T(8,128)(2,1)}, u32[]{:S(2)}) copy-start(bf16[128,4096]{1,0:T(8,128)(2,1)} %param.19) | copy-start | bytes 3145732
  10.7 1.2 copy-start.17
  10.9 71.1 %copy-start.1 = (bf16[1,128,1024]{2,1,0:T(8,128)(2,1)S(1)}, bf16[1,128,1024]{2,1,0:T(8,128)(2,1)}, u32[]{:S(2)}) copy-start(bf16[1,128,1024]{2,1,0:T(8,128)(2,1)} %param.14) | copy-start | bytes 786436
  11.0 71.1 %copy-start.4 = (bf16[1,128,1024]{2,1,0:T(8,128)(2,1)S(1)}, bf16[1,128,1024]{2,1,0:T(8,128)(2,1)}, u32[]{:S(2)}) copy-start(bf16[1,128,1024]{2,1,0:T(8,128)(2,1)} %param.27) | copy-start | bytes 786436
  79.6 0.7 copy-start.7
  80.3 0.7 copy-start.8
  81.0 0.7 copy-start.9
  82.0 1.0 copy-start.2
  83.0 61.0 %copy-start.3 = (bf16[1024,128]{1,0:T(8,128)(2,1)S(1)}, bf16[1024,128]{1,0:T(8,128)(2,1)}, u32[]{:S(2)}) copy-start(bf16[1024,128]{1,0:T(8,128)(2,1)} %get-tuple-element.57.att) | copy-start | bytes 786436
  142.3 0.8 copy-start.5
  143.1 0.9 copy-start.6
  205.4 0.7 copy-start.10
  206.2 0.7 copy-start.11
  206.8 0.7 copy-start.12
  207.5 0.6 copy-start.13
  208.2 0.6 copy-start.14
  208.8 0.6 copy-start.15
  209.4 0.6 copy-start.16

commit v3 on v2

v3 whole, which is shorter than its diff:
```python
import functools

import jax
import jax.numpy as jnp
from jax import lax
from jax.experimental import pallas as pl
from jax.experimental.pallas import tpu as pltpu
from jax.sharding import PartitionSpec as P

MESH = pl.DeviceIdType.MESH
EPS = 1e-06
BF = jnp.bfloat16
F32 = jnp.float32
D = 1024
T = 128
VMEM = pltpu.VMEM
ANY = pl.ANY
DMA = pltpu.SemaphoreType.DMA


class Place:
    def __init__(self):
        self.i, self.j = lax.axis_index("dp"), lax.axis_index("seq")
        self.zh, self.y = self.i // 4, self.i % 4
        self.zl, self.xc = self.j // 8, self.j % 8
        self.x, self.c = self.xc // 2, self.xc % 2
        self.z = self.zh * 2 + self.zl

    def in_group(self, dx, dc):
        return (self.i, self.zl * 8 + ((self.x + dx) % 4) * 2 + (self.c + dc) % 2)

    def sibling(self):
        return self.in_group(0, 1)

    def across(self):
        return (self.i, (1 - self.zl) * 8 + self.xc)

    def along_y(self, dy):
        return (self.zh * 4 + (self.y + dy) % 4, self.j)

    def along_z(self, dz):
        z = (self.z + dz) % 4
        return ((z // 2) * 4 + self.y, (z % 2) * 8 + self.xc)

    def mirror(self):
        return ((1 - self.zh) * 4 + self.y, (1 - self.zl) * 8 + self.xc)


GROUP = [(dx, dc) for dx in range(4) for dc in range(2) if (dx, dc) != (0, 0)]
STEPS = (1, 2, 3)


def greet(devices, more=0):
    barrier = pltpu.get_barrier_semaphore()
    for device in devices:
        pl.semaphore_signal(barrier, inc=1, device_id=device, device_id_type=MESH)
    pl.semaphore_wait(barrier, len(devices) + more)


class Lines:
    def __init__(self, send, recv):
        self.send, self.recv, self.used = send, recv, 0

    def copy(self, src, dst, device):
        k = self.used
        self.used += 1
        return pltpu.make_async_remote_copy(
            src_ref=src,
            dst_ref=dst,
            send_sem=self.send.at[k],
            recv_sem=self.recv.at[k],
            device_id=device,
            device_id_type=MESH,
        )


def slot_of(ref, k, size=T):
    return ref.at[pl.ds(pl.multiple_of(k * size, size), size)]


class Gather:
    def __init__(self, at, lines, own, slot):
        self.at, self.lines, self.slot = at, lines, slot
        self.ring, self.forwards = {}, {}
        for dx in (1, 3, 2):
            self.ring[dx] = lines.copy(own, slot(at.xc), at.in_group(dx, 0))
            self.ring[dx].start()
        self.beside = lines.copy(own, slot(at.xc), at.sibling())
        self.beside.start()

    def forward(self, dx):
        at = self.at
        self.ring[dx].wait_recv()
        here = self.slot(((at.x + 4 - dx) % 4) * 2 + at.c)
        self.forwards[dx] = self.lines.copy(here, here, at.sibling())
        self.forwards[dx].start()

    def arrived(self, dx):
        (self.forwards[dx] if dx else self.beside).wait_recv()

    def sent(self):
        self.beside.wait_send()
        for dx in (1, 3, 2):
            self.forwards[dx].wait_send()
            self.ring[dx].wait_send()

    def finish(self):
        for dx in (1, 3, 2):
            self.forward(dx)
        for dx in (0, 1, 3, 2):
            self.arrived(dx)
        self.sent()


class Reduce:
    def __init__(self, at, lines, slot, from_core, sums, from_ring):
        self.at, self.lines, self.slot = at, lines, slot
        self.from_core, self.sums, self.from_ring = from_core, sums, from_ring
        self.cores, self.ring = {}, {}

    def core(self, dx):
        at = self.at
        theirs = self.slot(((at.x + dx) % 4) * 2 + 1 - at.c)
        self.cores[dx] = self.lines.copy(theirs, self.from_core.at[dx], at.sibling())
        self.cores[dx].start()

    def pass_on(self, dx):
        at = self.at
        self.cores[dx].wait_recv()
        mine = self.slot(((at.x + dx) % 4) * 2 + at.c)
        self.sums[dx] = (mine[...].astype(F32) + self.from_core[dx].astype(F32)).astype(BF)
        copy = self.lines.copy(self.sums.at[dx], self.from_ring.at[dx], at.in_group(dx, 0))
        copy.start()
        self.ring[dx] = copy

    def total(self):
        self.cores[0].wait_recv()
        total = self.slot(self.at.xc)[...].astype(F32) + self.from_core[0].astype(F32)
        for dx, copy in self.ring.items():
            copy.wait_recv()
            total = total + self.from_ring[dx].astype(F32)
        return total

    def sent(self):
        for copy in [*self.cores.values(), *self.ring.values()]:
            copy.wait_send()


REDUCE_SCRATCH = [VMEM((4, T, D), BF), VMEM((4, T, D), BF), VMEM((4, T, D), BF)]


def normed(values):
    center = values - jnp.mean(values, axis=-1, keepdims=True)
    rstd = lax.rsqrt(jnp.mean(center * center, axis=-1, keepdims=True) + EPS)
    return center * rstd, rstd


def lanes_of(head, value):
    lane = lax.broadcasted_iota(jnp.int32, (1, 128), 1)
    mine = (lane < 64) if head == 0 else (lane >= 64)
    return jnp.where(mine, value, 0.0).astype(F32)


def by_head(zero, one):
    lane = lax.broadcasted_iota(jnp.int32, (1, 128), 1)
    return jnp.where(lane < 64, zero, one)


def dot(a, b, ca, cb):
    return lax.dot_general(a, b, (((ca,), (cb,)), ((), ())), preferred_element_type=F32)


def norm_back(pulled, hat, rstd, gain):
    scaled = pulled * gain
    inner = jnp.mean(scaled * hat, axis=-1, keepdims=True)
    return rstd * (scaled - jnp.mean(scaled, axis=-1, keepdims=True) - hat * inner)


class Halving:
    def __init__(self, at, lines, whole, first, sums, second, y_first, cut=None):
        self.at, self.lines, self.whole, self.y_first = at, lines, whole, y_first
        self.first, self.sums, self.second = first, sums, second
        self.cut = () if cut is None else (slice(None),) * 2 + (cut,)
        self.one, self.two = [], []

    def block(self, y, z):
        return self.whole[(z // 2, y, z % 2) + self.cut[2:]]

    def start(self):
        at = self.at
        for d in (2, 1, 3):
            if self.y_first:
                to, device = (slice(None), (at.y + d) % 4, slice(None)), at.along_y(d)
            else:
                z = (at.z + d) % 4
                to, device = (z // 2, slice(None), z % 2), at.along_z(d)
            copy = self.lines.copy(self.whole.at[to + self.cut[2:]], self.first.at[d - 1], device)
            copy.start()
            self.one.append(copy)

    def turn(self):
        at = self.at
        for copy in self.one:
            copy.wait_recv()
        for n in range(4):
            acc = self.block(at.y, n) if self.y_first else self.block(n, at.z)
            acc = acc.astype(F32)
            for d in range(3):
                got = self.first[d, n // 2, n % 2] if self.y_first else self.first[d, n]
                acc = acc + got.astype(F32)
            self.sums[n] = acc.astype(self.sums.dtype)
        for d in (2, 1, 3):
            if self.y_first:
                to, device = (at.z + d) % 4, at.along_z(d)
            else:
                to, device = (at.y + d) % 4, at.along_y(d)
            copy = self.lines.copy(self.sums.at[to], self.second.at[d - 1], device)
            copy.start()
            self.two.append(copy)

    def total(self):
        for copy in self.two:
            copy.wait_recv()
        acc = self.sums[self.at.z if self.y_first else self.at.y].astype(F32)
        for d in range(3):
            acc = acc + self.second[d].astype(F32)
        return acc

    def sent(self):
        for copy in self.one + self.two:
            copy.wait_send()


def halving_scratch(y_first, dims, of=BF):
    lead = (3, 2, 2) if y_first else (3, 4)
    return [VMEM(lead + dims, of), VMEM((4,) + dims, of), VMEM((3,) + dims, of)]


class Spread:
    def __init__(self, at, lines, slot, z_first):
        self.at, self.lines, self.slot, self.z_first = at, lines, slot, z_first
        self.y, self.again = {}, {}

    def start(self, own=None):
        at = self.at
        own = self.slot(at.i) if own is None else own
        self.z = self.lines.copy(own, self.slot(at.i), at.mirror())
        self.z.start()
        for d in STEPS:
            self.y[d] = self.lines.copy(own, self.slot(at.i), at.along_y(d))
            self.y[d].start()

    def forward(self):
        at = self.at
        if self.z_first:
            self.z.wait_recv()
            block = self.slot((1 - at.zh) * 4 + at.y)
            for d in STEPS:
                self.again[d] = self.lines.copy(block, block, at.along_y(d))
                self.again[d].start()
        else:
            for d in STEPS:
                self.y[d].wait_recv()
                block = self.slot(at.zh * 4 + (at.y + 4 - d) % 4)
                self.again[d] = self.lines.copy(block, block, at.mirror())
                self.again[d].start()

    def arrived(self):
        for copy in self.y.values() if self.z_first else [self.z]:
            copy.wait_recv()
        for copy in self.again.values():
            copy.wait_recv()

    def sent(self):
        for copy in [self.z, *self.y.values(), *self.again.values()]:
            copy.wait_send()


def any_spec():
    return pl.BlockSpec(memory_space=ANY)


def vm_spec():
    return pl.BlockSpec(memory_space=VMEM)


def shape(*dims, of=BF):
    return jax.ShapeDtypeStruct(dims, of)


def layer_kernel(
    x, cot, vec, w_qkv, w_out, w_up, w_down,
    xgrad, result, wide_q, wide_u, wdown_out, wout_out, small,
    vg, wkv, wq, wu, wd, wo_mine, wout, w_up_here, rows, ub,
    xg, n1, cg, q, k, v, kr, vr, att, lse, top, total, mixed, mid, own, n2g, act, dpre, dmid, low, db,
    parts_a, core_a, part_a, ring_a, ends, core_b, part_b, ring_b, parts_c, core_c, part_c, ring_c,
    do, delta, dq, dk, dv, away, back, dqkv, sums, up_sum,
    wup_grad, wdown_grad, wout_grad, wqkv_grad, points,
    u1, u2, u3, d1, d2, d3, o1, o2, o3, p1, p2, p3, g1, g2, g3, v1, v2, v3,
    low_u, low_q, turn, point, local, send, recv,
):
    at = Place()
    mine = pl.ds(pl.multiple_of(at.xc * 128, 128), 128)
    loads = []

    def load(src, dst):
        loads.append(pltpu.make_async_copy(src, dst, local.at[len(loads)]))
        loads[-1].start()
        return loads[-1]

    def columns(n):
        return w_qkv.at[:, pl.ds(pl.multiple_of(n * D + at.xc * 128, 128), 128)]

    got_kv = [load(columns(n + 1), wkv.at[at.i, :, n * 128 : n * 128 + 128]) for n in range(2)]
    got_q = load(columns(0), wq.at[at.i])
    got_up = load(w_up, w_up_here)
    got_wo = load(
        w_out.at[pl.ds(pl.multiple_of(at.xc * 16, 16), 16)], wo_mine.at[at.i]
    )
    got_wd = load(w_down.at[:, at.xc], wd.at[at.i])
    swapped = (at.xc, at.zl * 8 + at.i)
    barrier = pltpu.get_barrier_semaphore()

    @pl.when(at.i != at.xc)
    def _():
        pl.semaphore_signal(barrier, inc=1, device_id=swapped, device_id_type=MESH)

    greet(
        [at.in_group(*d) for d in GROUP]
        + [at.along_y(d) for d in STEPS]
        + [at.along_z(d) for d in STEPS],
        jnp.where(at.i != at.xc, 1, 0),
    )
    lines = Lines(send, recv)
    vec_in = Spread(at, lines, lambda i: vg.at[i], True)
    kv_in = Spread(at, lines, lambda i: wkv.at[i], True)
    q_in = Spread(at, lines, lambda i: wq.at[i], True)
    wo_in = Spread(at, lines, lambda i: wo_mine.at[i], True)
    wd_in = Spread(at, lines, lambda i: wd.at[i], True)
    wu_in = Spread(at, lines, lambda i: wu.at[i], False)

    x_in = Gather(at, lines, x, lambda n: slot_of(xg, n))
    vec_in.start(vec)
    for copy in got_kv:
        copy.wait()
    kv_in.start()
    got_q.wait()
    q_in.start()
    vg[at.i] = vec[...]
    slot_of(xg, at.xc)[...] = x[...]
    slot_of(cg, at.xc)[...] = cot[...]
    vec_in.forward()
    kv_in.forward()
    got_up.wait()
    at_row = lax.broadcasted_iota(jnp.int32, (1024, 128), 0)
    at_col = lax.broadcasted_iota(jnp.int32, (1024, 128), 1)
    spot = (at_col // 64) * 512 + ((at_col // 32) % 2) * 256 + at.xc * 32 + at_col % 32
    pick = jnp.where(at_row == spot, 1.0, 0.0).astype(BF)
    for n in range(4):
        wu[at.i, :, n * 128 : n * 128 + 128] = dot(
            w_up_here[:, n * 1024 : (n + 1) * 1024], pick, 1, 0
        ).astype(BF)
    q_in.forward()
    for copy in (got_wo, got_wd):
        copy.wait()
    wo_in.start()
    wu_in.start()
    wd_in.start()
    vec_in.arrived()
    for d in range(8):
        rows[0:6, d * 128 : d * 128 + 128] = vg[d, 0:6, :]
    kv_in.arrived()
    at_k = pl.ds(10 + at.xc % 2, 1)
    q_bias = vg[at.xc // 2, at_k, :]
    v_bias = vg[4 + at.xc // 2, at_k, :]
    swaps = []

    def kv_pair(dx):
        here = pl.ds(pl.multiple_of(((at.x + 4 - dx) % 4) * 256, 256), 256)
        hat, _ = normed(xg[here, :].astype(F32))
        hat = (hat * rows[2:3, :] + rows[3:4, :]).astype(BF)
        n1[here, :] = hat
        made = dot(hat, wkv[...].reshape(D, 256), 1, 0)
        k[here, :] = made[:, 0:128].astype(BF)
        v[here, :] = (made[:, 128:256] + v_bias).astype(BF)
        for src, dst in ((k, kr), (v, vr)):
            copy = lines.copy(src.at[here], dst.at[here], at.across())
            copy.start()
            swaps.append(copy)

    x_in.forward(1)
    x_in.forward(3)
    x_in.arrived(0)
    kv_pair(0)
    x_in.forward(2)
    x_in.arrived(1)
    kv_pair(1)
    x_in.arrived(3)
    kv_pair(3)
    x_in.arrived(2)
    kv_pair(2)
    cot_in = Gather(at, lines, cot, lambda n: slot_of(cg, n))
    wo_in.forward()
    wd_in.forward()
    q_in.arrived()
    for b in range(4):
        here = slice(b * 256, b * 256 + 256)
        q[here, :] = (dot(n1[here, :], wq[...].reshape(D, 128), 1, 0) + q_bias).astype(BF)

    def attend(part, keys, values, fresh):
        block = q[part, :]
        tops, masses, outs, fades = [], [], [], []
        for h in range(2):
            score = dot(block * lanes_of(h, 0.125).astype(BF), keys[...], 1, 1)
            peak = jnp.max(score, axis=-1, keepdims=True)
            if not fresh:
                old = top[part, 64 * h : 64 * h + 1]
                peak = jnp.maximum(old, peak)
                fades.append(jnp.exp(old - peak))
            expo = jnp.exp(score - peak)
            tops.append(peak)
            masses.append(jnp.sum(expo, axis=-1, keepdims=True))
            outs.append(dot(expo.astype(BF), values[...], 1, 0))
        peak, added, out = by_head(*tops), by_head(*masses), by_head(*outs)
        if fresh:
            top[part, :] = peak
            lse[part, :] = added
            total[part, :] = out
        else:
            fade = by_head(*fades)
            mass = lse[part, :] * fade + added
            att[part, :] = ((total[part, :] * fade + out) / mass).astype(BF)
            lse[part, :] = peak + jnp.log(mass)

    def near_step(t, _):
        attend(pl.ds(pl.multiple_of(t * 512, 512), 512), k, v, True)
        return 0

    lax.fori_loop(0, 2, near_step, 0)
    wu_in.forward()
    wo_in.arrived()
    wo_own = wo_mine
    out_in = Gather(at, lines, wo_own, lambda n: wout.at[:, n])
    wout[:, at.xc] = wo_mine[...]
    cot_in.forward(1)
    cot_in.forward(3)
    for copy in swaps:
        copy.wait_recv()
    given = []
    for dx in (2, 1, 3, 0):
        attend(pl.ds(pl.multiple_of(((at.x + dx) % 4) * 256, 256), 256), kr, vr, False)
        for dc in range(2):
            if (dx, dc) != (0, 0):
                to = ((at.x + dx) % 4) * 2 + (at.c + dc) % 2
                copy = lines.copy(slot_of(att, to), mixed.at[:, mine], at.in_group(dx, dc))
                copy.start()
                given.append(copy)
    mixed[:, mine] = slot_of(att, at.xc)[...]
    cot_in.forward(2)
    for dx in (1, 3, 2):
        out_in.forward(dx)
    lane = lax.broadcasted_iota(jnp.int32, (1, 128), 1)
    for m in range(4):
        word = jnp.zeros((1, 128), F32)
        for b in range(4):
            row = vg[m * 2 + b // 2, pl.ds(6 + (b % 2) * 2 + at.xc // 4, 1), :]
            row = pltpu.roll(row, (b * 32 + 128 - (at.xc % 4) * 32) % 128, 1)
            word = jnp.where(lane // 32 == b, row, word)
        ub[:, m * 128 : m * 128 + 128] = word
    for dx in (0, 1, 3, 2):
        out_in.arrived(dx)
    for copy in given:
        copy.wait_recv()

    middle = x[...].astype(F32) + rows[0:1, :]
    middle = middle + dot(mixed[...], wout[...].reshape(D, D), 1, 0)
    mid[...] = middle
    hat, rstd = normed(middle)
    own[...] = (hat * rows[4:5, :] + rows[5:6, :]).astype(BF)
    tokens_in = Gather(at, lines, own, lambda n: slot_of(n2g, n))
    slot_of(n2g, at.xc)[...] = own[...]
    up_sum[...] = jnp.zeros_like(up_sum)
    out = Reduce(at, lines, lambda n: slot_of(parts_a, n), core_a, part_a, ring_a)
    wd_in.arrived()
    wu_in.arrived()
    for dx in (0, 1, 3, 2):
        cot_in.arrived(dx)

    def pair(dx):
        here = pl.ds(pl.multiple_of(((at.x + 4 - dx) % 4) * 256, 256), 256)
        ups = wu[...].reshape(D, 512)
        pre = dot(n2g[here, :], ups, 1, 0) + ub[...]
        grad = dot(cg[here, :], wd[...].reshape(512, D), 1, 1)
        cdf = 0.5 * (1.0 + lax.erf(pre * (0.5**0.5)))
        act[here, :] = (pre * cdf).astype(BF)
        slope = cdf + pre * (jnp.exp(-0.5 * pre * pre) * 0.3989422804014327)
        pulled = (grad * slope).astype(BF)
        dpre[here, :] = pulled
        up_sum[...] += jnp.sum(pulled.astype(F32), axis=0, keepdims=True)
        parts_a[here, :] = dot(pulled, ups, 1, 1).astype(BF)
        out.core((4 - dx) % 4)

    tokens_in.arrived(0)
    pair(0)
    tokens_in.forward(1)
    tokens_in.forward(3)
    tokens_in.arrived(1)
    pair(1)
    tokens_in.forward(2)
    tokens_in.arrived(3)
    pair(3)
    out.pass_on(3)
    tokens_in.arrived(2)
    pair(2)
    out.pass_on(1)
    out.pass_on(2)

    def end_step(b, _):
        here = pl.ds(pl.multiple_of(b * 256, 256), 256)
        ends[here, :] = dot(act[here, :], wd[...].reshape(512, D), 1, 0).astype(BF)
        return 0

    lax.fori_loop(0, 4, end_step, 0)
    made = dot(act[...], cg[...], 0, 0).astype(BF)
    for n in range(16):
        wdown_grad[n // 8, (n // 2) % 4, n % 2] = made[n * 32 : n * 32 + 32, :]
    downs = Halving(at, lines, wdown_grad, d1, d2, d3, False)
    downs.start()
    pulled = out.total()
    sums[4:5, :] = jnp.sum(pulled * hat, axis=0, keepdims=True)
    sums[5:6, :] = jnp.sum(pulled, axis=0, keepdims=True)
    middle = cot[...].astype(F32) + norm_back(pulled, hat, rstd, rows[4:5, :])
    dmid[...] = middle
    low[...] = middle.astype(BF)
    back_in = Gather(at, lines, low, lambda n: slot_of(db, n))
    slot_of(db, at.xc)[...] = low[...]
    sums[0:1, :] = jnp.sum(low[...].astype(F32), axis=0, keepdims=True)
    sums[1:2, :] = jnp.sum(cot[...].astype(F32), axis=0, keepdims=True)
    made = dot(n2g[...], dpre[...], 0, 0).astype(BF)
    for n in range(16):
        wup_grad[n // 8, (n // 2) % 4, n % 2] = made[n * 64 : n * 64 + 64, :]
    ups = Halving(at, lines, wup_grad, u1, u2, u3, True)
    ups.start()
    back_in.finish()

    outs = Halving(at, lines, wout_grad, o1, o2, o3, False)
    closing = Reduce(at, lines, lambda n: slot_of(ends, n), core_b, part_b, ring_b)
    for dx in (2, 1, 3, 0):
        closing.core(dx)
    grads = dot(db[...], wout[at.xc].reshape(128, D), 1, 1).astype(BF)
    do[...] = grads
    both = grads.astype(F32) * att[...].astype(F32)
    delta[...] = by_head(
        jnp.sum(both * lanes_of(0, 1.0), axis=-1, keepdims=True),
        jnp.sum(both * lanes_of(1, 1.0), axis=-1, keepdims=True),
    )

    def pull(keys, values, half, fresh):
        there = slice(half * 512, half * 512 + 512)
        dk[:, there] = jnp.zeros((128, 512), F32)
        dv[:, there] = jnp.zeros((128, 512), F32)

        def step(t, _):
            part = pl.ds(pl.multiple_of(t * 512, 512), 512)
            block, grad = q[part, :], do[part, :]
            made = []
            for h in range(2):
                some = block * lanes_of(h, 0.125).astype(BF)
                pulled = grad * lanes_of(h, 1.0).astype(BF)
                prob = jnp.exp(dot(some, keys[there, :], 1, 1) - lse[part, 64 * h : 64 * h + 1])
                dprob = dot(pulled, values[there, :], 1, 1)
                raw = (prob * (dprob - delta[part, 64 * h : 64 * h + 1])).astype(BF)
                dv[:, there] += dot(pulled, prob.astype(BF), 0, 0)
                dk[:, there] += dot(some, raw, 0, 0)
                made.append(dot(raw, keys[there, :], 1, 0))
            out = by_head(*made) * 0.125
            dq[part, :] = out if fresh else dq[part, :] + out
            return 0

        lax.fori_loop(0, 2, step, 0)

    returns = []
    for half in range(2):
        pull(kr, vr, half, half == 0)
        there = slice(half * 512, half * 512 + 512)
        away[half, 0] = dk[:, there].astype(BF)
        away[half, 1] = dv[:, there].astype(BF)
        copy = lines.copy(away.at[half], back.at[half], at.across())
        copy.start()
        returns.append(copy)
        if half == 0:
            for dx in (2, 1, 3):
                closing.pass_on(dx)
            made = dot(att[...], db[...], 0, 0)
            for zl in range(2):
                for i in range(8):
                    b = (zl * 8 + i) * 8
                    wout_grad[i // 4, i % 4, zl] = made[b : b + 8, :]
            outs.start()
    downs.turn()
    pull(k, v, 0, False)
    ups.turn()
    pull(k, v, 1, False)
    outs.turn()
    dqkv[:, 0:128] = dq[...].astype(BF)
    for half in range(2):
        returns[half].wait_recv()
        there = slice(half * 512, half * 512 + 512)
        for n, ref in enumerate((dk, dv)):
            made = jnp.transpose(ref[:, there] + back[half, n].astype(F32))
            dqkv[there, 128 + n * 128 : 256 + n * 128] = made.astype(BF)

    inner = Reduce(at, lines, lambda n: slot_of(parts_c, n), core_c, part_c, ring_c)
    shift_sum = jnp.zeros((1, D), F32)
    both_sum = jnp.zeros((1, D), F32)
    before = None
    for dx in (2, 1, 3, 0):
        here = pl.ds(pl.multiple_of(((at.x + dx) % 4) * 256, 256), 256)
        made = dot(dqkv[here, 0:128], wq[...].reshape(D, 128), 1, 1)
        made = made + dot(dqkv[here, 128:384], wkv[...].reshape(D, 256), 1, 1)
        parts_c[here, :] = made.astype(BF)
        inner.core(dx)
        shift_sum = shift_sum + jnp.sum(made, axis=0, keepdims=True)
        both_sum = both_sum + jnp.sum(made * n1[here, :].astype(F32), axis=0, keepdims=True)
        if before is not None:
            inner.pass_on(before)
        before = dx
    made = dot(n1[...], dqkv[...], 0, 0).astype(BF)
    for n in range(16):
        wqkv_grad[n // 8, (n // 2) % 4, n % 2] = made[n * 64 : n * 64 + 64, :]
    firsts = Halving(at, lines, wqkv_grad, p1, p2, p3, True, slice(0, 32))
    seconds = Halving(at, lines, wqkv_grad, g1, g2, g3, False, slice(32, 64))
    firsts.start()
    seconds.start()
    qkv_sum = jnp.sum(dqkv[...].astype(F32), axis=0, keepdims=True)
    gain_sum = (both_sum - rows[3:4, :] * shift_sum) / rows[2:3, :]
    for n in range(16):
        wide = slice((n // 2) * 128, (n // 2) * 128 + 128)
        to = (n // 8, (n // 2) % 4, n % 2)
        points[to + (slice(0, 2),)] = sums[0:2, wide]
        points[to + (slice(2, 3),)] = gain_sum[:, wide]
        points[to + (slice(3, 4),)] = shift_sum[:, wide]
        points[to + (slice(4, 6),)] = sums[4:6, wide]
        points[to + (slice(6, 7),)] = up_sum[:, (n // 4) * 128 : (n // 4) * 128 + 128]
        some = qkv_sum[:, 0:128] if n < 8 else qkv_sum[:, 256:384]
        points[to + (slice(7, 8),)] = jnp.where(at.xc == n % 8, some, 0.0)
    vectors = Halving(at, lines, points, v1, v2, v3, True)
    vectors.start()
    third = []

    def to_group(src, dst):
        for dx, dc in GROUP:
            to = ((at.x + dx) % 4) * 2 + (at.c + dc) % 2
            copy = lines.copy(src(to), dst, at.in_group(dx, dc))
            copy.start()
            third.append(copy)

    acc = ups.total()
    for b in range(8):
        low_u[b] = acc[b * 8 : (b + 1) * 8, :]
    to_group(lambda n: low_u.at[n], wide_u.at[at.xc])
    wide_u[at.xc] = low_u[at.xc]
    wdown_out[...] = downs.total()
    turn[...] = outs.total()
    across = lines.copy(turn, wout_out, swapped)

    @pl.when(at.i != at.xc)
    def _():
        across.start()

    @pl.when(at.i == at.xc)
    def _():
        wout_out[...] = turn[...]

    result[...] = (mid[...] + closing.total() + rows[1:2, :]).astype(BF)
    vectors.turn()
    firsts.turn()
    seconds.turn()
    pulled = inner.total()
    hat, rstd = normed(x[...].astype(F32))
    xgrad[...] = (dmid[...] + norm_back(pulled, hat, rstd, rows[2:3, :])).astype(BF)
    point[...] = vectors.total()
    to_group(lambda n: point, small.at[at.xc])
    small[at.xc] = point[...]
    for half, acc in enumerate((firsts.total(), seconds.total())):
        for b in range(4):
            low_q[half * 4 + b] = acc[b * 8 : (b + 1) * 8, :]
    to_group(lambda n: low_q.at[n], wide_q.at[at.xc])
    wide_q[at.xc] = low_q[at.xc]

    @pl.when(at.i != at.xc)
    def _():
        across.wait()

    for copy in third:
        copy.wait()
    for copy in swaps + given + returns:
        copy.wait_send()
    for flow in (
        vec_in, kv_in, q_in, wo_in, wd_in, wu_in, x_in, cot_in, out_in, tokens_in,
        ups, downs, outs, firsts, seconds, vectors, out, inner, closing,
    ):
        flow.sent()


def lay_kernel(
    xgrad_at, result_at, wide_q, wide_u, wdown_at, wout_at, small,
    result, xgrad, wqkv, qv, wout, ob, wup, ub, wdown, db, g1, s1, g2, s2,
):
    at = Place()
    xgrad[...] = xgrad_at[...]
    result[...] = result_at[...]
    wdown[...] = wdown_at[...]
    wout[...] = wout_at[...]
    for n in range(3):
        for b in range(8):
            wqkv[:, n * D + b * 128 : n * D + b * 128 + 128] = wide_q[b, :, n * 128 : n * 128 + 128]
    lane = lax.broadcasted_iota(jnp.int32, (8, 128), 1)
    for m in range(16):
        for half in range(2):
            out = jnp.zeros((8, 128), F32)
            for b in range(4):
                word = wide_u[half * 4 + b, :, (m // 4) * 128 : (m // 4) * 128 + 128]
                turned = pltpu.roll(word, (b * 32 - (m % 4) * 32) % 128, 1)
                out = jnp.where(lane // 32 == b, turned, out)
            wup[:, m * 256 + half * 128 : m * 256 + half * 128 + 128] = out
    total = small[0]
    for b in range(1, 8):
        total = total + small[b]
    spot = at.zl * 64 + at.xc * 8
    eight = pltpu.roll(total, (128 - spot) % 128, 1)
    for k, ref in enumerate((ob, db, g1, s1, g2, s2)):
        ref[...] = eight[k : k + 1, 0:8]
    own = pltpu.roll(small[at.xc], (128 - ((at.i * 2 + at.zl) % 4) * 32) % 128, 1)
    ub[...] = own[6:7, 0:32]
    bias = pltpu.roll(total, (128 - at.xc * 16) % 128, 1)
    qv[...] = bias[7:8, 0:16]


def on_device(
    tokens, w_qkv, qv_bias, w_out, out_bias, w_up, up_bias, w_down, down_bias,
    gain_one, shift_one, gain_two, shift_two, cotangent,
):
    vec, row = jnp.zeros((16, 128), F32), 0
    for vector in (
        out_bias, down_bias, gain_one, shift_one, gain_two, shift_two, up_bias, qv_bias
    ):
        lines = vector.astype(F32).reshape(-1, 128)
        vec = vec + jnp.pad(lines, ((row, 16 - row - lines.shape[0]), (0, 0)))
        row += lines.shape[0]
    block, whole, half = VMEM((T, D), BF), VMEM((D, D), BF), VMEM((D, 512), BF)
    narrow, tall = VMEM((D, 128), BF), VMEM((D, 128), F32)
    n_lines = 6 * 7 + 5 * 7 + 8 + 7 + 3 * 7 + 2 + 6 * 6 + 3 * 7 + 1
    parts = pl.pallas_call(
        layer_kernel,
        name="layer",
        in_specs=[vm_spec()] * 3 + [any_spec()] * 4,
        out_specs=[vm_spec()] * 7,
        out_shape=[
            shape(T, D), shape(T, D), shape(8, 8, 384, of=F32), shape(8, 8, 512, of=F32),
            shape(32, D, of=F32), shape(8, D, of=F32), shape(8, 8, 128, of=F32),
        ],
        scratch_shapes=[
            VMEM((8, 16, 128), F32), VMEM((8, 128, 256), BF), VMEM((8, 128, 128), BF),
            VMEM((8, 128, 512), BF), VMEM((8, 2, 32, D), BF), VMEM((8, 16, D), BF),
            VMEM((8, 8, 16, D), BF), VMEM((128, 4 * D), BF), VMEM((8, D), F32), VMEM((1, 512), F32),
            whole, whole, whole, *[narrow] * 6, *[tall] * 3, block, VMEM((T, D), F32), block,
            whole, half, half, VMEM((T, D), F32), block, whole,
            *[whole, *REDUCE_SCRATCH] * 3,
            narrow, tall, tall, VMEM((128, D), F32), VMEM((128, D), F32),
            VMEM((2, 2, 128, 512), BF), VMEM((2, 2, 128, 512), BF), VMEM((D, 384), BF),
            VMEM((8, D), F32), VMEM((1, 512), F32),
            VMEM((2, 4, 2, 64, 512), BF), VMEM((2, 4, 2, 32, D), BF), VMEM((2, 4, 2, 8, D), F32),
            VMEM((2, 4, 2, 64, 384), BF), VMEM((2, 4, 2, 8, 128), F32),
            *halving_scratch(True, (64, 512)), *halving_scratch(False, (32, D)),
            *halving_scratch(False, (8, D), F32), *halving_scratch(True, (32, 384)),
            *halving_scratch(False, (32, 384)), *halving_scratch(True, (8, 128), F32),
            VMEM((8, 8, 512), F32), VMEM((8, 8, 384), F32), VMEM((8, D), F32), VMEM((8, 128), F32),
            DMA((8,)), DMA((n_lines,)), DMA((n_lines,)),
        ],
        compiler_params=pltpu.CompilerParams(
            collective_id=1, has_side_effects=True, vmem_limit_bytes=60 * 2**20
        ),
    )(tokens[0], cotangent[0], vec, w_qkv, w_out, w_up, w_down.reshape(2, 8, 32, D))
    line = shape(1, 8, of=F32)
    outs = pl.pallas_call(
        lay_kernel,
        name="lay_out",
        in_specs=[vm_spec()] * 7,
        out_specs=[vm_spec()] * 14,
        out_shape=[
            shape(T, D), shape(T, D), shape(8, 3 * D, of=F32), shape(1, 16, of=F32),
            shape(8, D, of=F32), line, shape(8, 4 * D, of=F32), shape(1, 32, of=F32),
            shape(32, D, of=F32), line, line, line, line, line,
        ],
    )(*parts)
    outs = list(outs)
    for n in (0, 1):
        outs[n] = outs[n][None]
    for n in (3, 5, 7, 9, 10, 11, 12, 13):
        outs[n] = outs[n].reshape(-1)
    return tuple(outs)


def solution(mesh):
    return jax.shard_map(
        on_device,
        mesh=mesh,
        in_specs=(
            P("dp", "seq", None), P("dp", None), P("dp"), P("dp", None), P("dp"), P("dp", None),
            P("dp"), P("dp", None), P("dp"), P("dp"), P("dp"), P("dp"), P("dp"),
            P("dp", "seq", None),
        ),
        out_specs=(
            P("dp", "seq", None), P("dp", "seq", None), P(("dp", "seq"), None), P(("dp", "seq")),
            P(("dp", "seq"), None), P(("dp", "seq")), P(("dp", "seq"), None), P(("dp", "seq")),
            P(("dp", "seq"), None), P(("dp", "seq")), P(("dp", "seq")), P(("dp", "seq")),
            P(("dp", "seq")), P(("dp", "seq")),
        ),
        check_vma=False,
    )
```

time: 213 us -> 155 us (0.73)
  Pallas kernels: 191 us -> 153 us
  local copies, waits for them, and re-layouts: 18.5 us -> 0.71 us
    pallas_call x3 -> x1, Pallas kernels: 188 us -> 151 us  [on_device(): pl.pallas_call(layer_kernel, name='layer', in_specs=[vm_spec()] * 3 + [an...]
    unnamed x46 -> x16, local copies, waits for them, and re-layouts: 17.2 us -> 0.71 us
where the time goes in v3:
time: 155 us
  Pallas kernels  153 us (99%)
    pallas_call x1, Pallas kernels, on_device(): pl.pallas_call(layer_kernel, name='layer', in_specs=[vm_spec()] * 3 + [an...  151 us

profile of v3, /device:TPU:1, one launch (start us, length us, event | category | flops | bytes accessed | tf_op | source)
XLA Modules:
  0.0 155.3 jit_solution(6092066208651929156)
XLA Ops:
  0.6 0.0 copy-start.6
  0.7 0.0 copy-start.7
  0.7 0.0 copy-start.2
  0.7 0.0 copy-start.3
  0.7 0.0 copy-start.4
  0.7 0.0 copy-start.5
  0.7 0.0 copy-start
  0.7 0.0 copy-start.1
  0.7 0.6 copy-done.6
  1.3 0.0 copy-done.7
  1.3 0.0 copy-done.2
  1.3 0.0 copy-done.3
  1.4 0.0 copy-done.4
  1.4 0.0 copy-done.5
  1.4 0.0 copy-done
  1.4 0.0 copy-done.1
  1.4 0.6 convert_add_fusion.vec
  2.0 150.8 %layer.1 = (bf16[128,1024]{1,0:T(8,128)(2,1)}, bf16[128,1024]{1,0:T(8,128)(2,1)}, f32[8,8,384]{2,1,0:T(8,128)}, f32[8,8,512]{2,1,0:T(8,128)}, f32[32,1024]{1,0:T...) custom-call(bf16[128,1024]{1,0:T(8,128)(2,1)} %bitcast.22, bf16[128,1024]{1,0:T(8,128)(2,1)} %bitcast.23, ...), custom_call_target="tpu_custom_call" | custom-call | tf_op jit(solution)/shard_map/layer/pallas_call | solution.py:754
  152.8 2.3 %lay_out.1 = (bf16[128,1024]{1,0:T(8,128)(2,1)}, bf16[128,1024]{1,0:T(8,128)(2,1)}, f32[8,3072]{1,0:T(8,128)}, f32[1,16]{1,0:T(1,128)}, f32[8,1024]{1,0:T(8,128)...) custom-call(bf16[128,1024]{1,0:T(8,128)(2,1)} %get-tuple-element.35., ...), custom_call_target="tpu_custom_call" | custom-call | tf_op jit(solution)/shard_map/lay_out/pallas_call | solution.py:786
Async XLA Ops:
  0.6 0.7 copy-start.6
  0.7 0.7 copy-start.7
  0.7 0.7 copy-start.2
  0.7 0.7 copy-start.3
  0.7 0.7 copy-start.4
  0.7 0.7 copy-start.5
  0.7 0.7 copy-start
  0.7 0.7 copy-start.1

commit v4 on v3

--- a/solution.py
+++ b/solution.py
@@ -25,6 +25,7 @@
         self.zl, self.xc = self.j // 8, self.j % 8
         self.x, self.c = self.xc // 2, self.xc % 2
         self.z = self.zh * 2 + self.zl
+        self.fc = ((self.x + self.y) % 4) * 2 + self.c
 
     def in_group(self, dx, dc):
         return (self.i, self.zl * 8 + ((self.x + dx) % 4) * 2 + (self.c + dc) % 2)
@@ -37,6 +38,15 @@
 
     def along_y(self, dy):
         return (self.zh * 4 + (self.y + dy) % 4, self.j)
+
+    def on_x(self, dx):
+        return self.in_group(dx, 0)
+
+    def aslant(self, dy):
+        return (
+            self.zh * 4 + (self.y + dy) % 4,
+            self.zl * 8 + ((self.x + 4 - dy) % 4) * 2 + self.c,
+        )
 
     def along_z(self, dz):
         z = (self.z + dz) % 4
@@ -79,20 +89,19 @@
 
 
 class Gather:
-    def __init__(self, at, lines, own, slot):
-        self.at, self.lines, self.slot = at, lines, slot
+    def __init__(self, at, lines, own, put, got, to):
+        self.at, self.lines, self.got = at, lines, got
         self.ring, self.forwards = {}, {}
         for dx in (1, 3, 2):
-            self.ring[dx] = lines.copy(own, slot(at.xc), at.in_group(dx, 0))
+            self.ring[dx] = lines.copy(own, put(dx), to(dx))
             self.ring[dx].start()
-        self.beside = lines.copy(own, slot(at.xc), at.sibling())
+        self.beside = lines.copy(own, put(0), at.sibling())
         self.beside.start()
 
     def forward(self, dx):
-        at = self.at
         self.ring[dx].wait_recv()
-        here = self.slot(((at.x + 4 - dx) % 4) * 2 + at.c)
-        self.forwards[dx] = self.lines.copy(here, here, at.sibling())
+        here = self.got(dx)
+        self.forwards[dx] = self.lines.copy(here, here, self.at.sibling())
         self.forwards[dx].start()
 
     def arrived(self, dx):
@@ -112,30 +121,69 @@
         self.sent()
 
 
+def gather_group(at, lines, own, slot):
+    return Gather(
+        at, lines, own,
+        lambda dx: slot(at.xc),
+        lambda dx: slot(((at.x + 4 - dx) % 4) * 2 + at.c),
+        at.on_x,
+    )
+
+
+def half_of(ref, back, ring, core):
+    start = back * 256 + ring * 128 + core * 64
+    return ref.at[pl.ds(pl.multiple_of(start, 64), 64)]
+
+
+class Halves:
+    def __init__(self, at, lines, own, ref):
+        self.both = [
+            Gather(
+                at, lines, own.at[64 * ring : 64 * ring + 64],
+                lambda d, ring=ring: half_of(ref, d, ring, at.c),
+                lambda d, ring=ring: half_of(ref, d, ring, at.c),
+                (at.on_x, at.along_y)[ring],
+            )
+            for ring in range(2)
+        ]
+        for ring in range(2):
+            half_of(ref, 0, ring, at.c)[...] = own[64 * ring : 64 * ring + 64, :]
+
+    def forward(self, d):
+        for one in self.both:
+            one.forward(d)
+
+    def arrived(self, d):
+        for one in self.both:
+            one.arrived(d)
+
+    def sent(self):
+        for one in self.both:
+            one.sent()
+
+
 class Reduce:
-    def __init__(self, at, lines, slot, from_core, sums, from_ring):
-        self.at, self.lines, self.slot = at, lines, slot
+    def __init__(self, at, lines, slot, to, from_core, sums, from_ring):
+        self.at, self.lines, self.slot, self.to = at, lines, slot, to
         self.from_core, self.sums, self.from_ring = from_core, sums, from_ring
         self.cores, self.ring = {}, {}
 
     def core(self, dx):
-        at = self.at
-        theirs = self.slot(((at.x + dx) % 4) * 2 + 1 - at.c)
-        self.cores[dx] = self.lines.copy(theirs, self.from_core.at[dx], at.sibling())
+        theirs = self.slot(dx, 1 - self.at.c)
+        self.cores[dx] = self.lines.copy(theirs, self.from_core.at[dx], self.at.sibling())
         self.cores[dx].start()
 
     def pass_on(self, dx):
-        at = self.at
         self.cores[dx].wait_recv()
-        mine = self.slot(((at.x + dx) % 4) * 2 + at.c)
+        mine = self.slot(dx, self.at.c)
         self.sums[dx] = (mine[...].astype(F32) + self.from_core[dx].astype(F32)).astype(BF)
-        copy = self.lines.copy(self.sums.at[dx], self.from_ring.at[dx], at.in_group(dx, 0))
+        copy = self.lines.copy(self.sums.at[dx], self.from_ring.at[dx], self.to(dx))
         copy.start()
         self.ring[dx] = copy
 
     def total(self):
         self.cores[0].wait_recv()
-        total = self.slot(self.at.xc)[...].astype(F32) + self.from_core[0].astype(F32)
+        total = self.slot(0, self.at.c)[...].astype(F32) + self.from_core[0].astype(F32)
         for dx, copy in self.ring.items():
             copy.wait_recv()
             total = total + self.from_ring[dx].astype(F32)
@@ -146,6 +194,32 @@
             copy.wait_send()
 
 
+class ReduceHalves:
+    def __init__(self, at, lines, ref, from_core, sums, from_ring):
+        self.both = [
+            Reduce(
+                at, lines,
+                lambda d, core, ring=ring: half_of(ref, (4 - d) % 4, ring, core),
+                (at.on_x, at.along_y)[ring],
+                from_core.at[ring], sums.at[ring], from_ring.at[ring],
+            )
+            for ring in range(2)
+        ]
+
+    def core(self, d):
+        for one in self.both:
+            one.core(d)
+
+    def pass_on(self, d):
+        for one in self.both:
+            one.pass_on(d)
+
+    def sent(self):
+        for one in self.both:
+            one.sent()
+
+
+HALVES_SCRATCH = [VMEM((2, 4, 64, D), BF)] * 3
 REDUCE_SCRATCH = [VMEM((4, T, D), BF), VMEM((4, T, D), BF), VMEM((4, T, D), BF)]
 
 
@@ -177,7 +251,8 @@
 
 
 class Halving:
-    def __init__(self, at, lines, whole, first, sums, second, y_first, cut=None):
+    def __init__(self, at, lines, whole, first, sums, second, y_first, cut=None, along=None):
+        self.along = at.along_y if along is None else along
         self.at, self.lines, self.whole, self.y_first = at, lines, whole, y_first
         self.first, self.sums, self.second = first, sums, second
         self.cut = () if cut is None else (slice(None),) * 2 + (cut,)
@@ -190,7 +265,7 @@
         at = self.at
         for d in (2, 1, 3):
             if self.y_first:
-                to, device = (slice(None), (at.y + d) % 4, slice(None)), at.along_y(d)
+                to, device = (slice(None), (at.y + d) % 4, slice(None)), self.along(d)
             else:
                 z = (at.z + d) % 4
                 to, device = (z // 2, slice(None), z % 2), at.along_z(d)
@@ -213,7 +288,7 @@
             if self.y_first:
                 to, device = (at.z + d) % 4, at.along_z(d)
             else:
-                to, device = (at.y + d) % 4, at.along_y(d)
+                to, device = (at.y + d) % 4, self.along(d)
             copy = self.lines.copy(self.sums.at[to], self.second.at[d - 1], device)
             copy.start()
             self.two.append(copy)
@@ -241,13 +316,14 @@
         self.at, self.lines, self.slot, self.z_first = at, lines, slot, z_first
         self.y, self.again = {}, {}
 
-    def start(self, own=None):
+    def start(self, own=None, others=None):
         at = self.at
         own = self.slot(at.i) if own is None else own
         self.z = self.lines.copy(own, self.slot(at.i), at.mirror())
         self.z.start()
         for d in STEPS:
-            self.y[d] = self.lines.copy(own, self.slot(at.i), at.along_y(d))
+            block = own if others is None else others(d)
+            self.y[d] = self.lines.copy(block, self.slot(at.i), at.along_y(d))
             self.y[d].start()
 
     def forward(self):
@@ -291,13 +367,13 @@
 def layer_kernel(
     x, cot, vec, w_qkv, w_out, w_up, w_down,
     xgrad, result, wide_q, wide_u, wdown_out, wout_out, small,
-    vg, wkv, wq, wu, wd, wo_mine, wout, w_up_here, rows, ub,
+    vg, wkv, wq, wu, wd, wo_mine, wout, w_up_here, picked, rows, ub,
     xg, n1, cg, q, k, v, kr, vr, att, lse, top, total, mixed, mid, own, n2g, act, dpre, dmid, low, db,
     parts_a, core_a, part_a, ring_a, ends, core_b, part_b, ring_b, parts_c, core_c, part_c, ring_c,
     do, delta, dq, dk, dv, away, back, dqkv, sums, up_sum,
     wup_grad, wdown_grad, wout_grad, wqkv_grad, points,
     u1, u2, u3, d1, d2, d3, o1, o2, o3, p1, p2, p3, g1, g2, g3, v1, v2, v3,
-    low_u, low_q, turn, point, local, send, recv,
+    low_u, low_q, turn, down_turn, point, local, send, recv,
 ):
     at = Place()
     mine = pl.ds(pl.multiple_of(at.xc * 128, 128), 128)
@@ -317,7 +393,7 @@
     got_wo = load(
         w_out.at[pl.ds(pl.multiple_of(at.xc * 16, 16), 16)], wo_mine.at[at.i]
     )
-    got_wd = load(w_down.at[:, at.xc], wd.at[at.i])
+    got_wd = load(w_down.at[:, at.fc], wd.at[at.i])
     swapped = (at.xc, at.zl * 8 + at.i)
     barrier = pltpu.get_barrier_semaphore()
 
@@ -336,40 +412,46 @@
     kv_in = Spread(at, lines, lambda i: wkv.at[i], True)
     q_in = Spread(at, lines, lambda i: wq.at[i], True)
     wo_in = Spread(at, lines, lambda i: wo_mine.at[i], True)
-    wd_in = Spread(at, lines, lambda i: wd.at[i], True)
+    wd_in = Spread(at, lines, lambda i: wd.at[i], False)
     wu_in = Spread(at, lines, lambda i: wu.at[i], False)
 
-    x_in = Gather(at, lines, x, lambda n: slot_of(xg, n))
+    x_in = gather_group(at, lines, x, lambda n: slot_of(xg, n))
     vec_in.start(vec)
     for copy in got_kv:
         copy.wait()
     kv_in.start()
+    got_wo.wait()
+    wo_in.start()
     got_q.wait()
     q_in.start()
     vg[at.i] = vec[...]
     slot_of(xg, at.xc)[...] = x[...]
-    slot_of(cg, at.xc)[...] = cot[...]
     vec_in.forward()
     kv_in.forward()
+    wo_in.forward()
+    q_in.forward()
     got_up.wait()
     at_row = lax.broadcasted_iota(jnp.int32, (1024, 128), 0)
     at_col = lax.broadcasted_iota(jnp.int32, (1024, 128), 1)
-    spot = (at_col // 64) * 512 + ((at_col // 32) % 2) * 256 + at.xc * 32 + at_col % 32
-    pick = jnp.where(at_row == spot, 1.0, 0.0).astype(BF)
-    for n in range(4):
-        wu[at.i, :, n * 128 : n * 128 + 128] = dot(
-            w_up_here[:, n * 1024 : (n + 1) * 1024], pick, 1, 0
-        ).astype(BF)
-    q_in.forward()
-    for copy in (got_wo, got_wd):
-        copy.wait()
-    wo_in.start()
-    wu_in.start()
-    wd_in.start()
+    spot = (at_col // 64) * 512 + ((at_col // 32) % 2) * 256 + at_col % 32
+
+    def part_on(d):
+        return ((at.x + at.y + d) % 4) * 2 + at.c
+
+    for d in range(4):
+        pick = jnp.where(at_row - spot == part_on(d) * 32, 1.0, 0.0).astype(BF)
+        for n in range(4):
+            picked[d, :, n * 128 : n * 128 + 128] = dot(
+                w_up_here[:, n * 1024 : (n + 1) * 1024], pick, 1, 0
+            ).astype(BF)
+    wu[at.i] = picked[0]
     vec_in.arrived()
     for d in range(8):
         rows[0:6, d * 128 : d * 128 + 128] = vg[d, 0:6, :]
     kv_in.arrived()
+    got_wd.wait()
+    wu_in.start(picked.at[0], lambda d: picked.at[d])
+    wd_in.start(None, lambda d: w_down.at[:, part_on(d)])
     at_k = pl.ds(10 + at.xc % 2, 1)
     q_bias = vg[at.xc // 2, at_k, :]
     v_bias = vg[4 + at.xc // 2, at_k, :]
@@ -399,9 +481,10 @@
     kv_pair(3)
     x_in.arrived(2)
     kv_pair(2)
-    cot_in = Gather(at, lines, cot, lambda n: slot_of(cg, n))
-    wo_in.forward()
-    wd_in.forward()
+    wo_in.arrived()
+    out_in = gather_group(at, lines, wo_mine, lambda n: wout.at[:, n])
+    wout[:, at.xc] = wo_mine[...]
+    cot_in = Halves(at, lines, cot, cg)
     q_in.arrived()
     for b in range(4):
         here = slice(b * 256, b * 256 + 256)
@@ -436,14 +519,12 @@
         attend(pl.ds(pl.multiple_of(t * 512, 512), 512), k, v, True)
         return 0
 
-    lax.fori_loop(0, 2, near_step, 0)
+    near_step(0, 0)
     wu_in.forward()
-    wo_in.arrived()
-    wo_own = wo_mine
-    out_in = Gather(at, lines, wo_own, lambda n: wout.at[:, n])
-    wout[:, at.xc] = wo_mine[...]
-    cot_in.forward(1)
-    cot_in.forward(3)
+    wd_in.forward()
+    near_step(1, 0)
+    out_in.forward(1)
+    out_in.forward(3)
     for copy in swaps:
         copy.wait_recv()
     given = []
@@ -456,15 +537,15 @@
                 copy.start()
                 given.append(copy)
     mixed[:, mine] = slot_of(att, at.xc)[...]
-    cot_in.forward(2)
+    out_in.forward(2)
     for dx in (1, 3, 2):
-        out_in.forward(dx)
+        cot_in.forward(dx)
     lane = lax.broadcasted_iota(jnp.int32, (1, 128), 1)
     for m in range(4):
         word = jnp.zeros((1, 128), F32)
         for b in range(4):
-            row = vg[m * 2 + b // 2, pl.ds(6 + (b % 2) * 2 + at.xc // 4, 1), :]
-            row = pltpu.roll(row, (b * 32 + 128 - (at.xc % 4) * 32) % 128, 1)
+            row = vg[m * 2 + b // 2, pl.ds(6 + (b % 2) * 2 + at.fc // 4, 1), :]
+            row = pltpu.roll(row, (b * 32 + 128 - (at.fc % 4) * 32) % 128, 1)
             word = jnp.where(lane // 32 == b, row, word)
         ub[:, m * 128 : m * 128 + 128] = word
     for dx in (0, 1, 3, 2):
@@ -477,17 +558,16 @@
     mid[...] = middle
     hat, rstd = normed(middle)
     own[...] = (hat * rows[4:5, :] + rows[5:6, :]).astype(BF)
-    tokens_in = Gather(at, lines, own, lambda n: slot_of(n2g, n))
-    slot_of(n2g, at.xc)[...] = own[...]
+    tokens_in = Halves(at, lines, own, n2g)
     up_sum[...] = jnp.zeros_like(up_sum)
-    out = Reduce(at, lines, lambda n: slot_of(parts_a, n), core_a, part_a, ring_a)
+    out = ReduceHalves(at, lines, parts_a, core_a, part_a, ring_a)
     wd_in.arrived()
     wu_in.arrived()
     for dx in (0, 1, 3, 2):
         cot_in.arrived(dx)
 
     def pair(dx):
-        here = pl.ds(pl.multiple_of(((at.x + 4 - dx) % 4) * 256, 256), 256)
+        here = slice(dx * 256, dx * 256 + 256)
         ups = wu[...].reshape(D, 512)
         pre = dot(n2g[here, :], ups, 1, 0) + ub[...]
         grad = dot(cg[here, :], wd[...].reshape(512, D), 1, 1)
@@ -524,27 +604,29 @@
     made = dot(act[...], cg[...], 0, 0).astype(BF)
     for n in range(16):
         wdown_grad[n // 8, (n // 2) % 4, n % 2] = made[n * 32 : n * 32 + 32, :]
-    downs = Halving(at, lines, wdown_grad, d1, d2, d3, False)
+    downs = Halving(at, lines, wdown_grad, d1, d2, d3, False, along=at.aslant)
     downs.start()
-    pulled = out.total()
+    for ring in range(2):
+        dmid[64 * ring : 64 * ring + 64, :] = out.both[ring].total()
+    pulled = dmid[...]
     sums[4:5, :] = jnp.sum(pulled * hat, axis=0, keepdims=True)
     sums[5:6, :] = jnp.sum(pulled, axis=0, keepdims=True)
     middle = cot[...].astype(F32) + norm_back(pulled, hat, rstd, rows[4:5, :])
     dmid[...] = middle
     low[...] = middle.astype(BF)
-    back_in = Gather(at, lines, low, lambda n: slot_of(db, n))
+    back_in = gather_group(at, lines, low, lambda n: slot_of(db, n))
     slot_of(db, at.xc)[...] = low[...]
     sums[0:1, :] = jnp.sum(low[...].astype(F32), axis=0, keepdims=True)
     sums[1:2, :] = jnp.sum(cot[...].astype(F32), axis=0, keepdims=True)
     made = dot(n2g[...], dpre[...], 0, 0).astype(BF)
     for n in range(16):
         wup_grad[n // 8, (n // 2) % 4, n % 2] = made[n * 64 : n * 64 + 64, :]
-    ups = Halving(at, lines, wup_grad, u1, u2, u3, True)
+    ups = Halving(at, lines, wup_grad, u1, u2, u3, True, along=at.aslant)
     ups.start()
     back_in.finish()
 
-    outs = Halving(at, lines, wout_grad, o1, o2, o3, False)
-    closing = Reduce(at, lines, lambda n: slot_of(ends, n), core_b, part_b, ring_b)
+    outs = Halving(at, lines, wout_grad, o1, o2, o3, True)
+    closing = ReduceHalves(at, lines, ends, core_b, part_b, ring_b)
     for dx in (2, 1, 3, 0):
         closing.core(dx)
     grads = dot(db[...], wout[at.xc].reshape(128, D), 1, 1).astype(BF)
@@ -610,7 +692,11 @@
             made = jnp.transpose(ref[:, there] + back[half, n].astype(F32))
             dqkv[there, 128 + n * 128 : 256 + n * 128] = made.astype(BF)
 
-    inner = Reduce(at, lines, lambda n: slot_of(parts_c, n), core_c, part_c, ring_c)
+    inner = Reduce(
+        at, lines,
+        lambda d, core: slot_of(parts_c, ((at.x + d) % 4) * 2 + core),
+        at.on_x, core_c, part_c, ring_c,
+    )
     shift_sum = jnp.zeros((1, D), F32)
     both_sum = jnp.zeros((1, D), F32)
     before = None
@@ -641,9 +727,14 @@
         points[to + (slice(2, 3),)] = gain_sum[:, wide]
         points[to + (slice(3, 4),)] = shift_sum[:, wide]
         points[to + (slice(4, 6),)] = sums[4:6, wide]
-        points[to + (slice(6, 7),)] = up_sum[:, (n // 4) * 128 : (n // 4) * 128 + 128]
+        some = up_sum[:, (n // 4) * 128 : (n // 4) * 128 + 128]
+        some = pltpu.roll(some, ((at.fc % 4) * 32 + 128 - (n % 4) * 32) % 128, 1)
+        some = jnp.where(lane // 32 == at.fc % 4, some, 0.0)
+        for b in range(2):
+            points[to + (slice(6 + b, 7 + b),)] = jnp.where(at.fc // 4 == b, some, 0.0)
         some = qkv_sum[:, 0:128] if n < 8 else qkv_sum[:, 256:384]
-        points[to + (slice(7, 8),)] = jnp.where(at.xc == n % 8, some, 0.0)
+        points[to + (slice(8, 9),)] = jnp.where(at.xc == n % 8, some, 0.0)
+        points[to + (slice(9, 16),)] = jnp.zeros((7, 128), F32)
     vectors = Halving(at, lines, points, v1, v2, v3, True)
     vectors.start()
     third = []
@@ -658,9 +749,19 @@
     acc = ups.total()
     for b in range(8):
         low_u[b] = acc[b * 8 : (b + 1) * 8, :]
-    to_group(lambda n: low_u.at[n], wide_u.at[at.xc])
-    wide_u[at.xc] = low_u[at.xc]
-    wdown_out[...] = downs.total()
+    to_group(lambda n: low_u.at[n], wide_u.at[at.fc])
+    wide_u[at.fc] = low_u[at.xc]
+    down_turn[...] = downs.total()
+    shifted = lines.copy(down_turn, wdown_out, at.on_x(at.y))
+
+    @pl.when(at.y != 0)
+    def _():
+        shifted.start()
+
+    @pl.when(at.y == 0)
+    def _():
+        wdown_out[...] = down_turn[...]
+
     turn[...] = outs.total()
     across = lines.copy(turn, wout_out, swapped)
 
@@ -672,7 +773,9 @@
     def _():
         wout_out[...] = turn[...]
 
-    result[...] = (mid[...] + closing.total() + rows[1:2, :]).astype(BF)
+    for ring in range(2):
+        some = slice(64 * ring, 64 * ring + 64)
+        result[some, :] = (mid[some, :] + closing.both[ring].total() + rows[1:2, :]).astype(BF)
     vectors.turn()
     firsts.turn()
     seconds.turn()
@@ -691,6 +794,10 @@
     @pl.when(at.i != at.xc)
     def _():
         across.wait()
+
+    @pl.when(at.y != 0)
+    def _():
+        shifted.wait()
 
     for copy in third:
         copy.wait()
@@ -731,10 +838,10 @@
     eight = pltpu.roll(total, (128 - spot) % 128, 1)
     for k, ref in enumerate((ob, db, g1, s1, g2, s2)):
         ref[...] = eight[k : k + 1, 0:8]
-    own = pltpu.roll(small[at.xc], (128 - ((at.i * 2 + at.zl) % 4) * 32) % 128, 1)
-    ub[...] = own[6:7, 0:32]
+    own = jnp.where(at.xc // 4 == 0, total[6:7, :], total[7:8, :])
+    ub[...] = pltpu.roll(own, (128 - (at.xc % 4) * 32) % 128, 1)[:, 0:32]
     bias = pltpu.roll(total, (128 - at.xc * 16) % 128, 1)
-    qv[...] = bias[7:8, 0:16]
+    qv[...] = bias[8:9, 0:16]
 
 
 def on_device(
@@ -750,7 +857,7 @@
         row += lines.shape[0]
     block, whole, half = VMEM((T, D), BF), VMEM((D, D), BF), VMEM((D, 512), BF)
     narrow, tall = VMEM((D, 128), BF), VMEM((D, 128), F32)
-    n_lines = 6 * 7 + 5 * 7 + 8 + 7 + 3 * 7 + 2 + 6 * 6 + 3 * 7 + 1
+    n_lines = 6 * 7 + 7 * 7 + 8 + 7 + 5 * 7 + 2 + 6 * 6 + 3 * 7 + 2
     parts = pl.pallas_call(
         layer_kernel,
         name="layer",
@@ -758,24 +865,26 @@
         out_specs=[vm_spec()] * 7,
         out_shape=[
             shape(T, D), shape(T, D), shape(8, 8, 384, of=F32), shape(8, 8, 512, of=F32),
-            shape(32, D, of=F32), shape(8, D, of=F32), shape(8, 8, 128, of=F32),
+            shape(32, D, of=F32), shape(8, D, of=F32), shape(8, 16, 128, of=F32),
         ],
         scratch_shapes=[
             VMEM((8, 16, 128), F32), VMEM((8, 128, 256), BF), VMEM((8, 128, 128), BF),
             VMEM((8, 128, 512), BF), VMEM((8, 2, 32, D), BF), VMEM((8, 16, D), BF),
-            VMEM((8, 8, 16, D), BF), VMEM((128, 4 * D), BF), VMEM((8, D), F32), VMEM((1, 512), F32),
+            VMEM((8, 8, 16, D), BF), VMEM((128, 4 * D), BF), VMEM((4, 128, 512), BF),
+            VMEM((8, D), F32), VMEM((1, 512), F32),
             whole, whole, whole, *[narrow] * 6, *[tall] * 3, block, VMEM((T, D), F32), block,
             whole, half, half, VMEM((T, D), F32), block, whole,
-            *[whole, *REDUCE_SCRATCH] * 3,
+            *[whole, *HALVES_SCRATCH] * 2, whole, *REDUCE_SCRATCH,
             narrow, tall, tall, VMEM((128, D), F32), VMEM((128, D), F32),
             VMEM((2, 2, 128, 512), BF), VMEM((2, 2, 128, 512), BF), VMEM((D, 384), BF),
             VMEM((8, D), F32), VMEM((1, 512), F32),
             VMEM((2, 4, 2, 64, 512), BF), VMEM((2, 4, 2, 32, D), BF), VMEM((2, 4, 2, 8, D), F32),
-            VMEM((2, 4, 2, 64, 384), BF), VMEM((2, 4, 2, 8, 128), F32),
+            VMEM((2, 4, 2, 64, 384), BF), VMEM((2, 4, 2, 16, 128), F32),
             *halving_scratch(True, (64, 512)), *halving_scratch(False, (32, D)),
-            *halving_scratch(False, (8, D), F32), *halving_scratch(True, (32, 384)),
-            *halving_scratch(False, (32, 384)), *halving_scratch(True, (8, 128), F32),
-            VMEM((8, 8, 512), F32), VMEM((8, 8, 384), F32), VMEM((8, D), F32), VMEM((8, 128), F32),
+            *halving_scratch(True, (8, D), F32), *halving_scratch(True, (32, 384)),
+            *halving_scratch(False, (32, 384)), *halving_scratch(True, (16, 128), F32),
+            VMEM((8, 8, 512), F32), VMEM((8, 8, 384), F32), VMEM((8, D), F32), VMEM((32, D), F32),
+            VMEM((16, 128), F32),
             DMA((8,)), DMA((n_lines,)), DMA((n_lines,)),
         ],
         compiler_params=pltpu.CompilerParams(

time: 155 us -> 144 us (0.929)
  Pallas kernels: 153 us -> 141 us
    pallas_call x1, Pallas kernels: 151 us -> 139 us  [on_device(): pl.pallas_call(layer_kernel, name='layer', in_specs=[vm_spec()] * 3 + [an...]
where the time goes in v4:
time: 144 us
  Pallas kernels  141 us (98%)
    pallas_call x1, Pallas kernels, on_device(): pl.pallas_call(layer_kernel, name='layer', in_specs=[vm_spec()] * 3 + [an...  139 us

profile of v4, /device:TPU:1, one launch (start us, length us, event | category | flops | bytes accessed | tf_op | source)
XLA Modules:
  0.0 143.6 jit_solution(14622231591009639851)
XLA Ops:
  0.6 0.0 copy-start.6
  0.7 0.0 copy-start.7
  0.7 0.0 copy-start.2
  0.7 0.0 copy-start.3
  0.7 0.0 copy-start.4
  0.7 0.0 copy-start.5
  0.7 0.0 copy-start
  0.7 0.0 copy-start.1
  0.7 0.6 copy-done.6
  1.3 0.0 copy-done.7
  1.3 0.0 copy-done.2
  1.3 0.0 copy-done.3
  1.4 0.0 copy-done.4
  1.4 0.0 copy-done.5
  1.4 0.0 copy-done
  1.4 0.0 copy-done.1
  1.4 0.6 convert_add_fusion.vec
  2.0 139.1 %layer.1 = (bf16[128,1024]{1,0:T(8,128)(2,1)}, bf16[128,1024]{1,0:T(8,128)(2,1)}, f32[8,8,384]{2,1,0:T(8,128)}, f32[8,8,512]{2,1,0:T(8,128)}, f32[32,1024]{1,0:T...) custom-call(bf16[128,1024]{1,0:T(8,128)(2,1)} %bitcast.22, bf16[128,1024]{1,0:T(8,128)(2,1)} %bitcast.23, ...), custom_call_target="tpu_custom_call" | custom-call | tf_op jit(solution)/shard_map/layer/pallas_call | solution.py:861
  141.2 2.3 %lay_out.1 = (bf16[128,1024]{1,0:T(8,128)(2,1)}, bf16[128,1024]{1,0:T(8,128)(2,1)}, f32[8,3072]{1,0:T(8,128)}, f32[1,16]{1,0:T(1,128)}, f32[8,1024]{1,0:T(8,128)...) custom-call(bf16[128,1024]{1,0:T(8,128)(2,1)} %get-tuple-element.35., ...), custom_call_target="tpu_custom_call" | custom-call | tf_op jit(solution)/shard_map/lay_out/pallas_call | solution.py:895
Async XLA Ops:
  0.6 0.7 copy-start.6
  0.7 0.7 copy-start.7
  0.7 0.7 copy-start.2
  0.7 0.7 copy-start.3
  0.7 0.7 copy-start.4
  0.7 0.7 copy-start.5
  0.7 0.7 copy-start
  0.7 0.7 copy-start.1

commit v5 on v4

--- a/solution.py
+++ b/solution.py
@@ -370,7 +370,7 @@
     vg, wkv, wq, wu, wd, wo_mine, wout, w_up_here, picked, rows, ub,
     xg, n1, cg, q, k, v, kr, vr, att, lse, top, total, mixed, mid, own, n2g, act, dpre, dmid, low, db,
     parts_a, core_a, part_a, ring_a, ends, core_b, part_b, ring_b, parts_c, core_c, part_c, ring_c,
-    do, delta, dq, dk, dv, away, back, dqkv, sums, up_sum,
+    pulls, do, delta, dq, dk, dv, away, back, dqkv, sums, up_sum,
     wup_grad, wdown_grad, wout_grad, wqkv_grad, points,
     u1, u2, u3, d1, d2, d3, o1, o2, o3, p1, p2, p3, g1, g2, g3, v1, v2, v3,
     low_u, low_q, turn, down_turn, point, local, send, recv,
@@ -614,8 +614,16 @@
     middle = cot[...].astype(F32) + norm_back(pulled, hat, rstd, rows[4:5, :])
     dmid[...] = middle
     low[...] = middle.astype(BF)
-    back_in = gather_group(at, lines, low, lambda n: slot_of(db, n))
-    slot_of(db, at.xc)[...] = low[...]
+    made = dot(low[...], wout[...].reshape(D, D), 1, 1).astype(BF)
+    for n in range(8):
+        pulls[n] = made[:, n * 128 : n * 128 + 128]
+    taken = []
+    for dx, dc in GROUP:
+        to = ((at.x + dx) % 4) * 2 + (at.c + dc) % 2
+        copy = lines.copy(pulls.at[to], slot_of(do, at.xc), at.in_group(dx, dc))
+        copy.start()
+        taken.append(copy)
+    slot_of(do, at.xc)[...] = pulls[at.xc]
     sums[0:1, :] = jnp.sum(low[...].astype(F32), axis=0, keepdims=True)
     sums[1:2, :] = jnp.sum(cot[...].astype(F32), axis=0, keepdims=True)
     made = dot(n2g[...], dpre[...], 0, 0).astype(BF)
@@ -623,15 +631,15 @@
         wup_grad[n // 8, (n // 2) % 4, n % 2] = made[n * 64 : n * 64 + 64, :]
     ups = Halving(at, lines, wup_grad, u1, u2, u3, True, along=at.aslant)
     ups.start()
-    back_in.finish()
-
     outs = Halving(at, lines, wout_grad, o1, o2, o3, True)
     closing = ReduceHalves(at, lines, ends, core_b, part_b, ring_b)
     for dx in (2, 1, 3, 0):
         closing.core(dx)
-    grads = dot(db[...], wout[at.xc].reshape(128, D), 1, 1).astype(BF)
-    do[...] = grads
-    both = grads.astype(F32) * att[...].astype(F32)
+    for copy in taken:
+        copy.wait_recv()
+    back_in = gather_group(at, lines, low, lambda n: slot_of(db, n))
+    slot_of(db, at.xc)[...] = low[...]
+    both = do[...].astype(F32) * att[...].astype(F32)
     delta[...] = by_head(
         jnp.sum(both * lanes_of(0, 1.0), axis=-1, keepdims=True),
         jnp.sum(both * lanes_of(1, 1.0), axis=-1, keepdims=True),
@@ -673,17 +681,20 @@
         if half == 0:
             for dx in (2, 1, 3):
                 closing.pass_on(dx)
-            made = dot(att[...], db[...], 0, 0)
-            for zl in range(2):
-                for i in range(8):
-                    b = (zl * 8 + i) * 8
-                    wout_grad[i // 4, i % 4, zl] = made[b : b + 8, :]
-            outs.start()
     downs.turn()
     pull(k, v, 0, False)
     ups.turn()
+    for dx in (1, 3, 2):
+        back_in.forward(dx)
     pull(k, v, 1, False)
-    outs.turn()
+    for dx in (0, 1, 3, 2):
+        back_in.arrived(dx)
+    made = dot(att[...], db[...], 0, 0)
+    for zl in range(2):
+        for i in range(8):
+            b = (zl * 8 + i) * 8
+            wout_grad[i // 4, i % 4, zl] = made[b : b + 8, :]
+    outs.start()
     dqkv[:, 0:128] = dq[...].astype(BF)
     for half in range(2):
         returns[half].wait_recv()
@@ -762,34 +773,35 @@
     def _():
         wdown_out[...] = down_turn[...]
 
-    turn[...] = outs.total()
-    across = lines.copy(turn, wout_out, swapped)
-
-    @pl.when(at.i != at.xc)
-    def _():
-        across.start()
-
-    @pl.when(at.i == at.xc)
-    def _():
-        wout_out[...] = turn[...]
-
     for ring in range(2):
         some = slice(64 * ring, 64 * ring + 64)
         result[some, :] = (mid[some, :] + closing.both[ring].total() + rows[1:2, :]).astype(BF)
     vectors.turn()
+    outs.turn()
     firsts.turn()
     seconds.turn()
+    for half, acc in enumerate((firsts.total(), seconds.total())):
+        for b in range(4):
+            low_q[half * 4 + b] = acc[b * 8 : (b + 1) * 8, :]
+    to_group(lambda n: low_q.at[n], wide_q.at[at.xc])
+    wide_q[at.xc] = low_q[at.xc]
     pulled = inner.total()
     hat, rstd = normed(x[...].astype(F32))
     xgrad[...] = (dmid[...] + norm_back(pulled, hat, rstd, rows[2:3, :])).astype(BF)
     point[...] = vectors.total()
     to_group(lambda n: point, small.at[at.xc])
     small[at.xc] = point[...]
-    for half, acc in enumerate((firsts.total(), seconds.total())):
-        for b in range(4):
-            low_q[half * 4 + b] = acc[b * 8 : (b + 1) * 8, :]
-    to_group(lambda n: low_q.at[n], wide_q.at[at.xc])
-    wide_q[at.xc] = low_q[at.xc]
+    turn[...] = outs.total()
+    across = lines.copy(turn, wout_out, swapped)
+
+    @pl.when(at.i != at.xc)
+    def _():
+        across.start()
+
+    @pl.when(at.i == at.xc)
+    def _():
+        wout_out[...] = turn[...]
+
 
     @pl.when(at.i != at.xc)
     def _():
@@ -801,10 +813,10 @@
 
     for copy in third:
         copy.wait()
-    for copy in swaps + given + returns:
+    for copy in swaps + given + taken + returns:
         copy.wait_send()
     for flow in (
-        vec_in, kv_in, q_in, wo_in, wd_in, wu_in, x_in, cot_in, out_in, tokens_in,
+        vec_in, kv_in, q_in, wo_in, wd_in, wu_in, x_in, cot_in, out_in, tokens_in, back_in,
         ups, downs, outs, firsts, seconds, vectors, out, inner, closing,
     ):
         flow.sent()
@@ -857,7 +869,7 @@
         row += lines.shape[0]
     block, whole, half = VMEM((T, D), BF), VMEM((D, D), BF), VMEM((D, 512), BF)
     narrow, tall = VMEM((D, 128), BF), VMEM((D, 128), F32)
-    n_lines = 6 * 7 + 7 * 7 + 8 + 7 + 5 * 7 + 2 + 6 * 6 + 3 * 7 + 2
+    n_lines = 6 * 7 + 7 * 7 + 8 + 7 + 7 + 5 * 7 + 2 + 6 * 6 + 3 * 7 + 2
     parts = pl.pallas_call(
         layer_kernel,
         name="layer",
@@ -875,7 +887,7 @@
             whole, whole, whole, *[narrow] * 6, *[tall] * 3, block, VMEM((T, D), F32), block,
             whole, half, half, VMEM((T, D), F32), block, whole,
             *[whole, *HALVES_SCRATCH] * 2, whole, *REDUCE_SCRATCH,
-            narrow, tall, tall, VMEM((128, D), F32), VMEM((128, D), F32),
+            VMEM((8, T, 128), BF), narrow, tall, tall, VMEM((128, D), F32), VMEM((128, D), F32),
             VMEM((2, 2, 128, 512), BF), VMEM((2, 2, 128, 512), BF), VMEM((D, 384), BF),
             VMEM((8, D), F32), VMEM((1, 512), F32),
             VMEM((2, 4, 2, 64, 512), BF), VMEM((2, 4, 2, 32, D), BF), VMEM((2, 4, 2, 8, D), F32),

time: 144 us -> 138 us (0.958)
  Pallas kernels: 141 us -> 135 us
    pallas_call x1, Pallas kernels: 139 us -> 133 us  [on_device(): pl.pallas_call(layer_kernel, name='layer', in_specs=[vm_spec()] * 3 + [an...]
where the time goes in v5:
time: 138 us; the launch traced here: 137 us
  Pallas kernels  135 us (98%)
    pallas_call x1, Pallas kernels, on_device(): pl.pallas_call(layer_kernel, name='layer', in_specs=[vm_spec()] * 3 + [an...  133 us

profile of v5, /device:TPU:1, one launch (start us, length us, event | category | flops | bytes accessed | tf_op | source)
XLA Modules:
  0.0 137.3 jit_solution(16905093204367746191)
XLA Ops:
  0.6 0.0 copy-start.6
  0.7 0.0 copy-start.7
  0.7 0.0 copy-start.2
  0.7 0.0 copy-start.3
  0.7 0.0 copy-start.4
  0.7 0.0 copy-start.5
  0.7 0.0 copy-start
  0.7 0.0 copy-start.1
  0.7 0.6 copy-done.6
  1.3 0.0 copy-done.7
  1.3 0.0 copy-done.2
  1.3 0.0 copy-done.3
  1.4 0.0 copy-done.4
  1.4 0.0 copy-done.5
  1.4 0.0 copy-done
  1.4 0.0 copy-done.1
  1.4 0.6 convert_add_fusion.vec
  2.0 132.8 %layer.1 = (bf16[128,1024]{1,0:T(8,128)(2,1)}, bf16[128,1024]{1,0:T(8,128)(2,1)}, f32[8,8,384]{2,1,0:T(8,128)}, f32[8,8,512]{2,1,0:T(8,128)}, f32[32,1024]{1,0:T...) custom-call(bf16[128,1024]{1,0:T(8,128)(2,1)} %bitcast.22, bf16[128,1024]{1,0:T(8,128)(2,1)} %bitcast.23, ...), custom_call_target="tpu_custom_call" | custom-call | tf_op jit(solution)/shard_map/layer/pallas_call | solution.py:873
  134.9 2.3 %lay_out.1 = (bf16[128,1024]{1,0:T(8,128)(2,1)}, bf16[128,1024]{1,0:T(8,128)(2,1)}, f32[8,3072]{1,0:T(8,128)}, f32[1,16]{1,0:T(1,128)}, f32[8,1024]{1,0:T(8,128)...) custom-call(bf16[128,1024]{1,0:T(8,128)(2,1)} %get-tuple-element.35., ...), custom_call_target="tpu_custom_call" | custom-call | tf_op jit(solution)/shard_map/lay_out/pallas_call | solution.py:907
Async XLA Ops:
  0.6 0.7 copy-start.6
  0.7 0.7 copy-start.7
  0.7 0.7 copy-start.2
  0.7 0.7 copy-start.3
  0.7 0.7 copy-start.4
  0.7 0.7 copy-start.5
  0.7 0.7 copy-start
  0.7 0.7 copy-start.1

commit v6 on v5

--- a/solution.py
+++ b/solution.py
@@ -316,11 +316,19 @@
         self.at, self.lines, self.slot, self.z_first = at, lines, slot, z_first
         self.y, self.again = {}, {}
 
-    def start(self, own=None, others=None):
+    def start(self, own=None):
+        self.start_z(own)
+        self.start_y(own)
+
+    def start_z(self, own=None):
         at = self.at
         own = self.slot(at.i) if own is None else own
         self.z = self.lines.copy(own, self.slot(at.i), at.mirror())
         self.z.start()
+
+    def start_y(self, own=None, others=None):
+        at = self.at
+        own = self.slot(at.i) if own is None else own
         for d in STEPS:
             block = own if others is None else others(d)
             self.y[d] = self.lines.copy(block, self.slot(at.i), at.along_y(d))
@@ -445,13 +453,14 @@
                 w_up_here[:, n * 1024 : (n + 1) * 1024], pick, 1, 0
             ).astype(BF)
     wu[at.i] = picked[0]
+    got_wd.wait()
+    wd_in.start_z()
+    wu_in.start_z(picked.at[0])
     vec_in.arrived()
     for d in range(8):
         rows[0:6, d * 128 : d * 128 + 128] = vg[d, 0:6, :]
     kv_in.arrived()
-    got_wd.wait()
-    wu_in.start(picked.at[0], lambda d: picked.at[d])
-    wd_in.start(None, lambda d: w_down.at[:, part_on(d)])
+    wd_in.start_y(None, lambda d: w_down.at[:, part_on(d)])
     at_k = pl.ds(10 + at.xc % 2, 1)
     q_bias = vg[at.xc // 2, at_k, :]
     v_bias = vg[4 + at.xc // 2, at_k, :]
@@ -474,6 +483,7 @@
     x_in.forward(3)
     x_in.arrived(0)
     kv_pair(0)
+    wu_in.start_y(None, lambda d: picked.at[d])
     x_in.forward(2)
     x_in.arrived(1)
     kv_pair(1)
@@ -520,9 +530,9 @@
         return 0
 
     near_step(0, 0)
-    wu_in.forward()
     wd_in.forward()
     near_step(1, 0)
+    wu_in.forward()
     out_in.forward(1)
     out_in.forward(3)
     for copy in swaps:

time: 138 us -> 138 us (level)
  no operation moved by 1% of the time
where the time goes in v6:
time: 138 us; the launch traced here: 137 us
  Pallas kernels  135 us (98%)
    pallas_call x1, Pallas kernels, on_device(): pl.pallas_call(layer_kernel, name='layer', in_specs=[vm_spec()] * 3 + [an...  133 us

profile of v6, /device:TPU:1, one launch (start us, length us, event | category | flops | bytes accessed | tf_op | source)
XLA Modules:
  0.0 137.3 jit_solution(13131996279867771728)
XLA Ops:
  0.6 0.0 copy-start.6
  0.7 0.0 copy-start.7
  0.7 0.0 copy-start.2
  0.7 0.0 copy-start.3
  0.7 0.0 copy-start.4
  0.7 0.0 copy-start.5
  0.7 0.0 copy-start
  0.7 0.0 copy-start.1
  0.7 0.6 copy-done.6
  1.3 0.0 copy-done.7
  1.3 0.0 copy-done.2
  1.3 0.0 copy-done.3
  1.4 0.0 copy-done.4
  1.4 0.0 copy-done.5
  1.4 0.0 copy-done
  1.4 0.0 copy-done.1
  1.4 0.6 convert_add_fusion.vec
  2.0 132.8 %layer.1 = (bf16[128,1024]{1,0:T(8,128)(2,1)}, bf16[128,1024]{1,0:T(8,128)(2,1)}, f32[8,8,384]{2,1,0:T(8,128)}, f32[8,8,512]{2,1,0:T(8,128)}, f32[32,1024]{1,0:T...) custom-call(bf16[128,1024]{1,0:T(8,128)(2,1)} %bitcast.22, bf16[128,1024]{1,0:T(8,128)(2,1)} %bitcast.23, ...), custom_call_target="tpu_custom_call" | custom-call | tf_op jit(solution)/shard_map/layer/pallas_call | solution.py:883
  134.9 2.3 %lay_out.1 = (bf16[128,1024]{1,0:T(8,128)(2,1)}, bf16[128,1024]{1,0:T(8,128)(2,1)}, f32[8,3072]{1,0:T(8,128)}, f32[1,16]{1,0:T(1,128)}, f32[8,1024]{1,0:T(8,128)...) custom-call(bf16[128,1024]{1,0:T(8,128)(2,1)} %get-tuple-element.35., ...), custom_call_target="tpu_custom_call" | custom-call | tf_op jit(solution)/shard_map/lay_out/pallas_call | solution.py:917
Async XLA Ops:
  0.6 0.7 copy-start.6
  0.7 0.7 copy-start.7
  0.7 0.7 copy-start.2
  0.7 0.7 copy-start.3
  0.7 0.7 copy-start.4
  0.7 0.7 copy-start.5
  0.7 0.7 copy-start
  0.7 0.7 copy-start.1
